TPU v7x, 512 devices: a whole 4x4x16 slice. The times are simulated.
512 devices in a mesh: row: 16 (over y_lo, x, core), col: 32 (over y_hi, z).
Axes of the slice: x: 4, y: 4 (y_hi: 2, y_lo: 2; y = y_hi * 2 + y_lo), z: 16, core: 2. Of those that a mesh axis runs over, the one named last changes fastest.
Arguments:
- valence_orbitals: bfloat16 [4, 48, 2, 2048], P(None, None, None, 'row'), may hold values from -6 to 6
- conduction_orbitals: bfloat16 [4, 64, 2, 2048], P(None, None, None, 'row'), may hold values from -6 to 6
- screened: bfloat16 [2, 2048, 2048], P(None, 'row'), may hold values from -1 to 1, as said below
- valence_index: int32 [4096], replicated, may hold values from 0 to 47
- conduction_index: int32 [4096], replicated, may hold values from 0 to 63
- kpoint_index: int32 [4096], replicated, may hold values from 0 to 3
Outputs:
- kernel: float32 [2, 32, 128, 4096], P(None, None, 'row', 'col')
Inputs may be any that keep to these rules, and one draw needn't show every extreme that they name: screened[0] is symmetric and screened[1] antisymmetric: the interaction is Hermitian.
All inputs are finite; a program needn't handle non-finite values.
Results may differ from a plain program's by a relative error of at most 0.0065.
Values may be sent and summed in bfloat16 or wider, within the bound.
No kernel may reach another device: no remote copies, remote signals or barrier semaphores. Data moves between devices by JAX's collectives and lax.ppermute only.
A program may use at most 64 MiB of HBM per device.

v0:
```python
import jax
import jax.numpy as jnp
from jax import lax
from jax.sharding import PartitionSpec as P


def pair_density(valence_table, conduction_table, valence_pick, conduction_pick, kpoint_pick):
    valence_rows = valence_table[kpoint_pick, valence_pick].astype(jnp.float32)
    conduction_rows = conduction_table[kpoint_pick, conduction_pick].astype(jnp.float32)
    real_part = (
        valence_rows[:, 0] * conduction_rows[:, 0] + valence_rows[:, 1] * conduction_rows[:, 1]
    )
    imag_part = (
        valence_rows[:, 0] * conduction_rows[:, 1] - valence_rows[:, 1] * conduction_rows[:, 0]
    )
    return jnp.stack([real_part, imag_part], 1).astype(jnp.bfloat16)


def shards(
    valence_orbitals, conduction_orbitals, screened, valence_index, conduction_index, kpoint_index
):
    row_count = lax.axis_size("row")
    col_count = lax.axis_size("col")
    row_id = lax.axis_index("row")
    col_id = lax.axis_index("col")
    fine_rows = valence_index.shape[0] // (row_count * col_count)
    col_width = row_count * fine_rows
    panel_rows = screened.shape[1]
    plane_all = screened.shape[2]
    col_start = col_id * col_width
    valence_cols = lax.dynamic_slice_in_dim(valence_index, col_start, col_width, 0)
    conduction_cols = lax.dynamic_slice_in_dim(conduction_index, col_start, col_width, 0)
    kpoint_cols = lax.dynamic_slice_in_dim(kpoint_index, col_start, col_width, 0)
    local_density = pair_density(
        valence_orbitals, conduction_orbitals, valence_cols, conduction_cols, kpoint_cols
    )
    col_density = lax.all_gather(local_density, "row", axis=2, tiled=True)
    own_block = lax.dynamic_slice_in_dim(col_density, row_id * fine_rows, fine_rows, 0)
    row_density = lax.all_gather(own_block, "col", axis=0, tiled=True)
    w_block = jnp.concatenate(
        [
            jnp.concatenate([screened[0], -screened[1]], 1),
            jnp.concatenate([screened[1], screened[0]], 1),
        ],
        0,
    )
    flat_cols = col_density.reshape(col_width, 2 * plane_all)
    screened_local = lax.dot_general(
        w_block, flat_cols, (((1,), (1,)), ((), ())), preferred_element_type=jnp.float32
    )
    screened_local = screened_local.astype(jnp.bfloat16).reshape(2, panel_rows, col_width)
    half_span = col_count // 2
    strip_count = half_span + 1
    flipped = row_density.reshape(col_count, fine_rows, 2, plane_all)[::-1]
    doubled = jnp.concatenate([flipped, flipped], 0)
    strips = lax.dynamic_slice_in_dim(doubled, col_count - 1 - col_id, strip_count, 0)
    strips = strips.reshape(strip_count * fine_rows, 2, plane_all)
    piece = lax.all_gather(screened_local, "row", axis=1, tiled=True)
    first_half = jnp.concatenate([piece[0], piece[1]], 1)
    second_half = jnp.concatenate([piece[1], -piece[0]], 1)
    running = jnp.dot(strips[:, 0], first_half, preferred_element_type=jnp.float32)
    direct = running + jnp.dot(strips[:, 1], second_half, preferred_element_type=jnp.float32)
    strip_parts = direct.reshape(strip_count, fine_rows, 2, col_width).transpose(2, 0, 1, 3)
    padded = jnp.concatenate(
        [strip_parts, jnp.zeros((2, col_count - strip_count, fine_rows, col_width), jnp.float32)], 1
    )
    reversed_parts = padded[:, ::-1]
    computed = lax.dynamic_slice_in_dim(
        jnp.concatenate([reversed_parts, reversed_parts], 1), col_count - 1 - col_id, col_count, 1
    )
    strip_index = jnp.arange(col_count, dtype=jnp.int32)[:, None]
    lane_index = jnp.arange(col_width, dtype=jnp.int32)[None, :] // fine_rows
    distance = (col_id - strip_index) % col_count
    formed = (
        (distance >= 1) & (distance < half_span)
        | (distance == 0) & (lane_index >= row_id)
        | (distance == half_span) & (lane_index <= row_id)
    )
    formed = formed[None, :, None, :]
    outgoing = jnp.where(formed, computed, 0.0).reshape(
        2, col_count, fine_rows, row_count, fine_rows
    )
    incoming = lax.all_to_all(
        lax.all_to_all(
            outgoing.astype(jnp.bfloat16), "row", split_axis=3, concat_axis=3, tiled=True
        ),
        "col",
        split_axis=1,
        concat_axis=1,
        tiled=True,
    ).astype(outgoing.dtype)
    mirrored = jnp.swapaxes(incoming, 2, 4).reshape(2, col_count, fine_rows, col_width)
    mirrored = jnp.stack([mirrored[0], -mirrored[1]])
    return jnp.where(formed, computed, mirrored)


def solution(mesh):
    in_specs = (
        P(None, None, None, "row"),
        P(None, None, None, "row"),
        P(None, "row", None),
        P(),
        P(),
        P(),
    )
    out_specs = P(None, None, "row", "col")
    return jax.shard_map(shards, mesh=mesh, in_specs=in_specs, out_specs=out_specs, check_vma=False)
```

profile of v0, /device:TPU:1, one launch (start us, length us, event | category | flops | bytes accessed | tf_op | source)
XLA Modules:
  0.0 317.1 jit_solution(8224100476771466283)
XLA Ops:
  6.5 0.0 copy-start
  6.5 0.0 copy-start.1
  6.5 0.0 all-gather.4.cloned.1.call-start
  6.5 0.9 fusion.28
  7.4 1.8 gather_fusion
  9.3 0.0 copy-done
  9.3 0.9 gather_fusion.1
  10.2 0.2 add_convert_fusion
  10.4 0.8 pad_maximum_fusion
  11.2 0.0 all-gather.4.cloned.1.call-update
  11.2 0.0 all-gather.8.cloned.1.call-start
  11.3 1.1 fusion.35
  12.4 0.0 copy-done.1
  12.4 0.1 slice_bitcast_fusion.7
  12.5 48.3 %all-gather.4.cloned.1.call-done = bf16[128,2,2048]{2,1,0:T(2,128)(2,1)} async-done(((bf16[128,2,128]{2,1,0:T(2,128)(2,1)}), bf16[128,2,2048]{2,1,0:T(2,128)(2,1)}) %all-gather.4.cloned.1.call-update) | async-done | bytes 1048592 | tf_op jit(solution)/shard_map/all_gather | solution.py:37
  60.8 1.6 copy.48
  62.4 1.4 fusion.9
  63.7 0.0 all-gather.8.cloned.1.call-update
  63.8 0.0 all-gather.6.cloned.1.call-start
  63.8 1.5 constant_dynamic-slice_fusion
  65.3 0.0 all-gather.6.cloned.1.call-update
  65.4 0.1 and_or_fusion
  65.5 0.1 copy.41
  65.6 39.7 %all-gather.8.cloned.1.call-done = bf16[2,2048,128]{2,1,0:T(8,128)(2,1)} async-done(((bf16[2,128,128]{2,1,0:T(8,128)(2,1)}), bf16[2,2048,128]{2,1,0:T(8,128)(2,1)}) %all-gather.8.cloned.1.call-update) | async-done | bytes 1048592 | tf_op jit(solution)/shard_map/all_gather | solution.py:58
  105.3 1.1 fusion.36
  106.4 2.1 slice_bitcast_fusion.6
  108.5 140.8 %all-gather.6.cloned.1.call-done = bf16[256,2,2048]{2,1,0:T(2,128)(2,1)} async-done(((bf16[8,2,2048]{2,1,0:T(2,128)(2,1)}), bf16[256,2,2048]{2,1,0:T(2,128)(2,1)}) %all-gather.6.cloned.1.call-update) | async-done | bytes 2097168 | tf_op jit(solution)/shard_map/all_gather | solution.py:39
  249.3 2.5 copy.42
  251.8 1.5 rev.6
  253.2 0.0 copy-start.2
  253.3 1.7 fusion.13
  255.0 0.0 copy-done.2
  255.0 0.3 fusion.14
  255.3 0.3 fusion.8
  255.7 0.4 copy.43
  256.1 0.1 concatenate.38
  256.2 1.4 rev.7
  257.6 0.6 copy_bitcast_fusion
  258.2 0.5 reshape.209
  258.7 19.9 %all_to_all.10 = bf16[16,2,2048]{2,1,0:T(2,128)(2,1)S(1)} all-to-all(bf16[16,2,2048]{2,1,0:T(2,128)(2,1)S(1)} %reshape.209), channel_id=1, replica_groups=mesh['row'=16,'col'=32] {'row'}, dimensions={0} | all-to-all | bytes 262144 | tf_op jit(solution)/shard_map/all_to_all | solution.py:84
  278.7 0.3 reshape.210
  278.9 1.7 copy.45
  280.6 1.1 reshape.211
  281.8 24.9 %all_to_all.11 = bf16[32,2,1024]{2,1,0:T(2,128)(2,1)S(1)} all-to-all(bf16[32,2,1024]{2,1,0:T(2,128)(2,1)S(1)} %reshape.211), channel_id=1, replica_groups=mesh['row'=16,'col'=32] {'col'}, dimensions={0} | all-to-all | bytes 262144 | tf_op jit(solution)/shard_map/all_to_all | solution.py:83
  306.7 0.7 reshape.212
  307.4 1.3 copy.46
  308.7 0.1 convert_bitcast_fusion
  308.8 0.1 slice_bitcast_fusion.4
  308.9 0.6 maximum_select_fusion
  309.5 1.0 copy.47
  (5 shorter events, 0.1 us)
Async XLA Ops:
  6.5 2.7 copy-start
  6.5 5.8 %copy-start.1 = (bf16[2,128,2048]{2,1,0:T(8,128)(2,1)S(1)}, bf16[2,128,2048]{2,1,0:T(8,128)(2,1)}, u32[]{:S(2)}) copy-start(bf16[2,128,2048]{2,1,0:T(8,128)(2,1)} %param.8) | copy-start | bytes 3145732
  6.5 54.2 %all-gather.4.cloned.1.call-start = ((), (), s32[]{:S(2)}) async-start(), calls=%async_computation.2 | async-start | bytes 1114112 | tf_op jit(solution)/shard_map/all_gather | solution.py:37
  11.2 94.0 %all-gather.8.cloned.1.call-start = ((), (), s32[]{:S(2)}) async-start(), calls=%async_computation.4 | async-start | bytes 1114112 | tf_op jit(solution)/shard_map/all_gather | solution.py:58
  63.8 185.6 %all-gather.6.cloned.1.call-start = ((), (), s32[]{:S(2)}) async-start(), calls=%async_computation.3 | async-start | bytes 2162688 | tf_op jit(solution)/shard_map/all_gather | solution.py:39
  253.2 1.7 copy-start.2
Sparse Core Ops, SparseCore 0:
  11.3 49.3 all-gather.3
  63.9 41.3 all-gather.7
  108.4 140.8 all-gather.5
where the time goes:
time: 318 us; the launch traced here: 317 us
  waiting for transfers between devices  229 us (72%)
  blocking collectives  44.9 us (14%)
  local copies, waits for them, and re-layouts  20.5 us (6%)
  between operations  13.3 us (4%)
  other arithmetic  7.41 us (2%)
    all_gather x1, waiting for transfers between devices, shards(): row_density = lax.all_gather(own_block, 'col', axis=0, tiled=True)  141 us
    all_gather x1, waiting for transfers between devices, shards(): col_density = lax.all_gather(local_density, 'row', axis=2, tiled=True)  48.3 us
    all_gather x1, waiting for transfers between devices, shards(): piece = lax.all_gather(screened_local, 'row', axis=1, tiled=True)  39.7 us
    all_to_all x1, blocking collectives, shards(): lax.all_to_all(lax.all_to_all(outgoing.astype(jnp.bfloat16), 'row', split...  24.9 us
    all_to_all x1, blocking collectives, shards(): lax.all_to_all(outgoing.astype(jnp.bfloat16), 'row', split_axis=3, concat...  19.9 us
  transfers between devices with their start and end apart: 3, of which 3 were waited for; matrix products, arithmetic and copies ran while one was open for 2% of the time, Pallas kernels for 0%

commit v1 on v0

v1 whole, which is shorter than its diff:
```python
import functools

import jax
import jax.numpy as jnp
from jax import lax
from jax.experimental import pallas as pl
from jax.experimental.pallas import tpu as pltpu
from jax.sharding import PartitionSpec as P

VAL = 48
CON = 64
FINE = 8
SLICE = 128
HALF = 64
KPAD = 256
VMEM = pltpu.CompilerParams(vmem_limit_bytes=48 * 1024 * 1024)


def lane_matrix(row):
    return jnp.broadcast_to(row.astype(jnp.float32), (128, 128)).T


def one_hot(index):
    lane = lax.broadcasted_iota(jnp.int32, index.shape, 1).astype(jnp.float32)
    low = jnp.where(index == lane, 1.0, 0.0)
    high = jnp.where(index == lane + 128.0, 1.0, 0.0)
    return jnp.concatenate([low, high], 1).astype(jnp.bfloat16)


def densities(valence, conduction):
    width = 2 * SLICE
    v_re, v_im = valence[:, :width], valence[:, width:]
    c_re, c_im = conduction[:, :width], conduction[:, width:]
    return v_re * c_re + v_im * c_im, v_re * c_im - v_im * c_re


def transition_rows(v_ref, n_ref, k_ref, start):
    v = v_ref[pl.ds(start, 1), :]
    n = n_ref[pl.ds(start, 1), :]
    k = k_ref[pl.ds(start, 1), :]
    return lane_matrix(k * VAL + v), lane_matrix(k * CON + n)


def pick(rows, parity, table):
    i = lax.broadcasted_iota(jnp.int32, (rows, table.shape[0]), 0)
    j = lax.broadcasted_iota(jnp.int32, (rows, table.shape[0]), 1)
    mask = jnp.where(j == 2 * i + parity, 1.0, 0.0).astype(jnp.bfloat16)
    return jnp.dot(mask, table, preferred_element_type=jnp.float32).astype(jnp.bfloat16)


def columns_kernel(own_ref, partner_ref, v_ref, n_ref, k_ref, table_ref, out_ref, held):
    core = lax.rem(lax.axis_index("row"), 2)
    column = lax.axis_index("col")
    split = 2 * VAL * 4
    both = jnp.concatenate([own_ref[...], partner_ref[...]], 1)
    for parity in range(2):
        lanes = pl.ds(parity * 2 * SLICE, 2 * SLICE)
        table_ref[0:KPAD, lanes] = pick(KPAD, parity, both[:split])
        table_ref[KPAD:, lanes] = pick(KPAD, parity, both[split:])
    v_at, c_at = transition_rows(v_ref, n_ref, k_ref, column)
    valence = jnp.dot(one_hot(v_at), table_ref[0:KPAD, :], preferred_element_type=jnp.float32)
    conduction = jnp.dot(one_hot(c_at), table_ref[KPAD:, :], preferred_element_type=jnp.float32)
    real, imag = densities(valence, conduction)
    held[0] = real
    held[1] = imag
    rows = pl.ds(pl.multiple_of(core * HALF, HALF), HALF)
    own = pl.ds(pl.multiple_of(core * SLICE, SLICE), SLICE)
    partner = pl.ds(pl.multiple_of((1 - core) * SLICE, SLICE), SLICE)
    for part in range(2):
        mine = held[part, rows, :].astype(jnp.bfloat16)
        for copy in range(out_ref.shape[0]):
            out_ref[copy, part * HALF : (part + 1) * HALF, own] = mine[:, :SLICE]
            out_ref[copy, part * HALF : (part + 1) * HALF, partner] = mine[:, SLICE:]


def direct_kernel(pairs_ref, own_ref, partner_ref, table_ref, v_ref, n_ref, k_ref, out_ref, screened):
    first = lax.broadcasted_iota(jnp.int32, (SLICE, 2 * HALF), 1) < HALF
    sign = jnp.where(first, -1.0, 1.0)
    width = pairs_ref.shape[2]
    for half, w_ref in enumerate((own_ref, partner_ref)):
        parts = []
        for part in range(2):
            total = jnp.zeros((SLICE, 2 * HALF), jnp.float32)
            for chip in range(pairs_ref.shape[0]):
                total += lax.dot_general(
                    w_ref[part, :, chip * width : (chip + 1) * width],
                    pairs_ref[chip],
                    (((1,), (1,)), ((), ())),
                    preferred_element_type=jnp.float32,
                )
            parts.append(total)
        x = (parts[0] + sign * pltpu.roll(parts[1], HALF, 1)).astype(jnp.bfloat16)
        screened[half * SLICE : (half + 1) * SLICE, :] = x
        x = x.astype(jnp.float32)
        turned = -sign * pltpu.roll(x, HALF, 1)
        screened[(2 + half) * SLICE : (3 + half) * SLICE, :] = turned.astype(jnp.bfloat16)

    strips = 4

    def step(m, carry):
        v_at, c_at = [], []
        for s in range(strips):
            v, c = transition_rows(v_ref, n_ref, k_ref, m * strips + s)
            v_at.append(v)
            c_at.append(c)
        valence = jnp.dot(one_hot(jnp.concatenate(v_at, 0)), table_ref[0:KPAD, :], preferred_element_type=jnp.float32)
        conduction = jnp.dot(one_hot(jnp.concatenate(c_at, 0)), table_ref[KPAD:, :], preferred_element_type=jnp.float32)
        density = jnp.concatenate(densities(valence, conduction), 1).astype(jnp.bfloat16)
        direct = jnp.dot(density, screened[...], preferred_element_type=jnp.float32)
        direct = direct.reshape(strips, 16, FINE, 2 * HALF)
        direct = jnp.concatenate([direct[s] for s in range(strips)], 1).astype(jnp.bfloat16)
        out_ref[:, pl.ds(pl.multiple_of(m * strips * FINE, strips * FINE), strips * FINE), :] = direct
        return carry

    lax.fori_loop(0, v_ref.shape[0] // strips, step, 0)


def total_kernel(in_ref, out_ref):
    first = lax.broadcasted_iota(jnp.int32, (in_ref.shape[1], 2 * HALF), 1) < HALF
    sums = []
    for core in range(2):
        total = in_ref[core].astype(jnp.float32)
        for chip in range(1, in_ref.shape[0] // 2):
            total += in_ref[2 * chip + core].astype(jnp.float32)
        sums.append(total)
    out_ref[0] = jnp.where(first, sums[0], pltpu.roll(sums[1], HALF, 1))
    out_ref[1] = jnp.where(first, pltpu.roll(sums[0], HALF, 1), sums[1])


def shards(valence_orbitals, conduction_orbitals, screened, valence_index, conduction_index, kpoint_index):
    rows = lax.axis_size("row")
    chips = rows // 2
    swap = [(i, i ^ 1) for i in range(rows)]
    same_core = [[2 * chip + core for chip in range(chips)] for core in range(2)]
    tables = jnp.concatenate(
        [valence_orbitals.reshape(-1, SLICE), conduction_orbitals.reshape(-1, SLICE)], 0
    )
    partner_tables = lax.ppermute(tables, "row", swap)
    partner_screened = lax.ppermute(screened, "row", swap)
    v = valence_index.reshape(-1, 128)
    n = conduction_index.reshape(-1, 128)
    k = kpoint_index.reshape(-1, 128)
    bf16 = jnp.bfloat16
    table, pairs = pl.pallas_call(
        columns_kernel,
        out_shape=(
            jax.ShapeDtypeStruct((2 * KPAD, 4 * SLICE), bf16),
            jax.ShapeDtypeStruct((chips, 2 * HALF, 2 * SLICE), bf16),
        ),
        scratch_shapes=[pltpu.VMEM((2, 128, 2 * SLICE), jnp.float32)],
        compiler_params=VMEM,
        name="columns",
    )(tables, partner_tables, v, n, k)
    pairs = lax.all_to_all(pairs, "row", 0, 0, axis_index_groups=same_core, tiled=True)
    partial = pl.pallas_call(
        direct_kernel,
        out_shape=jax.ShapeDtypeStruct((rows, v.shape[0] * FINE, 2 * HALF), bf16),
        scratch_shapes=[pltpu.VMEM((4 * SLICE, 2 * HALF), bf16)],
        compiler_params=VMEM,
        name="direct",
    )(pairs, screened, partner_screened, table, v, n, k)
    partial = lax.all_to_all(partial, "row", 0, 0, tiled=True)
    out = pl.pallas_call(
        total_kernel,
        out_shape=jax.ShapeDtypeStruct((2, partial.shape[1], 2 * HALF), jnp.float32),
        compiler_params=VMEM,
        name="total",
    )(partial)
    return out.reshape(2, v.shape[0], FINE, 2 * HALF)


def solution(mesh):
    in_specs = (
        P(None, None, None, "row"),
        P(None, None, None, "row"),
        P(None, "row", None),
        P(),
        P(),
        P(),
    )
    return jax.shard_map(
        shards, mesh=mesh, in_specs=in_specs, out_specs=P(None, None, "row", "col"), check_vma=False
    )
```

time: 318 us -> 56.8 us (0.18)
  waiting for transfers between devices: 229 us -> 1.46 us
  local copies, waits for them, and re-layouts: 20.5 us -> 2.15 us
  blocking collectives: 44.9 us -> 31.5 us
  between operations: 13.3 us -> 0.04 us
  starting transfers between devices: 0.09 us -> 10.8 us
  Pallas kernels: 0 us -> 9.39 us
  other arithmetic: 7.41 us -> 0.97 us
    all_gather x3 -> x0, waiting for transfers between devices: 229 us -> none  [the longest x1 141 us: shards(): row_density = lax.all_gather(own_block, 'col', axis=0, tiled=True)]
    all_to_all x2, blocking collectives: 44.9 us -> 31.5 us  [the longest x1 18.8 us: shards(): partial = lax.all_to_all(partial, 'row', 0, 0, tiled=True)]
    ppermute x0 -> x2, starting transfers between devices: none -> 10.8 us  [the longest x1 8.91 us: shards(): partner_screened = lax.ppermute(screened, 'row', swap)]
    pallas_call x0 -> x3, Pallas kernels: none -> 9.39 us  [the longest x1 7.76 us: shards(): pl.pallas_call(direct_kernel, out_shape=jax.ShapeDtypeStruct((rows, v.sha...]
  transfers between devices with their start and end apart: 3 -> 2, of which waited for: 3 -> 1; matrix products, arithmetic and copies ran while one was open for 2% -> 2% of each run, Pallas kernels for 0% -> 1%
where the time goes in v1:
time: 56.8 us; the launch traced here: 56.3 us
  blocking collectives  31.5 us (55%)
  starting transfers between devices  10.8 us (19%)
  Pallas kernels  9.39 us (17%)
  local copies, waits for them, and re-layouts  2.15 us (4%)
  waiting for transfers between devices  1.46 us (3%)
  other arithmetic  0.97 us (2%)
    all_to_all x1, blocking collectives, shards(): partial = lax.all_to_all(partial, 'row', 0, 0, tiled=True)  18.8 us
    all_to_all x1, blocking collectives, shards(): lax.all_to_all(pairs, 'row', 0, 0, axis_index_groups=same_core, tiled=True)  12.7 us
    ppermute x1, starting transfers between devices, shards(): partner_screened = lax.ppermute(screened, 'row', swap)  8.91 us
    pallas_call x1, Pallas kernels, shards(): pl.pallas_call(direct_kernel, out_shape=jax.ShapeDtypeStruct((rows, v.sha...  7.76 us
    unnamed x8, local copies, waits for them, and re-layouts  2.15 us
    ppermute x1, starting transfers between devices, shards(): partner_tables = lax.ppermute(tables, 'row', swap)  1.92 us
    ppermute x1, waiting for transfers between devices, shards(): partner_tables = lax.ppermute(tables, 'row', swap)  1.45 us
  transfers between devices with their start and end apart: 2, of which 1 were waited for; matrix products, arithmetic and copies ran while one was open for 2% of the time, Pallas kernels for 1%

profile of v1, /device:TPU:1, one launch (start us, length us, event | category | flops | bytes accessed | tf_op | source)
XLA Modules:
  0.0 56.3 jit_solution(6806421424152764861)
XLA Ops:
  0.0 0.0 copy-start
  0.0 8.9 %collective-permute-start.1 = (bf16[2,128,2048]{2,1,0:T(8,128)(2,1)}, bf16[2,128,2048]{2,1,0:T(8,128)(2,1)S(1)}, u32[]{:S(2)}, u32[]{:S(2)}) collective-permute-start(bf16[2,128,2048]{2,1,0:T(8,128)(2,1)} %own_ref.1), channel_id=1, source_target_pairs={{0,32},{32,0},{64,96},{96,64},{128,160},{160,128},{192,224},{224,1... | collective-permute-start | bytes 3145736 | tf_op jit(solution)/shard_map/ppermute | solution.py:139
  8.9 1.0 %pad_maximum_fusion.own_ref = bf16[896,128]{1,0:T(8,128)(2,1)S(1)} fusion(bf16[512,128]{1,0:T(8,128)(2,1)} %bitcast.12, bf16[384,128]{1,0:T(8,128)(2,1)} %bitcast.13), kind=kLoop, calls=%fused_computation | loop fusion | flops 458752 | bytes 458752 | tf_op jit(solution)/shard_map/concatenate | solution.py:135
  9.9 1.9 %collective-permute-start = (bf16[896,128]{1,0:T(8,128)(2,1)S(1)}, bf16[896,128]{1,0:T(8,128)(2,1)S(1)}, u32[]{:S(2)}, u32[]{:S(2)}) collective-permute-start(bf16[896,128]{1,0:T(8,128)(2,1)S(1)} %pad_maximum_fusion.own_ref), channel_id=1, source_target_pairs={{0,32},{32,0},{64,96},{96,64},{128,160},{160,128},{192,224},{224,1... | collective-permute-start | bytes 688136 | tf_op jit(solution)/shard_map/ppermute | solution.py:138
  11.8 1.5 %collective-permute-done.partner_ref = bf16[896,128]{1,0:T(8,128)(2,1)S(1)} collective-permute-done((bf16[896,128]{1,0:T(8,128)(2,1)S(1)}, bf16[896,128]{1,0:T(8,128)(2,1)S(1)}, u32[]{:S(2)}, u32[]{:S(2)}) %collective-permute-start) | collective-permute-done | bytes 229408 | tf_op jit(solution)/shard_map/ppermute | solution.py:138
  13.3 0.0 copy-start.1
  13.3 0.7 %copy-done.1 = s32[4096]{0:T(1024)S(1)} copy-done((s32[4096]{0:T(1024)S(1)}, s32[4096]{0:T(1024)}, u32[]{:S(2)}) %copy-start.1) | copy-done | bytes 16408
  14.0 0.0 copy-start.2
  14.0 0.7 %copy-done.2 = s32[4096]{0:T(1024)S(1)} copy-done((s32[4096]{0:T(1024)S(1)}, s32[4096]{0:T(1024)}, u32[]{:S(2)}) %copy-start.2) | copy-done | bytes 16408
  14.7 0.0 copy-start.3
  14.7 0.7 %copy-done.3 = s32[4096]{0:T(1024)S(1)} copy-done((s32[4096]{0:T(1024)S(1)}, s32[4096]{0:T(1024)}, u32[]{:S(2)}) %copy-start.3) | copy-done | bytes 16408
  15.4 0.7 %columns.1 = (bf16[512,512]{1,0:T(8,128)(2,1)S(1)}, bf16[8,128,256]{2,1,0:T(8,128)(2,1)S(1)}) custom-call(bf16[896,128]{1,0:T(8,128)(2,1)S(1)} %pad_maximum_fusion.own_ref, bf16[896,128]{1,0:T(8,128)(2,1)S(1)} %collective-permute-done.partner_ref, s32[32,128]{1,0:T(8,128)S(1)} %bitcast.6, s32[32,128]{1,0:T(8,128)S(1)} %bitcast.8, s32[32,128]{1,0:T(8,128)S(1)} %bitcast.10), custom_call_target="tpu_custom_call" | custom-call | tf_op jit(solution)/shard_map/columns/pallas_call | solution.py:144
  16.2 12.7 %all_to_all.10.pairs_ref = bf16[8,128,256]{2,1,0:T(8,128)(2,1)S(1)} all-to-all(bf16[8,128,256]{2,1,0:T(8,128)(2,1)S(1)} %get-tuple-element.7), channel_id=1, replica_groups={{0,64,128,192,256,320,384,448},{32,96,160,224,288,352,416,480},{1,65,12..., dimensions={0} | all-to-all | bytes 1048576 | tf_op jit(solution)/shard_map/all_to_all | solution.py:154
  28.9 0.0 collective-permute-done.1.partner_ref
  28.9 0.0 copy-done
  28.9 7.8 %direct.1 = bf16[16,256,128]{2,1,0:T(8,128)(2,1)S(1)} custom-call(bf16[8,128,256]{2,1,0:T(8,128)(2,1)S(1)} %all_to_all.10.pairs_ref, bf16[2,128,2048]{2,1,0:T(8,128)(2,1)S(1)} %copy-done, bf16[2,128,2048]{2,1,0:T(8,128)(2,1)S(1)} %collective-permute-done.1.partner_ref, bf16[512,512]{1,0:T(8,128)(2,1)S(1)} %get-tuple-element.8.table_ref, ...), custom_call_target="tpu_custom_call" | custom-call | tf_op jit(solution)/shard_map/direct/pallas_call | solution.py:155
  36.7 18.8 %all_to_all.11.in_ref = bf16[16,256,128]{2,1,0:T(8,128)(2,1)S(1)} all-to-all(bf16[16,256,128]{2,1,0:T(8,128)(2,1)S(1)} %direct.1), channel_id=1, replica_groups=mesh['row'=16,'col'=32] {'row'}, dimensions={0} | all-to-all | bytes 2097152 | tf_op jit(solution)/shard_map/all_to_all | solution.py:162
  55.4 0.9 %total.1 = f32[2,256,128]{2,1,0:T(8,128)} custom-call(bf16[16,256,128]{2,1,0:T(8,128)(2,1)S(1)} %all_to_all.11.in_ref), custom_call_target="tpu_custom_call" | custom-call | tf_op jit(solution)/shard_map/total/pallas_call | solution.py:163
Async XLA Ops:
  0.0 28.9 %copy-start = (bf16[2,128,2048]{2,1,0:T(8,128)(2,1)S(1)}, bf16[2,128,2048]{2,1,0:T(8,128)(2,1)}, u32[]{:S(2)}) copy-start(bf16[2,128,2048]{2,1,0:T(8,128)(2,1)} %own_ref.1) | copy-start | bytes 3145732
  0.0 28.9 %collective-permute-start.1 = (bf16[2,128,2048]{2,1,0:T(8,128)(2,1)}, bf16[2,128,2048]{2,1,0:T(8,128)(2,1)S(1)}, u32[]{:S(2)}, u32[]{:S(2)}) collective-permute-start(bf16[2,128,2048]{2,1,0:T(8,128)(2,1)} %own_ref.1), channel_id=1, source_target_pairs={{0,32},{32,0},{64,96},{96,64},{128,160},{160,128},{192,224},{224,1... | collective-permute-start | bytes 3145736 | tf_op jit(solution)/shard_map/ppermute | solution.py:139
  9.9 3.4 %collective-permute-start = (bf16[896,128]{1,0:T(8,128)(2,1)S(1)}, bf16[896,128]{1,0:T(8,128)(2,1)S(1)}, u32[]{:S(2)}, u32[]{:S(2)}) collective-permute-start(bf16[896,128]{1,0:T(8,128)(2,1)S(1)} %pad_maximum_fusion.own_ref), channel_id=1, source_target_pairs={{0,32},{32,0},{64,96},{96,64},{128,160},{160,128},{192,224},{224,1... | collective-permute-start | bytes 688136 | tf_op jit(solution)/shard_map/ppermute | solution.py:138
  13.3 0.7 %copy-start.1 = (s32[4096]{0:T(1024)S(1)}, s32[4096]{0:T(1024)}, u32[]{:S(2)}) copy-start(s32[4096]{0:T(1024)} %param.9) | copy-start | bytes 49156
  14.0 0.7 %copy-start.2 = (s32[4096]{0:T(1024)S(1)}, s32[4096]{0:T(1024)}, u32[]{:S(2)}) copy-start(s32[4096]{0:T(1024)} %param.10) | copy-start | bytes 49156
  14.7 0.7 %copy-start.3 = (s32[4096]{0:T(1024)S(1)}, s32[4096]{0:T(1024)}, u32[]{:S(2)}) copy-start(s32[4096]{0:T(1024)} %param.11) | copy-start | bytes 49156

commit v2 on v1

v2 whole, which is shorter than its diff:
```python
import functools

import jax
import jax.numpy as jnp
from jax import lax
from jax.experimental import pallas as pl
from jax.experimental.pallas import tpu as pltpu
from jax.sharding import PartitionSpec as P

VAL = 48
CON = 64
FINE = 8
SLICE = 128
HALF = 64
KPAD = 256
STRIPS = 4
VMEM = pltpu.CompilerParams(vmem_limit_bytes=16 * 1024 * 1024)
MOST = pltpu.CompilerParams(vmem_limit_bytes=50 * 1024 * 1024)


def lane_matrix(row):
    return jnp.broadcast_to(row, (128, 128)).T


def one_hot(index):
    lane = lax.broadcasted_iota(jnp.int32, index.shape, 1).astype(jnp.float32)
    low = jnp.where(index == lane, 1.0, 0.0)
    high = jnp.where(index == lane + 128.0, 1.0, 0.0)
    return jnp.concatenate([low, high], 1).astype(jnp.bfloat16)


def densities(valence, conduction):
    width = 2 * SLICE
    v_re, v_im = valence[:, :width], valence[:, width:]
    c_re, c_im = conduction[:, :width], conduction[:, width:]
    return v_re * c_re + v_im * c_im, v_re * c_im - v_im * c_re


def transition_rows(at_ref, start):
    return lane_matrix(at_ref[0, pl.ds(start, 1), :]), lane_matrix(at_ref[1, pl.ds(start, 1), :])


def pick(rows, parity, table):
    i = lax.broadcasted_iota(jnp.int32, (rows, table.shape[0]), 0)
    j = lax.broadcasted_iota(jnp.int32, (rows, table.shape[0]), 1)
    mask = jnp.where(j == 2 * i + parity, 1.0, 0.0).astype(jnp.bfloat16)
    return jnp.dot(mask, table, preferred_element_type=jnp.float32).astype(jnp.bfloat16)


def columns_kernel(own_ref, partner_ref, at_ref, table_ref, out_ref, held):
    core = lax.rem(lax.axis_index("row"), 2)
    column = lax.axis_index("col")
    split = 2 * VAL * 4
    both = jnp.concatenate([own_ref[...], partner_ref[...]], 1)
    for parity in range(2):
        lanes = pl.ds(parity * 2 * SLICE, 2 * SLICE)
        table_ref[0:KPAD, lanes] = pick(KPAD, parity, both[:split])
        table_ref[KPAD:, lanes] = pick(KPAD, parity, both[split:])
    v_at, c_at = transition_rows(at_ref, column)
    valence = jnp.dot(one_hot(v_at), table_ref[0:KPAD, :], preferred_element_type=jnp.float32)
    conduction = jnp.dot(one_hot(c_at), table_ref[KPAD:, :], preferred_element_type=jnp.float32)
    real, imag = densities(valence, conduction)
    held[0] = real
    held[1] = imag
    rows = pl.ds(pl.multiple_of(core * HALF, HALF), HALF)
    own = pl.ds(pl.multiple_of(core * SLICE, SLICE), SLICE)
    partner = pl.ds(pl.multiple_of((1 - core) * SLICE, SLICE), SLICE)
    for part in range(2):
        mine = held[part, rows, :].astype(jnp.bfloat16)
        for copy in range(out_ref.shape[0]):
            out_ref[copy, part * HALF : (part + 1) * HALF, own] = mine[:, :SLICE]
            out_ref[copy, part * HALF : (part + 1) * HALF, partner] = mine[:, SLICE:]


def direct_kernel(pairs_ref, own_ref, partner_ref, density_ref, out_ref, screened):
    @pl.when(pl.program_id(0) == 0)
    def _():
        first = lax.broadcasted_iota(jnp.int32, (SLICE, 2 * HALF), 1) < HALF
        sign = jnp.where(first, -1.0, 1.0)
        width = pairs_ref.shape[2]
        for half, w_ref in enumerate((own_ref, partner_ref)):
            parts = []
            for part in range(2):
                total = jnp.zeros((SLICE, 2 * HALF), jnp.float32)
                for chip in range(pairs_ref.shape[0]):
                    total += lax.dot_general(
                        w_ref[part, :, chip * width : (chip + 1) * width],
                        pairs_ref[chip],
                        (((1,), (1,)), ((), ())),
                        preferred_element_type=jnp.float32,
                    )
                parts.append(total)
            x = (parts[0] + sign * pltpu.roll(parts[1], HALF, 1)).astype(jnp.bfloat16)
            screened[half * SLICE : (half + 1) * SLICE, :] = x
            x = x.astype(jnp.float32)
            turned = -sign * pltpu.roll(x, HALF, 1)
            screened[(2 + half) * SLICE : (3 + half) * SLICE, :] = turned.astype(jnp.bfloat16)

    direct = jnp.dot(density_ref[...], screened[...], preferred_element_type=jnp.float32)
    direct = direct.reshape(STRIPS, 16, FINE, 2 * HALF)
    out_ref[...] = jnp.concatenate([direct[s] for s in range(STRIPS)], 1).astype(jnp.bfloat16)


def rows_kernel(table_ref, at_ref, density_ref):
    v_at, c_at = [], []
    for s in range(STRIPS):
        v, c = transition_rows(at_ref, pl.program_id(0) * STRIPS + s)
        v_at.append(v)
        c_at.append(c)
    valence = jnp.dot(one_hot(jnp.concatenate(v_at, 0)), table_ref[0:KPAD, :], preferred_element_type=jnp.float32)
    conduction = jnp.dot(one_hot(jnp.concatenate(c_at, 0)), table_ref[KPAD:, :], preferred_element_type=jnp.float32)
    density_ref[...] = jnp.concatenate(densities(valence, conduction), 1).astype(jnp.bfloat16)


def total_kernel(in_ref, out_ref):
    first = lax.broadcasted_iota(jnp.int32, (in_ref.shape[1], 2 * HALF), 1) < HALF
    sums = []
    for core in range(2):
        total = in_ref[core].astype(jnp.float32)
        for chip in range(1, in_ref.shape[0] // 2):
            total += in_ref[2 * chip + core].astype(jnp.float32)
        sums.append(total)
    out_ref[0] = jnp.where(first, sums[0], pltpu.roll(sums[1], HALF, 1))
    out_ref[1] = jnp.where(first, pltpu.roll(sums[0], HALF, 1), sums[1])


def whole(array):
    return pl.BlockSpec(array.shape, lambda *_: (0,) * array.ndim)


def shards(valence_orbitals, conduction_orbitals, screened, valence_index, conduction_index, kpoint_index):
    rows = lax.axis_size("row")
    chips = rows // 2
    swap = [(i, i ^ 1) for i in range(rows)]
    same_core = [[2 * chip + core for chip in range(chips)] for core in range(2)]
    tables = jnp.concatenate(
        [valence_orbitals.reshape(-1, SLICE), conduction_orbitals.reshape(-1, SLICE)], 0
    )
    screened, tables = lax.optimization_barrier((screened, tables))
    partner_screened = lax.ppermute(screened, "row", swap)
    partner_tables = lax.ppermute(tables, "row", swap)
    at = jnp.stack([kpoint_index * VAL + valence_index, kpoint_index * CON + conduction_index])
    at = at.reshape(2, -1, 128).astype(jnp.float32)
    strips = at.shape[1]
    steps = strips // STRIPS
    bf16 = jnp.bfloat16
    table, pairs = pl.pallas_call(
        columns_kernel,
        out_shape=(
            jax.ShapeDtypeStruct((2 * KPAD, 4 * SLICE), bf16),
            jax.ShapeDtypeStruct((chips, 2 * HALF, 2 * SLICE), bf16),
        ),
        scratch_shapes=[pltpu.VMEM((2, 128, 2 * SLICE), jnp.float32)],
        compiler_params=VMEM,
        name="columns",
    )(tables, partner_tables, at)
    pairs = lax.all_to_all(pairs, "row", 0, 0, axis_index_groups=same_core, tiled=True)
    density = pl.pallas_call(
        rows_kernel,
        out_shape=jax.ShapeDtypeStruct((strips * 128, 4 * SLICE), bf16),
        grid=(steps,),
        in_specs=[whole(table), whole(at)],
        out_specs=pl.BlockSpec((STRIPS * 128, 4 * SLICE), lambda m: (m, 0)),
        compiler_params=VMEM,
        cost_estimate=pl.CostEstimate(
            flops=4 * strips * 128 * KPAD * 4 * SLICE, bytes_accessed=5 << 20, transcendentals=0
        ),
        name="rows",
    )(table, at)
    partial = pl.pallas_call(
        direct_kernel,
        out_shape=jax.ShapeDtypeStruct((rows, strips * FINE, 2 * HALF), bf16),
        grid=(steps,),
        in_specs=[
            whole(pairs),
            whole(screened),
            whole(partner_screened),
            pl.BlockSpec((STRIPS * 128, 4 * SLICE), lambda m: (m, 0)),
        ],
        out_specs=pl.BlockSpec((rows, STRIPS * FINE, 2 * HALF), lambda m: (0, m, 0)),
        scratch_shapes=[pltpu.VMEM((4 * SLICE, 2 * HALF), bf16)],
        compiler_params=MOST,
        name="direct",
    )(pairs, screened, partner_screened, density)
    partial = lax.all_to_all(partial, "row", 0, 0, tiled=True)
    out = pl.pallas_call(
        total_kernel,
        out_shape=jax.ShapeDtypeStruct((2, partial.shape[1], 2 * HALF), jnp.float32),
        compiler_params=VMEM,
        name="total",
    )(partial)
    return out.reshape(2, strips, FINE, 2 * HALF)


def solution(mesh):
    in_specs = (
        P(None, None, None, "row"),
        P(None, None, None, "row"),
        P(None, "row", None),
        P(),
        P(),
        P(),
    )
    return jax.shard_map(
        shards, mesh=mesh, in_specs=in_specs, out_specs=P(None, None, "row", "col"), check_vma=False
    )
```

time: 56.8 us -> 55.3 us (0.974)
  blocking collectives: 31.5 us -> 18.8 us
  Pallas kernels: 9.39 us -> 13.2 us
  waiting for transfers between devices: 1.46 us -> 4.96 us
  starting transfers between devices: 10.8 us -> 14.2 us
  other arithmetic: 0.97 us -> 1.74 us
    all_to_all x1 -> x0, blocking collectives: 12.7 us -> none  [shards(): lax.all_to_all(pairs, 'row', 0, 0, axis_index_groups=same_core, tiled=True)]
    all_to_all x0 -> x1, waiting for transfers between devices: none -> 4.27 us  [shards(): lax.all_to_all(pairs, 'row', 0, 0, axis_index_groups=same_core, tiled=True)]
    all_to_all x0 -> x1, starting transfers between devices: none -> 3.49 us  [shards(): lax.all_to_all(pairs, 'row', 0, 0, axis_index_groups=same_core, tiled=True)]
    pallas_call x1 -> x2, Pallas kernels: 7.76 us -> 10.7 us  [the longest x1 6.73 us: shards(): pl.pallas_call(direct_kernel, out_shape=jax.ShapeDtypeStruct((rows, strip...]
    pallas_call x1, Pallas kernels: 0.72 us -> 1.53 us  [shards(): pl.pallas_call(columns_kernel, out_shape=(jax.ShapeDtypeStruct((2 * KPAD,...]
    ppermute x1, waiting for transfers between devices: 1.45 us -> 0.69 us  [shards(): partner_tables = lax.ppermute(tables, 'row', swap)]
    another operation x0 -> x1, other arithmetic: none -> 0.76 us  [shards(): jnp.stack([kpoint_index * VAL + valence_index, kpoint_index * CON + condu...]
    unnamed x8 -> x4, local copies, waits for them, and re-layouts: 2.15 us -> 1.94 us
  transfers between devices with their start and end apart: 2 -> 3, of which waited for: 1 -> 2; matrix products, arithmetic and copies ran while one was open for 2% -> 1% of each run, Pallas kernels for 1% -> 10%
where the time goes in v2:
time: 55.3 us; the launch traced here: 54.8 us
  blocking collectives  18.8 us (34%)
  starting transfers between devices  14.2 us (26%)
  Pallas kernels  13.2 us (24%)
  waiting for transfers between devices  4.96 us (9%)
  local copies, waits for them, and re-layouts  1.94 us (4%)
  other arithmetic  1.74 us (3%)
    all_to_all x1, blocking collectives, shards(): partial = lax.all_to_all(partial, 'row', 0, 0, tiled=True)  18.8 us
    ppermute x1, starting transfers between devices, shards(): partner_screened = lax.ppermute(screened, 'row', swap)  8.79 us
    pallas_call x1, Pallas kernels, shards(): pl.pallas_call(direct_kernel, out_shape=jax.ShapeDtypeStruct((rows, strip...  6.73 us
    all_to_all x1, waiting for transfers between devices, shards(): lax.all_to_all(pairs, 'row', 0, 0, axis_index_groups=same_core, tiled=True)  4.27 us
    pallas_call x1, Pallas kernels, shards(): pl.pallas_call(rows_kernel, out_shape=jax.ShapeDtypeStruct((strips * 128,...  4.01 us
    all_to_all x1, starting transfers between devices, shards(): lax.all_to_all(pairs, 'row', 0, 0, axis_index_groups=same_core, tiled=True)  3.49 us
    unnamed x4, local copies, waits for them, and re-layouts  1.94 us
    ppermute x1, starting transfers between devices, shards(): partner_tables = lax.ppermute(tables, 'row', swap)  1.92 us
  transfers between devices with their start and end apart: 3, of which 2 were waited for; matrix products, arithmetic and copies ran while one was open for 1% of the time, Pallas kernels for 10%

profile of v2, /device:TPU:1, one launch (start us, length us, event | category | flops | bytes accessed | tf_op | source)
XLA Modules:
  0.0 54.8 jit_solution(11970810655773771647)
XLA Ops:
  0.0 1.0 %pad_maximum_fusion.own_ref = bf16[896,128]{1,0:T(8,128)(2,1)S(1)} fusion(bf16[512,128]{1,0:T(8,128)(2,1)} %bitcast.7, bf16[384,128]{1,0:T(8,128)(2,1)} %bitcast.8), kind=kLoop, calls=%fused_computation | loop fusion | flops 458752 | bytes 458752 | tf_op jit(solution)/shard_map/concatenate | solution.py:136
  1.0 8.8 %collective-permute-start.1 = (bf16[2,128,2048]{2,1,0:T(8,128)(2,1)}, bf16[2,128,2048]{2,1,0:T(8,128)(2,1)S(1)}, u32[]{:S(2)}, u32[]{:S(2)}) collective-permute-start(bf16[2,128,2048]{2,1,0:T(8,128)(2,1)} %own_ref), channel_id=1, source_target_pairs={{0,32},{32,0},{64,96},{96,64},{128,160},{160,128},{192,224},{224,1... | collective-permute-start | bytes 3145736 | tf_op jit(solution)/shard_map/ppermute | solution.py:140
  9.8 1.9 %collective-permute-start = (bf16[896,128]{1,0:T(8,128)(2,1)S(1)}, bf16[896,128]{1,0:T(8,128)(2,1)S(1)}, u32[]{:S(2)}, u32[]{:S(2)}) collective-permute-start(bf16[896,128]{1,0:T(8,128)(2,1)S(1)} %pad_maximum_fusion.own_ref), channel_id=1, source_target_pairs={{0,32},{32,0},{64,96},{96,64},{128,160},{160,128},{192,224},{224,1... | collective-permute-start | bytes 688136 | tf_op jit(solution)/shard_map/ppermute | solution.py:141
  11.7 0.8 %add_bitcast_fusion.1 = (s32[1,32,128]{2,1,0:T(8,128)S(1)}, s32[1,32,128]{2,1,0:T(8,128)S(1)}) fusion(s32[4096]{0:T(1024)} %param.9, s32[4096]{0:T(1024)} %param.11, s32[4096]{0:T(1024)} %param.10), kind=kLoop, calls=%fused_computation.3 | loop fusion | flops 16384 | bytes 81920 | tf_op jit(solution)/shard_map/stack | solution.py:142
  12.5 0.7 %collective-permute-done.partner_ref = bf16[896,128]{1,0:T(8,128)(2,1)S(1)} collective-permute-done((bf16[896,128]{1,0:T(8,128)(2,1)S(1)}, bf16[896,128]{1,0:T(8,128)(2,1)S(1)}, u32[]{:S(2)}, u32[]{:S(2)}) %collective-permute-start) | collective-permute-done | bytes 229408 | tf_op jit(solution)/shard_map/ppermute | solution.py:141
  13.2 1.5 %columns.1 = (bf16[512,512]{1,0:T(8,128)(2,1)S(1)}, bf16[8,128,256]{2,1,0:T(8,128)(2,1)}) custom-call(bf16[896,128]{1,0:T(8,128)(2,1)S(1)} %pad_maximum_fusion.own_ref, bf16[896,128]{1,0:T(8,128)(2,1)S(1)} %collective-permute-done.partner_ref, f32[2,32,128]{2,1,0:T(8,128)S(1)} %add_convert_fusion.at_ref), custom_call_target="tpu_custom_call" | custom-call | tf_op jit(solution)/shard_map/columns/pallas_call | solution.py:147
  14.7 3.5 %all-to-all-start = ((bf16[8,128,256]{2,1,0:T(8,128)(2,1)}), bf16[8,128,256]{2,1,0:T(8,128)(2,1)S(1)}, u32[]{:S(2)}, u32[]{:S(2)}) async-start(bf16[8,128,256]{2,1,0:T(8,128)(2,1)} %get-tuple-element.10), calls=%async_computation | async-start | bytes 1048576 | tf_op jit(solution)/shard_map/all_to_all | solution.py:157
  18.2 0.0 copy-start.1
  18.2 4.0 %rows.1.density_ref = bf16[4096,512]{1,0:T(8,128)(2,1)S(1)} custom-call(bf16[512,512]{1,0:T(8,128)(2,1)S(1)} %get-tuple-element.12.table_ref, f32[2,32,128]{2,1,0:T(8,128)S(1)} %add_convert_fusion.at_ref), custom_call_target="tpu_custom_call" | custom-call | flops 2147483648 | bytes 5242880 | tf_op jit(solution)/shard_map/rows/pallas_call | solution.py:158
  22.2 0.0 copy-start
  22.2 1.9 %copy-done = bf16[4096,512]{1,0:T(8,128)(2,1)} copy-done((bf16[4096,512]{1,0:T(8,128)(2,1)}, bf16[4096,512]{1,0:T(8,128)(2,1)S(1)}, u32[]{:S(2)}) %copy-start) | copy-done | bytes 4194328
  24.2 4.3 %all-to-all-done.pairs_ref = bf16[8,128,256]{2,1,0:T(8,128)(2,1)S(1)} async-done(((bf16[8,128,256]{2,1,0:T(8,128)(2,1)}), bf16[8,128,256]{2,1,0:T(8,128)(2,1)S(1)}, u32[]{:S(2)}, u32[]{:S(2)}) %all-to-all-start) | async-done | bytes 524320 | tf_op jit(solution)/shard_map/all_to_all | solution.py:157
  28.4 0.0 collective-permute-done.1.partner_ref
  28.4 0.0 copy-done.1
  28.4 6.7 %direct.1 = bf16[16,256,128]{2,1,0:T(8,128)(2,1)S(1)} custom-call(bf16[8,128,256]{2,1,0:T(8,128)(2,1)S(1)} %all-to-all-done.pairs_ref, bf16[2,128,2048]{2,1,0:T(8,128)(2,1)S(1)} %copy-done.1, bf16[2,128,2048]{2,1,0:T(8,128)(2,1)S(1)} %collective-permute-done.1.partner_ref, bf16[4096,512]{1,0:T(8,128)(2,1)} %copy-done), custom_call_target="tpu_custom_call" | custom-call | tf_op jit(solution)/shard_map/direct/pallas_call | solution.py:170
  35.2 18.8 %all_to_all.10.in_ref = bf16[16,256,128]{2,1,0:T(8,128)(2,1)S(1)} all-to-all(bf16[16,256,128]{2,1,0:T(8,128)(2,1)S(1)} %direct.1), channel_id=1, replica_groups=mesh['row'=16,'col'=32] {'row'}, dimensions={0} | all-to-all | bytes 2097152 | tf_op jit(solution)/shard_map/all_to_all | solution.py:185
  53.9 0.9 %total.1 = f32[2,256,128]{2,1,0:T(8,128)} custom-call(bf16[16,256,128]{2,1,0:T(8,128)(2,1)S(1)} %all_to_all.10.in_ref), custom_call_target="tpu_custom_call" | custom-call | tf_op jit(solution)/shard_map/total/pallas_call | solution.py:186
  (1 shorter events, 0.0 us)
Async XLA Ops:
  1.0 27.5 %collective-permute-start.1 = (bf16[2,128,2048]{2,1,0:T(8,128)(2,1)}, bf16[2,128,2048]{2,1,0:T(8,128)(2,1)S(1)}, u32[]{:S(2)}, u32[]{:S(2)}) collective-permute-start(bf16[2,128,2048]{2,1,0:T(8,128)(2,1)} %own_ref), channel_id=1, source_target_pairs={{0,32},{32,0},{64,96},{96,64},{128,160},{160,128},{192,224},{224,1... | collective-permute-start | bytes 3145736 | tf_op jit(solution)/shard_map/ppermute | solution.py:140
  9.8 3.4 %collective-permute-start = (bf16[896,128]{1,0:T(8,128)(2,1)S(1)}, bf16[896,128]{1,0:T(8,128)(2,1)S(1)}, u32[]{:S(2)}, u32[]{:S(2)}) collective-permute-start(bf16[896,128]{1,0:T(8,128)(2,1)S(1)} %pad_maximum_fusion.own_ref), channel_id=1, source_target_pairs={{0,32},{32,0},{64,96},{96,64},{128,160},{160,128},{192,224},{224,1... | collective-permute-start | bytes 688136 | tf_op jit(solution)/shard_map/ppermute | solution.py:141
  14.7 13.7 %all-to-all-start = ((bf16[8,128,256]{2,1,0:T(8,128)(2,1)}), bf16[8,128,256]{2,1,0:T(8,128)(2,1)S(1)}, u32[]{:S(2)}, u32[]{:S(2)}) async-start(bf16[8,128,256]{2,1,0:T(8,128)(2,1)} %get-tuple-element.10), calls=%async_computation | async-start | bytes 1048576 | tf_op jit(solution)/shard_map/all_to_all | solution.py:157
  18.2 10.3 %copy-start.1 = (bf16[2,128,2048]{2,1,0:T(8,128)(2,1)S(1)}, bf16[2,128,2048]{2,1,0:T(8,128)(2,1)}, u32[]{:S(2)}) copy-start(bf16[2,128,2048]{2,1,0:T(8,128)(2,1)} %own_ref) | copy-start | bytes 3145732
  22.2 1.9 %copy-start = (bf16[4096,512]{1,0:T(8,128)(2,1)}, bf16[4096,512]{1,0:T(8,128)(2,1)S(1)}, u32[]{:S(2)}) copy-start(bf16[4096,512]{1,0:T(8,128)(2,1)S(1)} %rows.1.density_ref) | copy-start | bytes 12582916

commit v3 on v2

v3 whole, which is shorter than its diff:
```python
import functools

import jax
import jax.numpy as jnp
from jax import lax
from jax.experimental import pallas as pl
from jax.experimental.pallas import tpu as pltpu
from jax.sharding import PartitionSpec as P

VAL = 48
CON = 64
FINE = 8
SLICE = 128
HALF = 64
KPAD = 256
STRIPS = 8
VMEM = pltpu.CompilerParams(vmem_limit_bytes=16 * 1024 * 1024)
MOST = pltpu.CompilerParams(vmem_limit_bytes=50 * 1024 * 1024)


def lane_matrix(row):
    return jnp.broadcast_to(row, (128, 128)).T


def one_hot(index, width):
    lane = lax.broadcasted_iota(jnp.int32, index.shape, 1).astype(jnp.float32)
    parts = [jnp.where(index == lane + float(at), 1.0, 0.0) for at in range(0, width, index.shape[1])]
    return jnp.concatenate(parts, 1).astype(jnp.bfloat16)


def densities(valence, conduction):
    width = 2 * SLICE
    v_re, v_im = valence[:, :width], valence[:, width:]
    c_re, c_im = conduction[:, :width], conduction[:, width:]
    return v_re * c_re + v_im * c_im, v_re * c_im - v_im * c_re


def transition_rows(at_ref, start):
    return lane_matrix(at_ref[0, pl.ds(start, 1), :]), lane_matrix(at_ref[1, pl.ds(start, 1), :])


def pick(rows, parity, table):
    i = lax.broadcasted_iota(jnp.int32, (rows, table.shape[0]), 0)
    j = lax.broadcasted_iota(jnp.int32, (rows, table.shape[0]), 1)
    mask = jnp.where(j == 2 * i + parity, 1.0, 0.0).astype(jnp.bfloat16)
    return jnp.dot(mask, table, preferred_element_type=jnp.float32).astype(jnp.bfloat16)


def columns_kernel(own_ref, partner_ref, at_ref, out_ref, held):
    core = lax.rem(lax.axis_index("row"), 2)
    split = 2 * VAL * 4
    both = jnp.concatenate([own_ref[...], partner_ref[...]], 1)
    picked = []
    for index, table in zip(transition_rows(at_ref, lax.axis_index("col")), (both[:split], both[split:])):
        for parity in range(2):
            hot = one_hot(2.0 * index + parity, table.shape[0])
            picked.append(jnp.dot(hot, table, preferred_element_type=jnp.float32))
    v_re, v_im, c_re, c_im = picked
    real = (v_re * c_re + v_im * c_im).T
    imag = (v_re * c_im - v_im * c_re).T
    first = lax.broadcasted_iota(jnp.int32, real.shape, 1) < HALF
    held[0] = jnp.where(first, real, pltpu.roll(imag, HALF, 1))
    held[1] = jnp.where(first, pltpu.roll(real, HALF, 1), imag)
    mine = held[core].astype(jnp.bfloat16)
    own = pl.ds(pl.multiple_of(core * SLICE, SLICE), SLICE)
    partner = pl.ds(pl.multiple_of((1 - core) * SLICE, SLICE), SLICE)
    for copy in range(out_ref.shape[0]):
        out_ref[copy, own, :] = mine[:SLICE]
        out_ref[copy, partner, :] = mine[SLICE:]


def rows_kernel(own_ref, partner_ref, at_ref, density_ref, table):
    @pl.when(pl.program_id(0) == 0)
    def _():
        both = jnp.concatenate([own_ref[...], partner_ref[...]], 1)
        split = 2 * VAL * 4
        for parity in range(2):
            lanes = pl.ds(parity * 2 * SLICE, 2 * SLICE)
            table[0:KPAD, lanes] = pick(KPAD, parity, both[:split])
            table[KPAD:, lanes] = pick(KPAD, parity, both[split:])

    v_at, c_at = [], []
    for s in range(STRIPS):
        v, c = transition_rows(at_ref, pl.program_id(0) * STRIPS + s)
        v_at.append(v)
        c_at.append(c)
    valence = jnp.dot(one_hot(jnp.concatenate(v_at, 0), KPAD), table[0:KPAD, :], preferred_element_type=jnp.float32)
    conduction = jnp.dot(one_hot(jnp.concatenate(c_at, 0), KPAD), table[KPAD:, :], preferred_element_type=jnp.float32)
    density_ref[...] = jnp.concatenate(densities(valence, conduction), 1).astype(jnp.bfloat16)


def direct_kernel(pairs_ref, own_ref, partner_ref, density_ref, out_ref, held, screened, sems):
    steps, strip = held.shape[:2]
    copies = []
    for m in range(steps):
        span = pl.ds(m * strip, strip)
        copies.append(pltpu.make_async_copy(density_ref.at[span, :], held.at[m], sems.at[m]))
    for copy in copies:
        copy.start()
    first = lax.broadcasted_iota(jnp.int32, (SLICE, 2 * HALF), 1) < HALF
    sign = jnp.where(first, -1.0, 1.0)
    pairs = pairs_ref[...].reshape(-1, 2 * HALF)
    for half, w_ref in enumerate((own_ref, partner_ref)):
        parts = [jnp.dot(w_ref[part], pairs, preferred_element_type=jnp.float32) for part in range(2)]
        x = (parts[0] + sign * pltpu.roll(parts[1], HALF, 1)).astype(jnp.bfloat16)
        screened[half * SLICE : (half + 1) * SLICE, :] = x
        turned = -sign * pltpu.roll(x.astype(jnp.float32), HALF, 1)
        screened[(2 + half) * SLICE : (3 + half) * SLICE, :] = turned.astype(jnp.bfloat16)
    lanes = strip // 16
    for m, copy in enumerate(copies):
        copy.wait()
        direct = jnp.dot(held[m], screened[...], preferred_element_type=jnp.float32)
        direct = direct.reshape(strip // 128, 16, FINE, 2 * HALF)
        direct = jnp.concatenate([direct[s] for s in range(strip // 128)], 1).astype(jnp.bfloat16)
        out_ref[:, m * lanes : (m + 1) * lanes, :] = direct


def total_kernel(in_ref, out_ref):
    first = lax.broadcasted_iota(jnp.int32, (in_ref.shape[1], 2 * HALF), 1) < HALF
    sums = []
    for core in range(2):
        total = in_ref[core].astype(jnp.float32)
        for chip in range(1, in_ref.shape[0] // 2):
            total += in_ref[2 * chip + core].astype(jnp.float32)
        sums.append(total)
    out_ref[0] = jnp.where(first, sums[0], pltpu.roll(sums[1], HALF, 1))
    out_ref[1] = jnp.where(first, pltpu.roll(sums[0], HALF, 1), sums[1])


def whole(array):
    return pl.BlockSpec(array.shape, lambda *_: (0,) * array.ndim)


def shards(valence_orbitals, conduction_orbitals, screened, valence_index, conduction_index, kpoint_index):
    rows = lax.axis_size("row")
    chips = rows // 2
    swap = [(i, i ^ 1) for i in range(rows)]
    same_core = [[2 * chip + core for chip in range(chips)] for core in range(2)]
    tables = jnp.concatenate(
        [valence_orbitals.reshape(-1, SLICE), conduction_orbitals.reshape(-1, SLICE)], 0
    )
    screened, tables = lax.optimization_barrier((screened, tables))
    partner_screened = lax.ppermute(screened, "row", swap)
    partner_tables = lax.ppermute(tables, "row", swap)
    at = jnp.stack([kpoint_index * VAL + valence_index, kpoint_index * CON + conduction_index])
    at = at.reshape(2, -1, 128).astype(jnp.float32)
    strips = at.shape[1]
    steps = strips // STRIPS
    bf16 = jnp.bfloat16
    pairs = pl.pallas_call(
        columns_kernel,
        out_shape=jax.ShapeDtypeStruct((chips, 2 * SLICE, 2 * HALF), bf16),
        scratch_shapes=[pltpu.VMEM((2, 2 * SLICE, 2 * HALF), jnp.float32)],
        compiler_params=VMEM,
        name="columns",
    )(tables, partner_tables, at)
    pairs = lax.all_to_all(pairs, "row", 0, 0, axis_index_groups=same_core, tiled=True)
    density = pl.pallas_call(
        rows_kernel,
        out_shape=jax.ShapeDtypeStruct((strips * 128, 4 * SLICE), bf16),
        grid=(steps,),
        in_specs=[whole(tables), whole(partner_tables), whole(at)],
        out_specs=pl.BlockSpec((STRIPS * 128, 4 * SLICE), lambda m: (m, 0)),
        scratch_shapes=[pltpu.VMEM((2 * KPAD, 4 * SLICE), bf16)],
        compiler_params=VMEM,
        cost_estimate=pl.CostEstimate(
            flops=4 * strips * 128 * KPAD * 4 * SLICE, bytes_accessed=5 << 20, transcendentals=0
        ),
        name="rows",
    )(tables, partner_tables, at)
    partial = pl.pallas_call(
        direct_kernel,
        out_shape=jax.ShapeDtypeStruct((rows, strips * FINE, 2 * HALF), bf16),
        in_specs=[pl.BlockSpec(memory_space=pltpu.VMEM)] * 3 + [pl.BlockSpec(memory_space=pl.ANY)],
        scratch_shapes=[
            pltpu.VMEM((steps, STRIPS * 128, 4 * SLICE), bf16),
            pltpu.VMEM((4 * SLICE, 2 * HALF), bf16),
            pltpu.SemaphoreType.DMA((steps,)),
        ],
        compiler_params=MOST,
        name="direct",
    )(pairs, screened, partner_screened, density)
    partial = lax.all_to_all(partial, "row", 0, 0, tiled=True)
    out = pl.pallas_call(
        total_kernel,
        out_shape=jax.ShapeDtypeStruct((2, partial.shape[1], 2 * HALF), jnp.float32),
        compiler_params=VMEM,
        name="total",
    )(partial)
    return out.reshape(2, strips, FINE, 2 * HALF)


def solution(mesh):
    in_specs = (
        P(None, None, None, "row"),
        P(None, None, None, "row"),
        P(None, "row", None),
        P(),
        P(),
        P(),
    )
    return jax.shard_map(
        shards, mesh=mesh, in_specs=in_specs, out_specs=P(None, None, "row", "col"), check_vma=False
    )
```

time: 55.3 us -> 52.9 us (0.957)
  Pallas kernels: 13.2 us -> 10.5 us
    pallas_call x1, Pallas kernels: 6.73 us -> 4.59 us  [shards(): pl.pallas_call(direct_kernel, out_shape=jax.ShapeDtypeStruct((rows, strip...]
where the time goes in v3:
time: 52.9 us; the launch traced here: 52.6 us
  blocking collectives  18.8 us (36%)
  starting transfers between devices  14.2 us (27%)
  Pallas kernels  10.5 us (20%)
  waiting for transfers between devices  5.37 us (10%)
  local copies, waits for them, and re-layouts  1.94 us (4%)
  other arithmetic  1.74 us (3%)
    all_to_all x1, blocking collectives, shards(): partial = lax.all_to_all(partial, 'row', 0, 0, tiled=True)  18.8 us
    ppermute x1, starting transfers between devices, shards(): partner_screened = lax.ppermute(screened, 'row', swap)  8.79 us
    all_to_all x1, waiting for transfers between devices, shards(): lax.all_to_all(pairs, 'row', 0, 0, axis_index_groups=same_core, tiled=True)  4.69 us
    pallas_call x1, Pallas kernels, shards(): pl.pallas_call(direct_kernel, out_shape=jax.ShapeDtypeStruct((rows, strip...  4.59 us
    pallas_call x1, Pallas kernels, shards(): pl.pallas_call(rows_kernel, out_shape=jax.ShapeDtypeStruct((strips * 128,...  3.59 us
    all_to_all x1, starting transfers between devices, shards(): lax.all_to_all(pairs, 'row', 0, 0, axis_index_groups=same_core, tiled=True)  3.49 us
    unnamed x4, local copies, waits for them, and re-layouts  1.94 us
    ppermute x1, starting transfers between devices, shards(): partner_tables = lax.ppermute(tables, 'row', swap)  1.92 us
  transfers between devices with their start and end apart: 3, of which 2 were waited for; matrix products, arithmetic and copies ran while one was open for 1% of the time, Pallas kernels for 10%

profile of v3, /device:TPU:1, one launch (start us, length us, event | category | flops | bytes accessed | tf_op | source)
XLA Modules:
  0.0 52.6 jit_solution(15439981862714542253)
XLA Ops:
  0.0 1.0 %pad_maximum_fusion.own_ref = bf16[896,128]{1,0:T(8,128)(2,1)S(1)} fusion(bf16[512,128]{1,0:T(8,128)(2,1)} %bitcast.7, bf16[384,128]{1,0:T(8,128)(2,1)} %bitcast.8), kind=kLoop, calls=%fused_computation | loop fusion | flops 458752 | bytes 458752 | tf_op jit(solution)/shard_map/concatenate | solution.py:139
  1.0 8.8 %collective-permute-start.1 = (bf16[2,128,2048]{2,1,0:T(8,128)(2,1)}, bf16[2,128,2048]{2,1,0:T(8,128)(2,1)S(1)}, u32[]{:S(2)}, u32[]{:S(2)}) collective-permute-start(bf16[2,128,2048]{2,1,0:T(8,128)(2,1)} %own_ref), channel_id=1, source_target_pairs={{0,32},{32,0},{64,96},{96,64},{128,160},{160,128},{192,224},{224,1... | collective-permute-start | bytes 3145736 | tf_op jit(solution)/shard_map/ppermute | solution.py:143
  9.8 1.9 %collective-permute-start = (bf16[896,128]{1,0:T(8,128)(2,1)S(1)}, bf16[896,128]{1,0:T(8,128)(2,1)S(1)}, u32[]{:S(2)}, u32[]{:S(2)}) collective-permute-start(bf16[896,128]{1,0:T(8,128)(2,1)S(1)} %pad_maximum_fusion.own_ref), channel_id=1, source_target_pairs={{0,32},{32,0},{64,96},{96,64},{128,160},{160,128},{192,224},{224,1... | collective-permute-start | bytes 688136 | tf_op jit(solution)/shard_map/ppermute | solution.py:144
  11.7 0.8 %add_bitcast_fusion.1 = (s32[1,32,128]{2,1,0:T(8,128)S(1)}, s32[1,32,128]{2,1,0:T(8,128)S(1)}) fusion(s32[4096]{0:T(1024)} %param.9, s32[4096]{0:T(1024)} %param.11, s32[4096]{0:T(1024)} %param.10), kind=kLoop, calls=%fused_computation.3 | loop fusion | flops 16384 | bytes 81920 | tf_op jit(solution)/shard_map/stack | solution.py:145
  12.5 0.7 %collective-permute-done.partner_ref = bf16[896,128]{1,0:T(8,128)(2,1)S(1)} collective-permute-done((bf16[896,128]{1,0:T(8,128)(2,1)S(1)}, bf16[896,128]{1,0:T(8,128)(2,1)S(1)}, u32[]{:S(2)}, u32[]{:S(2)}) %collective-permute-start) | collective-permute-done | bytes 229408 | tf_op jit(solution)/shard_map/ppermute | solution.py:144
  13.2 1.4 %columns.1 = bf16[8,256,128]{2,1,0:T(8,128)(2,1)} custom-call(bf16[896,128]{1,0:T(8,128)(2,1)S(1)} %pad_maximum_fusion.own_ref, bf16[896,128]{1,0:T(8,128)(2,1)S(1)} %collective-permute-done.partner_ref, f32[2,32,128]{2,1,0:T(8,128)S(1)} %add_convert_fusion.at_ref), custom_call_target="tpu_custom_call" | custom-call | tf_op jit(solution)/shard_map/columns/pallas_call | solution.py:150
  14.6 3.5 %all-to-all-start = ((bf16[8,256,128]{2,1,0:T(8,128)(2,1)}), bf16[8,256,128]{2,1,0:T(8,128)(2,1)S(1)}, u32[]{:S(2)}, u32[]{:S(2)}) async-start(bf16[8,256,128]{2,1,0:T(8,128)(2,1)} %columns.1), calls=%async_computation | async-start | bytes 1048576 | tf_op jit(solution)/shard_map/all_to_all | solution.py:157
  18.1 0.0 copy-start.1
  18.1 3.6 %rows.1.density_ref = bf16[4096,512]{1,0:T(8,128)(2,1)S(1)} custom-call(bf16[896,128]{1,0:T(8,128)(2,1)S(1)} %pad_maximum_fusion.own_ref, bf16[896,128]{1,0:T(8,128)(2,1)S(1)} %collective-permute-done.partner_ref, f32[2,32,128]{2,1,0:T(8,128)S(1)} %add_convert_fusion.at_ref), custom_call_target="tpu_custom_call" | custom-call | flops 2147483648 | bytes 5242880 | tf_op jit(solution)/shard_map/rows/pallas_call | solution.py:158
  21.7 0.0 copy-start
  21.7 1.9 %copy-done = bf16[4096,512]{1,0:T(8,128)(2,1)} copy-done((bf16[4096,512]{1,0:T(8,128)(2,1)}, bf16[4096,512]{1,0:T(8,128)(2,1)S(1)}, u32[]{:S(2)}) %copy-start) | copy-done | bytes 4194328
  23.6 4.7 %all-to-all-done.pairs_ref = bf16[8,256,128]{2,1,0:T(8,128)(2,1)S(1)} async-done(((bf16[8,256,128]{2,1,0:T(8,128)(2,1)}), bf16[8,256,128]{2,1,0:T(8,128)(2,1)S(1)}, u32[]{:S(2)}, u32[]{:S(2)}) %all-to-all-start) | async-done | bytes 524320 | tf_op jit(solution)/shard_map/all_to_all | solution.py:157
  28.3 0.0 collective-permute-done.1.partner_ref
  28.3 0.0 copy-done.1
  28.3 4.6 %direct.1 = bf16[16,256,128]{2,1,0:T(8,128)(2,1)S(1)} custom-call(bf16[8,256,128]{2,1,0:T(8,128)(2,1)S(1)} %all-to-all-done.pairs_ref, bf16[2,128,2048]{2,1,0:T(8,128)(2,1)S(1)} %copy-done.1, bf16[2,128,2048]{2,1,0:T(8,128)(2,1)S(1)} %collective-permute-done.1.partner_ref, bf16[4096,512]{1,0:T(8,128)(2,1)} %copy-done), custom_call_target="tpu_custom_call" | custom-call | tf_op jit(solution)/shard_map/direct/pallas_call | solution.py:171
  32.9 18.8 %all_to_all.10.in_ref = bf16[16,256,128]{2,1,0:T(8,128)(2,1)S(1)} all-to-all(bf16[16,256,128]{2,1,0:T(8,128)(2,1)S(1)} %direct.1), channel_id=1, replica_groups=mesh['row'=16,'col'=32] {'row'}, dimensions={0} | all-to-all | bytes 2097152 | tf_op jit(solution)/shard_map/all_to_all | solution.py:183
  51.7 0.9 %total.1 = f32[2,256,128]{2,1,0:T(8,128)} custom-call(bf16[16,256,128]{2,1,0:T(8,128)(2,1)S(1)} %all_to_all.10.in_ref), custom_call_target="tpu_custom_call" | custom-call | tf_op jit(solution)/shard_map/total/pallas_call | solution.py:184
  (1 shorter events, 0.0 us)
Async XLA Ops:
  1.0 27.4 %collective-permute-start.1 = (bf16[2,128,2048]{2,1,0:T(8,128)(2,1)}, bf16[2,128,2048]{2,1,0:T(8,128)(2,1)S(1)}, u32[]{:S(2)}, u32[]{:S(2)}) collective-permute-start(bf16[2,128,2048]{2,1,0:T(8,128)(2,1)} %own_ref), channel_id=1, source_target_pairs={{0,32},{32,0},{64,96},{96,64},{128,160},{160,128},{192,224},{224,1... | collective-permute-start | bytes 3145736 | tf_op jit(solution)/shard_map/ppermute | solution.py:143
  9.8 3.4 %collective-permute-start = (bf16[896,128]{1,0:T(8,128)(2,1)S(1)}, bf16[896,128]{1,0:T(8,128)(2,1)S(1)}, u32[]{:S(2)}, u32[]{:S(2)}) collective-permute-start(bf16[896,128]{1,0:T(8,128)(2,1)S(1)} %pad_maximum_fusion.own_ref), channel_id=1, source_target_pairs={{0,32},{32,0},{64,96},{96,64},{128,160},{160,128},{192,224},{224,1... | collective-permute-start | bytes 688136 | tf_op jit(solution)/shard_map/ppermute | solution.py:144
  14.6 13.7 %all-to-all-start = ((bf16[8,256,128]{2,1,0:T(8,128)(2,1)}), bf16[8,256,128]{2,1,0:T(8,128)(2,1)S(1)}, u32[]{:S(2)}, u32[]{:S(2)}) async-start(bf16[8,256,128]{2,1,0:T(8,128)(2,1)} %columns.1), calls=%async_computation | async-start | bytes 1048576 | tf_op jit(solution)/shard_map/all_to_all | solution.py:157
  18.1 10.3 %copy-start.1 = (bf16[2,128,2048]{2,1,0:T(8,128)(2,1)S(1)}, bf16[2,128,2048]{2,1,0:T(8,128)(2,1)}, u32[]{:S(2)}) copy-start(bf16[2,128,2048]{2,1,0:T(8,128)(2,1)} %own_ref) | copy-start | bytes 3145732
  21.7 1.9 %copy-start = (bf16[4096,512]{1,0:T(8,128)(2,1)}, bf16[4096,512]{1,0:T(8,128)(2,1)S(1)}, u32[]{:S(2)}) copy-start(bf16[4096,512]{1,0:T(8,128)(2,1)S(1)} %rows.1.density_ref) | copy-start | bytes 12582916

commit v4 on v3

v4 whole, which is shorter than its diff:
```python
import jax
import jax.numpy as jnp
from jax import lax
from jax.experimental import pallas as pl
from jax.experimental.pallas import tpu as pltpu
from jax.sharding import PartitionSpec as P

VAL = 48
CON = 64
FINE = 8
SLICE = 128
WIDTH = 128
KPAD = 256
RING = (0, 1, 2, 3, 7, 6, 5, 4)
STRIPS = 16
MIB = 1024 * 1024
LITTLE = pltpu.CompilerParams(vmem_limit_bytes=16 * MIB)
MUCH = pltpu.CompilerParams(vmem_limit_bytes=48 * MIB)
ALL = pltpu.CompilerParams(vmem_limit_bytes=63 * MIB)


def core_of():
    return lax.rem(lax.axis_index("row"), 2)


def lane_matrix(row):
    return jnp.broadcast_to(row, (128, 128)).T


def one_hot(index, width):
    lane = lax.broadcasted_iota(jnp.int32, index.shape, 1).astype(jnp.float32)
    parts = [jnp.where(index == lane + float(at), 1.0, 0.0) for at in range(0, width, index.shape[1])]
    return jnp.concatenate(parts, 1).astype(jnp.bfloat16)


def densities(valence, conduction):
    width = valence.shape[1] // 2
    v_re, v_im = valence[:, :width], valence[:, width:]
    c_re, c_im = conduction[:, :width], conduction[:, width:]
    return v_re * c_re + v_im * c_im, v_re * c_im - v_im * c_re


def pick(rows, parity, table):
    i = lax.broadcasted_iota(jnp.int32, (rows, table.shape[0]), 0)
    j = lax.broadcasted_iota(jnp.int32, (rows, table.shape[0]), 1)
    mask = jnp.where(j == 2 * i + parity, 1.0, 0.0).astype(jnp.bfloat16)
    return jnp.dot(mask, table, preferred_element_type=jnp.float32).astype(jnp.bfloat16)


def columns_kernel(
    valence_ref, conduction_ref, v_ref, n_ref, k_ref, w_ref, at_ref, table_ref, out_ref, re_ref, im_ref, sems
):
    core = core_of()
    copies = []
    for part, ref in enumerate((re_ref, im_ref)):
        for place, chip in enumerate(RING):
            lanes = pl.ds(pl.multiple_of((2 * chip + 1 - core) * SLICE, SLICE), SLICE)
            to = ref.at[:, place * SLICE : (place + 1) * SLICE]
            copies.append(pltpu.make_async_copy(w_ref.at[part, :, lanes], to, sems.at[part, place]))
    for copy in copies:
        copy.start()
    split = valence_ref.shape[0]
    table_ref[0:split, :] = valence_ref[...]
    table_ref[split:, :] = conduction_ref[...]
    at_ref[0] = (k_ref[...] * VAL + v_ref[...]).astype(jnp.float32)
    at_ref[1] = (k_ref[...] * CON + n_ref[...]).astype(jnp.float32)
    picked = []
    for which, ref in enumerate((valence_ref, conduction_ref)):
        index = lane_matrix(at_ref[which, pl.ds(lax.axis_index("col"), 1), :])
        parts = []
        for parity in range(2):
            hot = one_hot(2.0 * index + parity, ref.shape[0])
            parts.append(jnp.dot(hot, ref[...], preferred_element_type=jnp.float32))
        picked.append(jnp.concatenate(parts, 1))
    real, imag = densities(*picked)
    both = jnp.concatenate([real.T, imag.T], 1).astype(jnp.bfloat16)
    for place in range(out_ref.shape[0]):
        out_ref[place] = both
    for copy in copies:
        copy.wait()


def rows_kernel(own_ref, partner_ref, at_ref, density_ref, table):
    core = core_of()

    @pl.when(pl.program_id(0) == 0)
    def _():
        both = jnp.concatenate([own_ref[...], partner_ref[...]], 1)
        split = 2 * VAL * 4
        for parity in range(2):
            lanes = pl.ds(parity * 2 * SLICE, 2 * SLICE)
            table[0:KPAD, lanes] = pick(KPAD, parity, both[:split])
            table[KPAD:, lanes] = pick(KPAD, parity, both[split:])

    picked = []
    for which in range(2):
        index = []
        for s in range(STRIPS):
            strip = lane_matrix(at_ref[which, pl.ds(pl.program_id(0) * STRIPS + s, 1), :]).reshape(-1, 2, FINE, 128)
            index.append(jnp.where(core == 0, strip[:, 0], strip[:, 1]).reshape(-1, 128))
        hot = one_hot(jnp.concatenate(index, 0), KPAD)
        picked.append(
            jnp.dot(hot, table[which * KPAD : (which + 1) * KPAD, :], preferred_element_type=jnp.float32)
        )
    density_ref[...] = jnp.concatenate(densities(*picked), 1).astype(jnp.bfloat16)


def screened_kernel(pairs_ref, own_ref, re_ref, im_ref, density_ref, out_ref, near_ref, sem):
    core = core_of()
    copy = pltpu.make_async_copy(density_ref, near_ref, sem)
    copy.start()
    for half in range(2):
        parts = []
        for part in range(2):
            total = jnp.zeros((SLICE, 2 * WIDTH), jnp.float32)
            for place, chip in enumerate(RING):
                if half == 0:
                    w = own_ref[part, :, pl.ds(pl.multiple_of((2 * chip + core) * SLICE, SLICE), SLICE)]
                else:
                    w = (re_ref, im_ref)[part][:, place * SLICE : (place + 1) * SLICE]
                total += jnp.dot(w, pairs_ref[place], preferred_element_type=jnp.float32)
            parts.append(total)
        out_ref[half, :, :WIDTH] = parts[0][:, :WIDTH] - parts[1][:, WIDTH:]
        out_ref[half, :, WIDTH:] = parts[0][:, WIDTH:] + parts[1][:, :WIDTH]
    copy.wait()


def direct_kernel(mine_ref, other_ref, density_ref, out_ref, screened):
    for half in range(2):
        x = (mine_ref[half] + other_ref[1 - half]).astype(jnp.bfloat16)
        screened[half * SLICE : (half + 1) * SLICE, :] = x
        screened[(2 + half) * SLICE : (3 + half) * SLICE, :WIDTH] = x[:, WIDTH:]
        screened[(2 + half) * SLICE : (3 + half) * SLICE, WIDTH:] = -x[:, :WIDTH]
    parts = 4
    rows = density_ref.shape[0] // parts
    strips = rows // 64
    for m in range(parts):
        direct = jnp.dot(
            density_ref[m * rows : (m + 1) * rows, :], screened[...], preferred_element_type=jnp.float32
        )
        direct = direct.reshape(strips, -1, FINE, 2 * WIDTH)
        direct = jnp.concatenate([direct[s] for s in range(strips)], 1).astype(jnp.bfloat16)
        for place, chip in enumerate(RING):
            out_ref[place, m * strips * FINE : (m + 1) * strips * FINE, :] = direct[chip]


def total_kernel(in_ref, out_ref):
    for part in range(2):
        lanes = slice(part * WIDTH, (part + 1) * WIDTH)
        total = in_ref[0, :, lanes].astype(jnp.float32)
        for chip in range(1, in_ref.shape[0]):
            total += in_ref[chip, :, lanes].astype(jnp.float32)
        out_ref[part] = total


def whole(array):
    return pl.BlockSpec(array.shape, lambda *_: (0,) * len(array.shape))


def shards(valence_orbitals, conduction_orbitals, screened, valence_index, conduction_index, kpoint_index):
    bf16, f32 = jnp.bfloat16, jnp.float32
    rows = lax.axis_size("row")
    chips = rows // 2
    swap = [(i, i ^ 1) for i in range(rows)]
    same_core = [[2 * chip + core for chip in RING] for core in range(2)]
    anywhere = pl.BlockSpec(memory_space=pl.ANY)
    in_vmem = pl.BlockSpec(memory_space=pltpu.VMEM)
    index = [array.reshape(-1, 128) for array in (valence_index, conduction_index, kpoint_index)]
    strips = index[0].shape[0]
    valence = valence_orbitals.reshape(-1, SLICE)
    conduction = conduction_orbitals.reshape(-1, SLICE)
    raw = (valence, conduction, *index)
    shapes = (
        jax.ShapeDtypeStruct((2, strips, 128), f32),
        jax.ShapeDtypeStruct((valence.shape[0] + conduction.shape[0], SLICE), bf16),
        jax.ShapeDtypeStruct((chips, SLICE, 2 * WIDTH), bf16),
    )
    half_w = jax.ShapeDtypeStruct((SLICE, chips * SLICE), bf16)
    at, tables, pairs, w_re, w_im = pl.pallas_call(
        columns_kernel,
        out_shape=(*shapes, half_w, half_w),
        grid=(1,),
        in_specs=[whole(array) for array in raw] + [anywhere],
        out_specs=(*[whole(array) for array in shapes], anywhere, anywhere),
        scratch_shapes=[pltpu.SemaphoreType.DMA((2, chips))],
        compiler_params=ALL,
        name="columns",
    )(*raw, screened)
    pairs = lax.all_to_all(pairs, "row", 0, 0, axis_index_groups=same_core, tiled=True)
    partner_tables = lax.ppermute(tables, "row", swap)
    w_re = lax.ppermute(w_re, "row", swap)
    w_im = lax.ppermute(w_im, "row", swap)
    density = pl.pallas_call(
        rows_kernel,
        out_shape=jax.ShapeDtypeStruct((strips * 64, 4 * SLICE), bf16),
        grid=(strips // STRIPS,),
        in_specs=[whole(tables), whole(partner_tables), whole(at)],
        out_specs=pl.BlockSpec((STRIPS * 64, 4 * SLICE), lambda m: (m, 0)),
        scratch_shapes=[pltpu.VMEM((2 * KPAD, 4 * SLICE), bf16)],
        compiler_params=LITTLE,
        cost_estimate=pl.CostEstimate(
            flops=4 * strips * 64 * KPAD * 4 * SLICE, bytes_accessed=3 << 20, transcendentals=0
        ),
        name="rows",
    )(tables, partner_tables, at)
    pairs, density = lax.optimization_barrier((pairs, density))
    mine, density = pl.pallas_call(
        screened_kernel,
        out_shape=(
            jax.ShapeDtypeStruct((2, SLICE, 2 * WIDTH), f32),
            jax.ShapeDtypeStruct(density.shape, bf16),
        ),
        in_specs=[in_vmem] * 4 + [anywhere],
        scratch_shapes=[pltpu.SemaphoreType.DMA],
        compiler_params=MUCH,
        name="screened",
    )(pairs, screened, w_re, w_im, density)
    other = lax.ppermute(mine, "row", swap)
    partial = pl.pallas_call(
        direct_kernel,
        out_shape=jax.ShapeDtypeStruct((chips, strips * FINE, 2 * WIDTH), bf16),
        scratch_shapes=[pltpu.VMEM((4 * SLICE, 2 * WIDTH), bf16)],
        compiler_params=LITTLE,
        name="direct",
    )(mine, other, density)
    partial = lax.all_to_all(partial, "row", 0, 0, axis_index_groups=same_core, tiled=True)
    out = pl.pallas_call(
        total_kernel,
        out_shape=jax.ShapeDtypeStruct((2, strips * FINE, WIDTH), f32),
        compiler_params=LITTLE,
        name="total",
    )(partial)
    return out.reshape(2, strips, FINE, WIDTH)


def solution(mesh):
    in_specs = (
        P(None, None, None, "row"),
        P(None, None, None, "row"),
        P(None, "row", None),
        P(),
        P(),
        P(),
    )
    return jax.shard_map(
        shards, mesh=mesh, in_specs=in_specs, out_specs=P(None, None, "row", "col"), check_vma=False
    )
```

time: 52.9 us -> 67.6 us (1.28)
  Pallas kernels: 10.5 us -> 24.2 us
  starting transfers between devices: 14.2 us -> 18.7 us
  waiting for transfers between devices: 5.37 us -> 1.51 us
  other arithmetic: 1.74 us -> 0 us
  local copies, waits for them, and re-layouts: 1.94 us -> 3.01 us
  blocking collectives: 18.8 us -> 19.5 us
    pallas_call x4 -> x5, Pallas kernels: 10.5 us -> 24.2 us  [the longest x1 19 us: shards(): pl.pallas_call(columns_kernel, out_shape=(*shapes, half_w, half_w), grid=...]
    all_to_all x1, waiting for transfers between devices: 4.69 us -> 0.01 us  [shards(): lax.all_to_all(pairs, 'row', 0, 0, axis_index_groups=same_core, tiled=True)]
    ppermute x1, starting transfers between devices: 1.92 us -> 6.56 us  [shards(): partner_tables = lax.ppermute(tables, 'row', swap)]
    ppermute x1 -> x3, starting transfers between devices: 8.79 us -> 6.25 us  [the longest x1 2.41 us: shards(): w_im = lax.ppermute(w_im, 'row', swap)]
    all_to_all x1, starting transfers between devices: 3.49 us -> 5.87 us  [shards(): lax.all_to_all(pairs, 'row', 0, 0, axis_index_groups=same_core, tiled=True)]
    ppermute x1 -> x3, waiting for transfers between devices: 0.01 us -> 1.5 us  [the longest x1 1.5 us: shards(): other = lax.ppermute(mine, 'row', swap)]
    unnamed x4 -> x8, local copies, waits for them, and re-layouts: 1.94 us -> 3.01 us
    concatenate x1 -> x0, other arithmetic: 0.97 us -> none  [shards(): jnp.concatenate([valence_orbitals.reshape(-1, SLICE), conduction_orbitals...]
  transfers between devices with their start and end apart: 3 -> 5, of which waited for: 2 -> 1; matrix products, arithmetic and copies ran while one was open for 1% -> 0% of each run, Pallas kernels for 10% -> 3%
where the time goes in v4:
time: 67.6 us; the launch traced here: 67 us
  Pallas kernels  24.2 us (36%)
  blocking collectives  19.5 us (29%)
  starting transfers between devices  18.7 us (28%)
  local copies, waits for them, and re-layouts  3.01 us (4%)
  waiting for transfers between devices  1.51 us (2%)
    all_to_all x1, blocking collectives, shards(): lax.all_to_all(partial, 'row', 0, 0, axis_index_groups=same_core, tiled=T...  19.5 us
    pallas_call x1, Pallas kernels, shards(): pl.pallas_call(columns_kernel, out_shape=(*shapes, half_w, half_w), grid=...  19 us
    ppermute x1, starting transfers between devices, shards(): partner_tables = lax.ppermute(tables, 'row', swap)  6.56 us
    all_to_all x1, starting transfers between devices, shards(): lax.all_to_all(pairs, 'row', 0, 0, axis_index_groups=same_core, tiled=True)  5.87 us
    unnamed x8, local copies, waits for them, and re-layouts  3.01 us
    ppermute x1, starting transfers between devices, shards(): w_im = lax.ppermute(w_im, 'row', swap)  2.41 us
    pallas_call x1, Pallas kernels, shards(): pl.pallas_call(rows_kernel, out_shape=jax.ShapeDtypeStruct((strips * 64,...  2.08 us
    ppermute x1, starting transfers between devices, shards(): other = lax.ppermute(mine, 'row', swap)  1.92 us
  transfers between devices with their start and end apart: 5, of which 1 were waited for; matrix products, arithmetic and copies ran while one was open for 0% of the time, Pallas kernels for 3%

profile of v4, /device:TPU:1, one launch (start us, length us, event | category | flops | bytes accessed | tf_op | source)
XLA Modules:
  0.0 67.0 jit_solution(9883290635936848579)
XLA Ops:
  0.0 19.0 %columns.1 = (f32[2,32,128]{2,1,0:T(8,128)}, bf16[896,128]{1,0:T(8,128)(2,1)}, bf16[8,128,256]{2,1,0:T(8,128)(2,1)}, bf16[128,1024]{1,0:T(8,128)(2,1)}, bf16[128,1024]{1,0:T(8,128)(2,1)}) custom-call(bf16[384,128]{1,0:T(8,128)(2,1)} %bitcast.7, bf16[512,128]{1,0:T(8,128)(2,1)} %bitcast.6, s32[32,128]{1,0:T(8,128)} %bitcast.8, s32[32,128]{1,0:T(8,128)} %bitcast.9, ...), custom_call_target="tpu_custom_call" | custom-call | tf_op jit(solution)/shard_map/columns/pallas_call | solution.py:179
  19.0 5.9 %all-to-all-start = ((bf16[8,128,256]{2,1,0:T(8,128)(2,1)}), bf16[8,128,256]{2,1,0:T(8,128)(2,1)S(1)}, u32[]{:S(2)}, u32[]{:S(2)}) async-start(bf16[8,128,256]{2,1,0:T(8,128)(2,1)} %get-tuple-element.14), calls=%async_computation | async-start | bytes 1048576 | tf_op jit(solution)/shard_map/all_to_all | solution.py:189
  24.9 0.0 copy-start
  24.9 6.6 %collective-permute-start = (bf16[896,128]{1,0:T(8,128)(2,1)}, bf16[896,128]{1,0:T(8,128)(2,1)S(1)}, u32[]{:S(2)}, u32[]{:S(2)}) collective-permute-start(bf16[896,128]{1,0:T(8,128)(2,1)} %get-tuple-element.15.own_ref), channel_id=1, source_target_pairs={{0,32},{32,0},{64,96},{96,64},{128,160},{160,128},{192,224},{224,1... | collective-permute-start | bytes 688136 | tf_op jit(solution)/shard_map/ppermute | solution.py:190
  31.4 1.9 %collective-permute-start.1 = (bf16[128,1024]{1,0:T(8,128)(2,1)}, bf16[128,1024]{1,0:T(8,128)(2,1)S(1)}, u32[]{:S(2)}, u32[]{:S(2)}) collective-permute-start(bf16[128,1024]{1,0:T(8,128)(2,1)} %get-tuple-element.18), channel_id=1, source_target_pairs={{0,32},{32,0},{64,96},{96,64},{128,160},{160,128},{192,224},{224,1... | collective-permute-start | bytes 786440 | tf_op jit(solution)/shard_map/ppermute | solution.py:191
  33.4 2.4 %collective-permute-start.2 = (bf16[128,1024]{1,0:T(8,128)(2,1)}, bf16[128,1024]{1,0:T(8,128)(2,1)S(1)}, u32[]{:S(2)}, u32[]{:S(2)}) collective-permute-start(bf16[128,1024]{1,0:T(8,128)(2,1)} %get-tuple-element.19), channel_id=1, source_target_pairs={{0,32},{32,0},{64,96},{96,64},{128,160},{160,128},{192,224},{224,1... | collective-permute-start | bytes 786440 | tf_op jit(solution)/shard_map/ppermute | solution.py:192
  35.8 0.0 collective-permute-done.partner_ref
  35.8 0.0 copy-start.2
  35.8 0.9 %copy-done.2 = bf16[896,128]{1,0:T(8,128)(2,1)S(1)} copy-done((bf16[896,128]{1,0:T(8,128)(2,1)S(1)}, bf16[896,128]{1,0:T(8,128)(2,1)}, u32[]{:S(2)}) %copy-start.2) | copy-done | bytes 229400
  36.7 0.0 copy-start.3
  36.7 0.8 %copy-done.3 = f32[2,32,128]{2,1,0:T(8,128)S(1)} copy-done((f32[2,32,128]{2,1,0:T(8,128)S(1)}, f32[2,32,128]{2,1,0:T(8,128)}, u32[]{:S(2)}) %copy-start.3) | copy-done | bytes 32792
  37.5 2.1 %rows.1.density_ref = bf16[2048,512]{1,0:T(8,128)(2,1)S(1)} custom-call(bf16[896,128]{1,0:T(8,128)(2,1)S(1)} %copy-done.2, bf16[896,128]{1,0:T(8,128)(2,1)S(1)} %collective-permute-done.partner_ref, f32[2,32,128]{2,1,0:T(8,128)S(1)} %copy-done.3), custom_call_target="tpu_custom_call" | custom-call | flops 1073741824 | bytes 3145728 | tf_op jit(solution)/shard_map/rows/pallas_call | solution.py:193
  39.6 0.0 copy-start.1
  39.6 1.3 %copy-done.1 = bf16[2048,512]{1,0:T(8,128)(2,1)} copy-done((bf16[2048,512]{1,0:T(8,128)(2,1)}, bf16[2048,512]{1,0:T(8,128)(2,1)S(1)}, u32[]{:S(2)}) %copy-start.1) | copy-done | bytes 2097176
  40.9 0.0 all-to-all-done.pairs_ref
  40.9 0.0 collective-permute-done.1.re_ref
  40.9 0.0 collective-permute-done.2.im_ref
  40.9 0.0 copy-done
  40.9 1.6 %screened.1 = (f32[2,128,256]{2,1,0:T(8,128)S(1)}, bf16[2048,512]{1,0:T(8,128)(2,1)S(1)}) custom-call(bf16[8,128,256]{2,1,0:T(8,128)(2,1)S(1)} %all-to-all-done.pairs_ref, bf16[2,128,2048]{2,1,0:T(8,128)(2,1)S(1)} %copy-done, bf16[128,1024]{1,0:T(8,128)(2,1)S(1)} %collective-permute-done.1.re_ref, bf16[128,1024]{1,0:T(8,128)(2,1)S(1)} %collective-permute-done.2.im_ref, ...), custom_call_target="tpu_custom_call" | custom-call | tf_op jit(solution)/shard_map/screened/pallas_call | solution.py:207
  42.6 1.9 %collective-permute-start.3 = (f32[2,128,256]{2,1,0:T(8,128)S(1)}, f32[2,128,256]{2,1,0:T(8,128)S(1)}, u32[]{:S(2)}, u32[]{:S(2)}) collective-permute-start(f32[2,128,256]{2,1,0:T(8,128)S(1)} %get-tuple-element.21.mine_ref), channel_id=1, source_target_pairs={{0,32},{32,0},{64,96},{96,64},{128,160},{160,128},{192,224},{224,1... | collective-permute-start | bytes 786440 | tf_op jit(solution)/shard_map/ppermute | solution.py:218
  44.5 1.5 %collective-permute-done.3.other_ref = f32[2,128,256]{2,1,0:T(8,128)S(1)} collective-permute-done((f32[2,128,256]{2,1,0:T(8,128)S(1)}, f32[2,128,256]{2,1,0:T(8,128)S(1)}, u32[]{:S(2)}, u32[]{:S(2)}) %collective-permute-start.3) | collective-permute-done | bytes 262176 | tf_op jit(solution)/shard_map/ppermute | solution.py:218
  46.0 0.7 %direct.1 = bf16[8,256,256]{2,1,0:T(8,128)(2,1)S(1)} custom-call(f32[2,128,256]{2,1,0:T(8,128)S(1)} %get-tuple-element.21.mine_ref, f32[2,128,256]{2,1,0:T(8,128)S(1)} %collective-permute-done.3.other_ref, bf16[2048,512]{1,0:T(8,128)(2,1)S(1)} %get-tuple-element.22.density_ref), custom_call_target="tpu_custom_call" | custom-call | tf_op jit(solution)/shard_map/direct/pallas_call | solution.py:219
  46.7 19.5 %all_to_all.10.in_ref = bf16[8,256,256]{2,1,0:T(8,128)(2,1)S(1)} all-to-all(bf16[8,256,256]{2,1,0:T(8,128)(2,1)S(1)} %direct.1), channel_id=1, replica_groups={{0,64,128,192,448,384,320,256},{32,96,160,224,480,416,352,288},{1,65,12..., dimensions={0} | all-to-all | bytes 2097152 | tf_op jit(solution)/shard_map/all_to_all | solution.py:226
  66.2 0.8 %total.1 = f32[2,256,128]{2,1,0:T(8,128)} custom-call(bf16[8,256,256]{2,1,0:T(8,128)(2,1)S(1)} %all_to_all.10.in_ref), custom_call_target="tpu_custom_call" | custom-call | tf_op jit(solution)/shard_map/total/pallas_call | solution.py:227
Async XLA Ops:
  19.0 21.9 %all-to-all-start = ((bf16[8,128,256]{2,1,0:T(8,128)(2,1)}), bf16[8,128,256]{2,1,0:T(8,128)(2,1)S(1)}, u32[]{:S(2)}, u32[]{:S(2)}) async-start(bf16[8,128,256]{2,1,0:T(8,128)(2,1)} %get-tuple-element.14), calls=%async_computation | async-start | bytes 1048576 | tf_op jit(solution)/shard_map/all_to_all | solution.py:189
  24.9 16.1 %copy-start = (bf16[2,128,2048]{2,1,0:T(8,128)(2,1)S(1)}, bf16[2,128,2048]{2,1,0:T(8,128)(2,1)}, u32[]{:S(2)}) copy-start(bf16[2,128,2048]{2,1,0:T(8,128)(2,1)} %own_ref.1) | copy-start | bytes 3145732
  24.9 10.9 %collective-permute-start = (bf16[896,128]{1,0:T(8,128)(2,1)}, bf16[896,128]{1,0:T(8,128)(2,1)S(1)}, u32[]{:S(2)}, u32[]{:S(2)}) collective-permute-start(bf16[896,128]{1,0:T(8,128)(2,1)} %get-tuple-element.15.own_ref), channel_id=1, source_target_pairs={{0,32},{32,0},{64,96},{96,64},{128,160},{160,128},{192,224},{224,1... | collective-permute-start | bytes 688136 | tf_op jit(solution)/shard_map/ppermute | solution.py:190
  31.4 9.5 %collective-permute-start.1 = (bf16[128,1024]{1,0:T(8,128)(2,1)}, bf16[128,1024]{1,0:T(8,128)(2,1)S(1)}, u32[]{:S(2)}, u32[]{:S(2)}) collective-permute-start(bf16[128,1024]{1,0:T(8,128)(2,1)} %get-tuple-element.18), channel_id=1, source_target_pairs={{0,32},{32,0},{64,96},{96,64},{128,160},{160,128},{192,224},{224,1... | collective-permute-start | bytes 786440 | tf_op jit(solution)/shard_map/ppermute | solution.py:191
  33.4 7.6 %collective-permute-start.2 = (bf16[128,1024]{1,0:T(8,128)(2,1)}, bf16[128,1024]{1,0:T(8,128)(2,1)S(1)}, u32[]{:S(2)}, u32[]{:S(2)}) collective-permute-start(bf16[128,1024]{1,0:T(8,128)(2,1)} %get-tuple-element.19), channel_id=1, source_target_pairs={{0,32},{32,0},{64,96},{96,64},{128,160},{160,128},{192,224},{224,1... | collective-permute-start | bytes 786440 | tf_op jit(solution)/shard_map/ppermute | solution.py:192
  35.8 0.9 %copy-start.2 = (bf16[896,128]{1,0:T(8,128)(2,1)S(1)}, bf16[896,128]{1,0:T(8,128)(2,1)}, u32[]{:S(2)}) copy-start(bf16[896,128]{1,0:T(8,128)(2,1)} %get-tuple-element.15.own_ref) | copy-start | bytes 688132
  36.7 0.8 %copy-start.3 = (f32[2,32,128]{2,1,0:T(8,128)S(1)}, f32[2,32,128]{2,1,0:T(8,128)}, u32[]{:S(2)}) copy-start(f32[2,32,128]{2,1,0:T(8,128)} %get-tuple-element.16.at_ref) | copy-start | bytes 98308
  39.6 1.3 %copy-start.1 = (bf16[2048,512]{1,0:T(8,128)(2,1)}, bf16[2048,512]{1,0:T(8,128)(2,1)S(1)}, u32[]{:S(2)}) copy-start(bf16[2048,512]{1,0:T(8,128)(2,1)S(1)} %rows.1.density_ref) | copy-start | bytes 6291460
  42.6 3.4 %collective-permute-start.3 = (f32[2,128,256]{2,1,0:T(8,128)S(1)}, f32[2,128,256]{2,1,0:T(8,128)S(1)}, u32[]{:S(2)}, u32[]{:S(2)}) collective-permute-start(f32[2,128,256]{2,1,0:T(8,128)S(1)} %get-tuple-element.21.mine_ref), channel_id=1, source_target_pairs={{0,32},{32,0},{64,96},{96,64},{128,160},{160,128},{192,224},{224,1... | collective-permute-start | bytes 786440 | tf_op jit(solution)/shard_map/ppermute | solution.py:218

commit v5 on v4

--- a/solution.py
+++ b/solution.py
@@ -181,7 +181,7 @@
         out_shape=(*shapes, half_w, half_w),
         grid=(1,),
         in_specs=[whole(array) for array in raw] + [anywhere],
-        out_specs=(*[whole(array) for array in shapes], anywhere, anywhere),
+        out_specs=tuple(whole(array) for array in (*shapes, half_w, half_w)),
         scratch_shapes=[pltpu.SemaphoreType.DMA((2, chips))],
         compiler_params=ALL,
         name="columns",

time: 67.6 us -> 51.9 us (0.77)
  Pallas kernels: 24.2 us -> 8.48 us
    pallas_call x1, Pallas kernels: 19 us -> 3.22 us  [shards(): pl.pallas_call(columns_kernel, out_shape=(*shapes, half_w, half_w), grid=...]
  transfers between devices with their start and end apart: 5 -> 5, of which waited for: 1 -> 1; matrix products, arithmetic and copies ran while one was open for 0% -> 0% of each run, Pallas kernels for 3% -> 4%
where the time goes in v5:
time: 51.9 us; the launch traced here: 51.3 us
  blocking collectives  19.5 us (38%)
  starting transfers between devices  18.7 us (36%)
  Pallas kernels  8.48 us (16%)
  local copies, waits for them, and re-layouts  3.01 us (6%)
  waiting for transfers between devices  1.5 us (3%)
    all_to_all x1, blocking collectives, shards(): lax.all_to_all(partial, 'row', 0, 0, axis_index_groups=same_core, tiled=T...  19.5 us
    ppermute x1, starting transfers between devices, shards(): partner_tables = lax.ppermute(tables, 'row', swap)  6.57 us
    all_to_all x1, starting transfers between devices, shards(): lax.all_to_all(pairs, 'row', 0, 0, axis_index_groups=same_core, tiled=True)  5.87 us
    pallas_call x1, Pallas kernels, shards(): pl.pallas_call(columns_kernel, out_shape=(*shapes, half_w, half_w), grid=...  3.22 us
    unnamed x8, local copies, waits for them, and re-layouts  3.01 us
    ppermute x1, starting transfers between devices, shards(): w_im = lax.ppermute(w_im, 'row', swap)  2.41 us
    pallas_call x1, Pallas kernels, shards(): pl.pallas_call(rows_kernel, out_shape=jax.ShapeDtypeStruct((strips * 64,...  2.08 us
    ppermute x1, starting transfers between devices, shards(): other = lax.ppermute(mine, 'row', swap)  1.93 us
  transfers between devices with their start and end apart: 5, of which 1 were waited for; matrix products, arithmetic and copies ran while one was open for 0% of the time, Pallas kernels for 4%

profile of v5, /device:TPU:1, one launch (start us, length us, event | category | flops | bytes accessed | tf_op | source)
XLA Modules:
  0.0 51.3 jit_solution(143146288930151024)
XLA Ops:
  0.0 3.2 %columns.1 = (f32[2,32,128]{2,1,0:T(8,128)}, bf16[896,128]{1,0:T(8,128)(2,1)}, bf16[8,128,256]{2,1,0:T(8,128)(2,1)}, bf16[128,1024]{1,0:T(8,128)(2,1)}, bf16[128,1024]{1,0:T(8,128)(2,1)}) custom-call(bf16[384,128]{1,0:T(8,128)(2,1)} %bitcast.7, bf16[512,128]{1,0:T(8,128)(2,1)} %bitcast.6, s32[32,128]{1,0:T(8,128)} %bitcast.8, s32[32,128]{1,0:T(8,128)} %bitcast.9, ...), custom_call_target="tpu_custom_call" | custom-call | tf_op jit(solution)/shard_map/columns/pallas_call | solution.py:179
  3.2 5.9 %all-to-all-start = ((bf16[8,128,256]{2,1,0:T(8,128)(2,1)}), bf16[8,128,256]{2,1,0:T(8,128)(2,1)S(1)}, u32[]{:S(2)}, u32[]{:S(2)}) async-start(bf16[8,128,256]{2,1,0:T(8,128)(2,1)} %get-tuple-element.14), calls=%async_computation | async-start | bytes 1048576 | tf_op jit(solution)/shard_map/all_to_all | solution.py:189
  9.1 0.0 copy-start
  9.1 6.6 %collective-permute-start = (bf16[896,128]{1,0:T(8,128)(2,1)}, bf16[896,128]{1,0:T(8,128)(2,1)S(1)}, u32[]{:S(2)}, u32[]{:S(2)}) collective-permute-start(bf16[896,128]{1,0:T(8,128)(2,1)} %get-tuple-element.15.own_ref), channel_id=1, source_target_pairs={{0,32},{32,0},{64,96},{96,64},{128,160},{160,128},{192,224},{224,1... | collective-permute-start | bytes 688136 | tf_op jit(solution)/shard_map/ppermute | solution.py:190
  15.7 1.9 %collective-permute-start.1 = (bf16[128,1024]{1,0:T(8,128)(2,1)}, bf16[128,1024]{1,0:T(8,128)(2,1)S(1)}, u32[]{:S(2)}, u32[]{:S(2)}) collective-permute-start(bf16[128,1024]{1,0:T(8,128)(2,1)} %get-tuple-element.18), channel_id=1, source_target_pairs={{0,32},{32,0},{64,96},{96,64},{128,160},{160,128},{192,224},{224,1... | collective-permute-start | bytes 786440 | tf_op jit(solution)/shard_map/ppermute | solution.py:191
  17.6 2.4 %collective-permute-start.2 = (bf16[128,1024]{1,0:T(8,128)(2,1)}, bf16[128,1024]{1,0:T(8,128)(2,1)S(1)}, u32[]{:S(2)}, u32[]{:S(2)}) collective-permute-start(bf16[128,1024]{1,0:T(8,128)(2,1)} %get-tuple-element.19), channel_id=1, source_target_pairs={{0,32},{32,0},{64,96},{96,64},{128,160},{160,128},{192,224},{224,1... | collective-permute-start | bytes 786440 | tf_op jit(solution)/shard_map/ppermute | solution.py:192
  20.0 0.0 collective-permute-done.partner_ref
  20.0 0.0 copy-start.2
  20.0 0.9 %copy-done.2 = bf16[896,128]{1,0:T(8,128)(2,1)S(1)} copy-done((bf16[896,128]{1,0:T(8,128)(2,1)S(1)}, bf16[896,128]{1,0:T(8,128)(2,1)}, u32[]{:S(2)}) %copy-start.2) | copy-done | bytes 229400
  21.0 0.0 copy-start.3
  21.0 0.8 %copy-done.3 = f32[2,32,128]{2,1,0:T(8,128)S(1)} copy-done((f32[2,32,128]{2,1,0:T(8,128)S(1)}, f32[2,32,128]{2,1,0:T(8,128)}, u32[]{:S(2)}) %copy-start.3) | copy-done | bytes 32792
  21.7 2.1 %rows.1.density_ref = bf16[2048,512]{1,0:T(8,128)(2,1)S(1)} custom-call(bf16[896,128]{1,0:T(8,128)(2,1)S(1)} %copy-done.2, bf16[896,128]{1,0:T(8,128)(2,1)S(1)} %collective-permute-done.partner_ref, f32[2,32,128]{2,1,0:T(8,128)S(1)} %copy-done.3), custom_call_target="tpu_custom_call" | custom-call | flops 1073741824 | bytes 3145728 | tf_op jit(solution)/shard_map/rows/pallas_call | solution.py:193
  23.8 0.0 copy-start.1
  23.8 1.3 %copy-done.1 = bf16[2048,512]{1,0:T(8,128)(2,1)} copy-done((bf16[2048,512]{1,0:T(8,128)(2,1)}, bf16[2048,512]{1,0:T(8,128)(2,1)S(1)}, u32[]{:S(2)}) %copy-start.1) | copy-done | bytes 2097176
  25.2 0.0 all-to-all-done.pairs_ref
  25.2 0.0 collective-permute-done.1.re_ref
  25.2 0.0 collective-permute-done.2.im_ref
  25.2 0.0 copy-done
  25.2 1.6 %screened.1 = (f32[2,128,256]{2,1,0:T(8,128)S(1)}, bf16[2048,512]{1,0:T(8,128)(2,1)S(1)}) custom-call(bf16[8,128,256]{2,1,0:T(8,128)(2,1)S(1)} %all-to-all-done.pairs_ref, bf16[2,128,2048]{2,1,0:T(8,128)(2,1)S(1)} %copy-done, bf16[128,1024]{1,0:T(8,128)(2,1)S(1)} %collective-permute-done.1.re_ref, bf16[128,1024]{1,0:T(8,128)(2,1)S(1)} %collective-permute-done.2.im_ref, ...), custom_call_target="tpu_custom_call" | custom-call | tf_op jit(solution)/shard_map/screened/pallas_call | solution.py:207
  26.8 1.9 %collective-permute-start.3 = (f32[2,128,256]{2,1,0:T(8,128)S(1)}, f32[2,128,256]{2,1,0:T(8,128)S(1)}, u32[]{:S(2)}, u32[]{:S(2)}) collective-permute-start(f32[2,128,256]{2,1,0:T(8,128)S(1)} %get-tuple-element.21.mine_ref), channel_id=1, source_target_pairs={{0,32},{32,0},{64,96},{96,64},{128,160},{160,128},{192,224},{224,1... | collective-permute-start | bytes 786440 | tf_op jit(solution)/shard_map/ppermute | solution.py:218
  28.8 1.5 %collective-permute-done.3.other_ref = f32[2,128,256]{2,1,0:T(8,128)S(1)} collective-permute-done((f32[2,128,256]{2,1,0:T(8,128)S(1)}, f32[2,128,256]{2,1,0:T(8,128)S(1)}, u32[]{:S(2)}, u32[]{:S(2)}) %collective-permute-start.3) | collective-permute-done | bytes 262176 | tf_op jit(solution)/shard_map/ppermute | solution.py:218
  30.2 0.7 %direct.1 = bf16[8,256,256]{2,1,0:T(8,128)(2,1)S(1)} custom-call(f32[2,128,256]{2,1,0:T(8,128)S(1)} %get-tuple-element.21.mine_ref, f32[2,128,256]{2,1,0:T(8,128)S(1)} %collective-permute-done.3.other_ref, bf16[2048,512]{1,0:T(8,128)(2,1)S(1)} %get-tuple-element.22.density_ref), custom_call_target="tpu_custom_call" | custom-call | tf_op jit(solution)/shard_map/direct/pallas_call | solution.py:219
  31.0 19.5 %all_to_all.10.in_ref = bf16[8,256,256]{2,1,0:T(8,128)(2,1)S(1)} all-to-all(bf16[8,256,256]{2,1,0:T(8,128)(2,1)S(1)} %direct.1), channel_id=1, replica_groups={{0,64,128,192,448,384,320,256},{32,96,160,224,480,416,352,288},{1,65,12..., dimensions={0} | all-to-all | bytes 2097152 | tf_op jit(solution)/shard_map/all_to_all | solution.py:226
  50.4 0.8 %total.1 = f32[2,256,128]{2,1,0:T(8,128)} custom-call(bf16[8,256,256]{2,1,0:T(8,128)(2,1)S(1)} %all_to_all.10.in_ref), custom_call_target="tpu_custom_call" | custom-call | tf_op jit(solution)/shard_map/total/pallas_call | solution.py:227
Async XLA Ops:
  3.2 21.9 %all-to-all-start = ((bf16[8,128,256]{2,1,0:T(8,128)(2,1)}), bf16[8,128,256]{2,1,0:T(8,128)(2,1)S(1)}, u32[]{:S(2)}, u32[]{:S(2)}) async-start(bf16[8,128,256]{2,1,0:T(8,128)(2,1)} %get-tuple-element.14), calls=%async_computation | async-start | bytes 1048576 | tf_op jit(solution)/shard_map/all_to_all | solution.py:189
  9.1 16.1 %copy-start = (bf16[2,128,2048]{2,1,0:T(8,128)(2,1)S(1)}, bf16[2,128,2048]{2,1,0:T(8,128)(2,1)}, u32[]{:S(2)}) copy-start(bf16[2,128,2048]{2,1,0:T(8,128)(2,1)} %own_ref.1) | copy-start | bytes 3145732
  9.1 10.9 %collective-permute-start = (bf16[896,128]{1,0:T(8,128)(2,1)}, bf16[896,128]{1,0:T(8,128)(2,1)S(1)}, u32[]{:S(2)}, u32[]{:S(2)}) collective-permute-start(bf16[896,128]{1,0:T(8,128)(2,1)} %get-tuple-element.15.own_ref), channel_id=1, source_target_pairs={{0,32},{32,0},{64,96},{96,64},{128,160},{160,128},{192,224},{224,1... | collective-permute-start | bytes 688136 | tf_op jit(solution)/shard_map/ppermute | solution.py:190
  15.7 9.5 %collective-permute-start.1 = (bf16[128,1024]{1,0:T(8,128)(2,1)}, bf16[128,1024]{1,0:T(8,128)(2,1)S(1)}, u32[]{:S(2)}, u32[]{:S(2)}) collective-permute-start(bf16[128,1024]{1,0:T(8,128)(2,1)} %get-tuple-element.18), channel_id=1, source_target_pairs={{0,32},{32,0},{64,96},{96,64},{128,160},{160,128},{192,224},{224,1... | collective-permute-start | bytes 786440 | tf_op jit(solution)/shard_map/ppermute | solution.py:191
  17.6 7.6 %collective-permute-start.2 = (bf16[128,1024]{1,0:T(8,128)(2,1)}, bf16[128,1024]{1,0:T(8,128)(2,1)S(1)}, u32[]{:S(2)}, u32[]{:S(2)}) collective-permute-start(bf16[128,1024]{1,0:T(8,128)(2,1)} %get-tuple-element.19), channel_id=1, source_target_pairs={{0,32},{32,0},{64,96},{96,64},{128,160},{160,128},{192,224},{224,1... | collective-permute-start | bytes 786440 | tf_op jit(solution)/shard_map/ppermute | solution.py:192
  20.0 0.9 %copy-start.2 = (bf16[896,128]{1,0:T(8,128)(2,1)S(1)}, bf16[896,128]{1,0:T(8,128)(2,1)}, u32[]{:S(2)}) copy-start(bf16[896,128]{1,0:T(8,128)(2,1)} %get-tuple-element.15.own_ref) | copy-start | bytes 688132
  21.0 0.8 %copy-start.3 = (f32[2,32,128]{2,1,0:T(8,128)S(1)}, f32[2,32,128]{2,1,0:T(8,128)}, u32[]{:S(2)}) copy-start(f32[2,32,128]{2,1,0:T(8,128)} %get-tuple-element.16.at_ref) | copy-start | bytes 98308
  23.8 1.3 %copy-start.1 = (bf16[2048,512]{1,0:T(8,128)(2,1)}, bf16[2048,512]{1,0:T(8,128)(2,1)S(1)}, u32[]{:S(2)}) copy-start(bf16[2048,512]{1,0:T(8,128)(2,1)S(1)} %rows.1.density_ref) | copy-start | bytes 6291460
  26.8 3.4 %collective-permute-start.3 = (f32[2,128,256]{2,1,0:T(8,128)S(1)}, f32[2,128,256]{2,1,0:T(8,128)S(1)}, u32[]{:S(2)}, u32[]{:S(2)}) collective-permute-start(f32[2,128,256]{2,1,0:T(8,128)S(1)} %get-tuple-element.21.mine_ref), channel_id=1, source_target_pairs={{0,32},{32,0},{64,96},{96,64},{128,160},{160,128},{192,224},{224,1... | collective-permute-start | bytes 786440 | tf_op jit(solution)/shard_map/ppermute | solution.py:218

commit v6 on v5

--- a/solution.py
+++ b/solution.py
@@ -15,7 +15,7 @@
 STRIPS = 16
 MIB = 1024 * 1024
 LITTLE = pltpu.CompilerParams(vmem_limit_bytes=16 * MIB)
-MUCH = pltpu.CompilerParams(vmem_limit_bytes=48 * MIB)
+MUCH = pltpu.CompilerParams(vmem_limit_bytes=52 * MIB)
 ALL = pltpu.CompilerParams(vmem_limit_bytes=63 * MIB)
 
 
@@ -48,7 +48,7 @@
 
 
 def columns_kernel(
-    valence_ref, conduction_ref, v_ref, n_ref, k_ref, w_ref, at_ref, table_ref, out_ref, re_ref, im_ref, sems
+    valence_ref, conduction_ref, v_ref, n_ref, k_ref, w_ref, table_ref, out_ref, re_ref, im_ref, sems
 ):
     core = core_of()
     copies = []
@@ -59,14 +59,18 @@
             copies.append(pltpu.make_async_copy(w_ref.at[part, :, lanes], to, sems.at[part, place]))
     for copy in copies:
         copy.start()
-    split = valence_ref.shape[0]
-    table_ref[0:split, :] = valence_ref[...]
-    table_ref[split:, :] = conduction_ref[...]
-    at_ref[0] = (k_ref[...] * VAL + v_ref[...]).astype(jnp.float32)
-    at_ref[1] = (k_ref[...] * CON + n_ref[...]).astype(jnp.float32)
+    bands = valence_ref.shape[0] + conduction_ref.shape[0]
+    strips = v_ref.shape[0]
+    table_ref[0 : valence_ref.shape[0], :] = valence_ref[...]
+    table_ref[valence_ref.shape[0] : bands, :] = conduction_ref[...]
     picked = []
-    for which, ref in enumerate((valence_ref, conduction_ref)):
-        index = lane_matrix(at_ref[which, pl.ds(lax.axis_index("col"), 1), :])
+    for which, (index_ref, count, ref) in enumerate(((v_ref, VAL, valence_ref), (n_ref, CON, conduction_ref))):
+        place = bands + which * strips
+        table_ref[place : place + strips, :] = (
+            (k_ref[...] * count + index_ref[...]).astype(jnp.float32).astype(jnp.bfloat16)
+        )
+        own = pl.ds(lax.axis_index("col"), 1)
+        index = lane_matrix((k_ref[own, :] * count + index_ref[own, :]).astype(jnp.float32))
         parts = []
         for parity in range(2):
             hot = one_hot(2.0 * index + parity, ref.shape[0])
@@ -80,17 +84,21 @@
         copy.wait()
 
 
-def rows_kernel(own_ref, partner_ref, at_ref, density_ref, table):
+def rows_kernel(own_ref, partner_ref, density_ref, table, at_ref):
     core = core_of()
 
     @pl.when(pl.program_id(0) == 0)
     def _():
+        strips = at_ref.shape[1]
+        split = 2 * VAL * 4
+        bands = own_ref.shape[0] - 2 * strips
+        at_ref[0] = own_ref[bands : bands + strips, :].astype(jnp.float32)
+        at_ref[1] = own_ref[bands + strips :, :].astype(jnp.float32)
         both = jnp.concatenate([own_ref[...], partner_ref[...]], 1)
-        split = 2 * VAL * 4
         for parity in range(2):
             lanes = pl.ds(parity * 2 * SLICE, 2 * SLICE)
             table[0:KPAD, lanes] = pick(KPAD, parity, both[:split])
-            table[KPAD:, lanes] = pick(KPAD, parity, both[split:])
+            table[KPAD:, lanes] = pick(KPAD, parity, both[split:bands])
 
     picked = []
     for which in range(2):
@@ -105,24 +113,26 @@
     density_ref[...] = jnp.concatenate(densities(*picked), 1).astype(jnp.bfloat16)
 
 
-def screened_kernel(pairs_ref, own_ref, re_ref, im_ref, density_ref, out_ref, near_ref, sem):
+def screened_kernel(pairs_ref, own_ref, re_ref, im_ref, out_ref, held, sems):
     core = core_of()
-    copy = pltpu.make_async_copy(density_ref, near_ref, sem)
-    copy.start()
-    for half in range(2):
+    copies = []
+    for place, chip in enumerate(RING):
+        lanes = pl.ds(pl.multiple_of((2 * chip + core) * SLICE, SLICE), SLICE)
+        to = held.at[:, :, place * SLICE : (place + 1) * SLICE]
+        copies.append(pltpu.make_async_copy(own_ref.at[:, :, lanes], to, sems.at[place]))
+    for copy in copies:
+        copy.start()
+    pairs = pairs_ref[...].reshape(-1, 2 * WIDTH)
+    for half in (1, 0):
+        if half == 0:
+            for copy in copies:
+                copy.wait()
         parts = []
         for part in range(2):
-            total = jnp.zeros((SLICE, 2 * WIDTH), jnp.float32)
-            for place, chip in enumerate(RING):
-                if half == 0:
-                    w = own_ref[part, :, pl.ds(pl.multiple_of((2 * chip + core) * SLICE, SLICE), SLICE)]
-                else:
-                    w = (re_ref, im_ref)[part][:, place * SLICE : (place + 1) * SLICE]
-                total += jnp.dot(w, pairs_ref[place], preferred_element_type=jnp.float32)
-            parts.append(total)
+            w = (re_ref, im_ref)[part][...] if half else held[part]
+            parts.append(jnp.dot(w, pairs, preferred_element_type=jnp.float32))
         out_ref[half, :, :WIDTH] = parts[0][:, :WIDTH] - parts[1][:, WIDTH:]
         out_ref[half, :, WIDTH:] = parts[0][:, WIDTH:] + parts[1][:, :WIDTH]
-    copy.wait()
 
 
 def direct_kernel(mine_ref, other_ref, density_ref, out_ref, screened):
@@ -171,12 +181,11 @@
     conduction = conduction_orbitals.reshape(-1, SLICE)
     raw = (valence, conduction, *index)
     shapes = (
-        jax.ShapeDtypeStruct((2, strips, 128), f32),
-        jax.ShapeDtypeStruct((valence.shape[0] + conduction.shape[0], SLICE), bf16),
+        jax.ShapeDtypeStruct((valence.shape[0] + conduction.shape[0] + 2 * strips, SLICE), bf16),
         jax.ShapeDtypeStruct((chips, SLICE, 2 * WIDTH), bf16),
     )
     half_w = jax.ShapeDtypeStruct((SLICE, chips * SLICE), bf16)
-    at, tables, pairs, w_re, w_im = pl.pallas_call(
+    tables, pairs, w_re, w_im = pl.pallas_call(
         columns_kernel,
         out_shape=(*shapes, half_w, half_w),
         grid=(1,),
@@ -194,27 +203,24 @@
         rows_kernel,
         out_shape=jax.ShapeDtypeStruct((strips * 64, 4 * SLICE), bf16),
         grid=(strips // STRIPS,),
-        in_specs=[whole(tables), whole(partner_tables), whole(at)],
+        in_specs=[whole(tables), whole(partner_tables)],
         out_specs=pl.BlockSpec((STRIPS * 64, 4 * SLICE), lambda m: (m, 0)),
-        scratch_shapes=[pltpu.VMEM((2 * KPAD, 4 * SLICE), bf16)],
+        scratch_shapes=[pltpu.VMEM((2 * KPAD, 4 * SLICE), bf16), pltpu.VMEM((2, strips, 128), f32)],
         compiler_params=LITTLE,
         cost_estimate=pl.CostEstimate(
             flops=4 * strips * 64 * KPAD * 4 * SLICE, bytes_accessed=3 << 20, transcendentals=0
         ),
         name="rows",
-    )(tables, partner_tables, at)
+    )(tables, partner_tables)
     pairs, density = lax.optimization_barrier((pairs, density))
-    mine, density = pl.pallas_call(
+    mine = pl.pallas_call(
         screened_kernel,
-        out_shape=(
-            jax.ShapeDtypeStruct((2, SLICE, 2 * WIDTH), f32),
-            jax.ShapeDtypeStruct(density.shape, bf16),
-        ),
-        in_specs=[in_vmem] * 4 + [anywhere],
-        scratch_shapes=[pltpu.SemaphoreType.DMA],
+        out_shape=jax.ShapeDtypeStruct((2, SLICE, 2 * WIDTH), f32),
+        in_specs=[in_vmem, anywhere, in_vmem, in_vmem],
+        scratch_shapes=[pltpu.VMEM((2, SLICE, chips * SLICE), bf16), pltpu.SemaphoreType.DMA((chips,))],
         compiler_params=MUCH,
         name="screened",
-    )(pairs, screened, w_re, w_im, density)
+    )(pairs, screened, w_re, w_im)
     other = lax.ppermute(mine, "row", swap)
     partial = pl.pallas_call(
         direct_kernel,

time: 51.9 us -> 49.6 us (0.956)
  local copies, waits for them, and re-layouts: 3.01 us -> 0.94 us
    unnamed x8 -> x2, local copies, waits for them, and re-layouts: 3.01 us -> 0.94 us
where the time goes in v6:
time: 49.6 us; the launch traced here: 49 us
  blocking collectives  19.4 us (39%)
  starting transfers between devices  18.6 us (38%)
  Pallas kernels  8.49 us (17%)
  waiting for transfers between devices  1.5 us (3%)
  local copies, waits for them, and re-layouts  0.94 us (2%)
    all_to_all x1, blocking collectives, shards(): lax.all_to_all(partial, 'row', 0, 0, axis_index_groups=same_core, tiled=T...  19.4 us
    ppermute x1, starting transfers between devices, shards(): partner_tables = lax.ppermute(tables, 'row', swap)  6.42 us
    all_to_all x1, starting transfers between devices, shards(): lax.all_to_all(pairs, 'row', 0, 0, axis_index_groups=same_core, tiled=True)  5.87 us
    pallas_call x1, Pallas kernels, shards(): pl.pallas_call(columns_kernel, out_shape=(*shapes, half_w, half_w), grid=...  3.2 us
    ppermute x1, starting transfers between devices, shards(): w_im = lax.ppermute(w_im, 'row', swap)  2.41 us
    pallas_call x1, Pallas kernels, shards(): pl.pallas_call(rows_kernel, out_shape=jax.ShapeDtypeStruct((strips * 64,...  2.08 us
    ppermute x1, starting transfers between devices, shards(): other = lax.ppermute(mine, 'row', swap)  1.93 us
    ppermute x1, starting transfers between devices, shards(): w_re = lax.ppermute(w_re, 'row', swap)  1.92 us
  transfers between devices with their start and end apart: 5, of which 1 were waited for; matrix products, arithmetic and copies ran while one was open for 0% of the time, Pallas kernels for 4%

profile of v6, /device:TPU:1, one launch (start us, length us, event | category | flops | bytes accessed | tf_op | source)
XLA Modules:
  0.0 49.0 jit_solution(7857268185911141877)
XLA Ops:
  0.0 3.2 %columns.1 = (bf16[960,128]{1,0:T(8,128)(2,1)}, bf16[8,128,256]{2,1,0:T(8,128)(2,1)}, bf16[128,1024]{1,0:T(8,128)(2,1)}, bf16[128,1024]{1,0:T(8,128)(2,1)}) custom-call(bf16[384,128]{1,0:T(8,128)(2,1)} %bitcast.7, bf16[512,128]{1,0:T(8,128)(2,1)} %bitcast.6, s32[32,128]{1,0:T(8,128)} %bitcast.8, s32[32,128]{1,0:T(8,128)} %bitcast.9, s32[32,128]{1,0:T(8,128)} %bitcast.10, ...), custom_call_target="tpu_custom_call" | custom-call | tf_op jit(solution)/shard_map/columns/pallas_call | solution.py:188
  3.2 5.9 %all-to-all-start = ((bf16[8,128,256]{2,1,0:T(8,128)(2,1)}), bf16[8,128,256]{2,1,0:T(8,128)(2,1)S(1)}, u32[]{:S(2)}, u32[]{:S(2)}) async-start(bf16[8,128,256]{2,1,0:T(8,128)(2,1)} %get-tuple-element.11), calls=%async_computation | async-start | bytes 1048576 | tf_op jit(solution)/shard_map/all_to_all | solution.py:198
  9.1 6.4 %collective-permute-start = (bf16[960,128]{1,0:T(8,128)(2,1)}, bf16[960,128]{1,0:T(8,128)(2,1)S(1)}, u32[]{:S(2)}, u32[]{:S(2)}) collective-permute-start(bf16[960,128]{1,0:T(8,128)(2,1)} %get-tuple-element.12.own_ref), channel_id=1, source_target_pairs={{0,32},{32,0},{64,96},{96,64},{128,160},{160,128},{192,224},{224,1... | collective-permute-start | bytes 737288 | tf_op jit(solution)/shard_map/ppermute | solution.py:199
  15.5 1.9 %collective-permute-start.1 = (bf16[128,1024]{1,0:T(8,128)(2,1)}, bf16[128,1024]{1,0:T(8,128)(2,1)S(1)}, u32[]{:S(2)}, u32[]{:S(2)}) collective-permute-start(bf16[128,1024]{1,0:T(8,128)(2,1)} %get-tuple-element.14), channel_id=1, source_target_pairs={{0,32},{32,0},{64,96},{96,64},{128,160},{160,128},{192,224},{224,1... | collective-permute-start | bytes 786440 | tf_op jit(solution)/shard_map/ppermute | solution.py:200
  17.4 2.4 %collective-permute-start.2 = (bf16[128,1024]{1,0:T(8,128)(2,1)}, bf16[128,1024]{1,0:T(8,128)(2,1)S(1)}, u32[]{:S(2)}, u32[]{:S(2)}) collective-permute-start(bf16[128,1024]{1,0:T(8,128)(2,1)} %get-tuple-element.15), channel_id=1, source_target_pairs={{0,32},{32,0},{64,96},{96,64},{128,160},{160,128},{192,224},{224,1... | collective-permute-start | bytes 786440 | tf_op jit(solution)/shard_map/ppermute | solution.py:201
  19.9 0.0 collective-permute-done.partner_ref
  19.9 0.0 copy-start
  19.9 0.9 %copy-done = bf16[960,128]{1,0:T(8,128)(2,1)S(1)} copy-done((bf16[960,128]{1,0:T(8,128)(2,1)S(1)}, bf16[960,128]{1,0:T(8,128)(2,1)}, u32[]{:S(2)}) %copy-start) | copy-done | bytes 245784
  20.8 2.1 %rows.1.density_ref = bf16[2048,512]{1,0:T(8,128)(2,1)S(1)} custom-call(bf16[960,128]{1,0:T(8,128)(2,1)S(1)} %copy-done, bf16[960,128]{1,0:T(8,128)(2,1)S(1)} %collective-permute-done.partner_ref), custom_call_target="tpu_custom_call" | custom-call | flops 1073741824 | bytes 3145728 | tf_op jit(solution)/shard_map/rows/pallas_call | solution.py:202
  22.9 0.0 all-to-all-done.pairs_ref
  22.9 0.0 collective-permute-done.1.re_ref
  22.9 0.0 collective-permute-done.2.im_ref
  22.9 1.6 %screened.1.mine_ref = f32[2,128,256]{2,1,0:T(8,128)S(1)} custom-call(bf16[8,128,256]{2,1,0:T(8,128)(2,1)S(1)} %all-to-all-done.pairs_ref, bf16[2,128,2048]{2,1,0:T(8,128)(2,1)} %own_ref.1, bf16[128,1024]{1,0:T(8,128)(2,1)S(1)} %collective-permute-done.1.re_ref, bf16[128,1024]{1,0:T(8,128)(2,1)S(1)} %collective-permute-done.2.im_ref), custom_call_target="tpu_custom_call" | custom-call | tf_op jit(solution)/shard_map/screened/pallas_call | solution.py:216
  24.6 1.9 %collective-permute-start.3 = (f32[2,128,256]{2,1,0:T(8,128)S(1)}, f32[2,128,256]{2,1,0:T(8,128)S(1)}, u32[]{:S(2)}, u32[]{:S(2)}) collective-permute-start(f32[2,128,256]{2,1,0:T(8,128)S(1)} %screened.1.mine_ref), channel_id=1, source_target_pairs={{0,32},{32,0},{64,96},{96,64},{128,160},{160,128},{192,224},{224,1... | collective-permute-start | bytes 786440 | tf_op jit(solution)/shard_map/ppermute | solution.py:224
  26.5 1.5 %collective-permute-done.3.other_ref = f32[2,128,256]{2,1,0:T(8,128)S(1)} collective-permute-done((f32[2,128,256]{2,1,0:T(8,128)S(1)}, f32[2,128,256]{2,1,0:T(8,128)S(1)}, u32[]{:S(2)}, u32[]{:S(2)}) %collective-permute-start.3) | collective-permute-done | bytes 262176 | tf_op jit(solution)/shard_map/ppermute | solution.py:224
  28.0 0.7 %direct.1 = bf16[8,256,256]{2,1,0:T(8,128)(2,1)S(1)} custom-call(f32[2,128,256]{2,1,0:T(8,128)S(1)} %screened.1.mine_ref, f32[2,128,256]{2,1,0:T(8,128)S(1)} %collective-permute-done.3.other_ref, bf16[2048,512]{1,0:T(8,128)(2,1)S(1)} %rows.1.density_ref), custom_call_target="tpu_custom_call" | custom-call | tf_op jit(solution)/shard_map/direct/pallas_call | solution.py:225
  28.7 19.4 %all_to_all.10.in_ref = bf16[8,256,256]{2,1,0:T(8,128)(2,1)S(1)} all-to-all(bf16[8,256,256]{2,1,0:T(8,128)(2,1)S(1)} %direct.1), channel_id=1, replica_groups={{0,64,128,192,448,384,320,256},{32,96,160,224,480,416,352,288},{1,65,12..., dimensions={0} | all-to-all | bytes 2097152 | tf_op jit(solution)/shard_map/all_to_all | solution.py:232
  48.2 0.8 %total.1 = f32[2,256,128]{2,1,0:T(8,128)} custom-call(bf16[8,256,256]{2,1,0:T(8,128)(2,1)S(1)} %all_to_all.10.in_ref), custom_call_target="tpu_custom_call" | custom-call | tf_op jit(solution)/shard_map/total/pallas_call | solution.py:233
Async XLA Ops:
  3.2 19.7 %all-to-all-start = ((bf16[8,128,256]{2,1,0:T(8,128)(2,1)}), bf16[8,128,256]{2,1,0:T(8,128)(2,1)S(1)}, u32[]{:S(2)}, u32[]{:S(2)}) async-start(bf16[8,128,256]{2,1,0:T(8,128)(2,1)} %get-tuple-element.11), calls=%async_computation | async-start | bytes 1048576 | tf_op jit(solution)/shard_map/all_to_all | solution.py:198
  9.1 10.8 %collective-permute-start = (bf16[960,128]{1,0:T(8,128)(2,1)}, bf16[960,128]{1,0:T(8,128)(2,1)S(1)}, u32[]{:S(2)}, u32[]{:S(2)}) collective-permute-start(bf16[960,128]{1,0:T(8,128)(2,1)} %get-tuple-element.12.own_ref), channel_id=1, source_target_pairs={{0,32},{32,0},{64,96},{96,64},{128,160},{160,128},{192,224},{224,1... | collective-permute-start | bytes 737288 | tf_op jit(solution)/shard_map/ppermute | solution.py:199
  15.5 7.4 %collective-permute-start.1 = (bf16[128,1024]{1,0:T(8,128)(2,1)}, bf16[128,1024]{1,0:T(8,128)(2,1)S(1)}, u32[]{:S(2)}, u32[]{:S(2)}) collective-permute-start(bf16[128,1024]{1,0:T(8,128)(2,1)} %get-tuple-element.14), channel_id=1, source_target_pairs={{0,32},{32,0},{64,96},{96,64},{128,160},{160,128},{192,224},{224,1... | collective-permute-start | bytes 786440 | tf_op jit(solution)/shard_map/ppermute | solution.py:200
  17.4 5.5 %collective-permute-start.2 = (bf16[128,1024]{1,0:T(8,128)(2,1)}, bf16[128,1024]{1,0:T(8,128)(2,1)S(1)}, u32[]{:S(2)}, u32[]{:S(2)}) collective-permute-start(bf16[128,1024]{1,0:T(8,128)(2,1)} %get-tuple-element.15), channel_id=1, source_target_pairs={{0,32},{32,0},{64,96},{96,64},{128,160},{160,128},{192,224},{224,1... | collective-permute-start | bytes 786440 | tf_op jit(solution)/shard_map/ppermute | solution.py:201
  19.9 0.9 %copy-start = (bf16[960,128]{1,0:T(8,128)(2,1)S(1)}, bf16[960,128]{1,0:T(8,128)(2,1)}, u32[]{:S(2)}) copy-start(bf16[960,128]{1,0:T(8,128)(2,1)} %get-tuple-element.12.own_ref) | copy-start | bytes 737284
  24.6 3.4 %collective-permute-start.3 = (f32[2,128,256]{2,1,0:T(8,128)S(1)}, f32[2,128,256]{2,1,0:T(8,128)S(1)}, u32[]{:S(2)}, u32[]{:S(2)}) collective-permute-start(f32[2,128,256]{2,1,0:T(8,128)S(1)} %screened.1.mine_ref), channel_id=1, source_target_pairs={{0,32},{32,0},{64,96},{96,64},{128,160},{160,128},{192,224},{224,1... | collective-permute-start | bytes 786440 | tf_op jit(solution)/shard_map/ppermute | solution.py:224

commit v7 on v6

--- a/solution.py
+++ b/solution.py
@@ -13,6 +13,7 @@
 KPAD = 256
 RING = (0, 1, 2, 3, 7, 6, 5, 4)
 STRIPS = 16
+JOINED = 2
 MIB = 1024 * 1024
 LITTLE = pltpu.CompilerParams(vmem_limit_bytes=16 * MIB)
 MUCH = pltpu.CompilerParams(vmem_limit_bytes=52 * MIB)
@@ -48,39 +49,60 @@
 
 
 def columns_kernel(
-    valence_ref, conduction_ref, v_ref, n_ref, k_ref, w_ref, table_ref, out_ref, re_ref, im_ref, sems
+    valence_ref, conduction_ref, v_ref, n_ref, k_ref, w_ref,
+    table_ref, out_ref, block_ref,
+    bands, index, sums, pairs, blocks, in_sems, w_sems, out_sems, pair_sems,
 ):
     core = core_of()
-    copies = []
-    for part, ref in enumerate((re_ref, im_ref)):
+    split = valence_ref.shape[0]
+    count, strips = bands.shape[0], index.shape[1]
+    places = [bands.at[pl.ds(0, split), :], bands.at[pl.ds(split, count - split), :], *[index.at[i] for i in range(3)]]
+    loads = []
+    for i, (ref, place) in enumerate(zip((valence_ref, conduction_ref, v_ref, n_ref, k_ref), places)):
+        loads.append(pltpu.make_async_copy(ref, place, in_sems.at[i]))
+    for copy in loads:
+        copy.start()
+    gathers = []
+    for part in range(2):
         for place, chip in enumerate(RING):
             lanes = pl.ds(pl.multiple_of((2 * chip + 1 - core) * SLICE, SLICE), SLICE)
-            to = ref.at[:, place * SLICE : (place + 1) * SLICE]
-            copies.append(pltpu.make_async_copy(w_ref.at[part, :, lanes], to, sems.at[part, place]))
-    for copy in copies:
+            to = blocks.at[pl.ds((part * len(RING) + place) * SLICE, SLICE), :]
+            gathers.append(pltpu.make_async_copy(w_ref.at[part, :, lanes], to, w_sems.at[part, place]))
+    for copy in gathers:
         copy.start()
-    bands = valence_ref.shape[0] + conduction_ref.shape[0]
-    strips = v_ref.shape[0]
-    table_ref[0 : valence_ref.shape[0], :] = valence_ref[...]
-    table_ref[valence_ref.shape[0] : bands, :] = conduction_ref[...]
+    for copy in loads:
+        copy.wait()
+    stores = [pltpu.make_async_copy(bands, table_ref.at[pl.ds(0, count), :], out_sems.at[0])]
+    stores[0].start()
+    own = pl.ds(lax.axis_index("col"), 1)
     picked = []
-    for which, (index_ref, count, ref) in enumerate(((v_ref, VAL, valence_ref), (n_ref, CON, conduction_ref))):
-        place = bands + which * strips
-        table_ref[place : place + strips, :] = (
-            (k_ref[...] * count + index_ref[...]).astype(jnp.float32).astype(jnp.bfloat16)
+    for which, (width, start, stop) in enumerate(((VAL, 0, split), (CON, split, count))):
+        sums[which * strips : (which + 1) * strips, :] = (
+            (index[2] * width + index[which]).astype(jnp.float32).astype(jnp.bfloat16)
         )
-        own = pl.ds(lax.axis_index("col"), 1)
-        index = lane_matrix((k_ref[own, :] * count + index_ref[own, :]).astype(jnp.float32))
+        here = lane_matrix((index[2, own, :] * width + index[which, own, :]).astype(jnp.float32))
         parts = []
         for parity in range(2):
-            hot = one_hot(2.0 * index + parity, ref.shape[0])
-            parts.append(jnp.dot(hot, ref[...], preferred_element_type=jnp.float32))
+            hot = one_hot(2.0 * here + parity, stop - start)
+            parts.append(jnp.dot(hot, bands[start:stop, :], preferred_element_type=jnp.float32))
         picked.append(jnp.concatenate(parts, 1))
+    stores.append(pltpu.make_async_copy(sums, table_ref.at[pl.ds(count, 2 * strips), :], out_sems.at[1]))
+    stores[-1].start()
     real, imag = densities(*picked)
-    both = jnp.concatenate([real.T, imag.T], 1).astype(jnp.bfloat16)
+    pairs[...] = jnp.concatenate([real.T, imag.T], 1).astype(jnp.bfloat16)
     for place in range(out_ref.shape[0]):
-        out_ref[place] = both
-    for copy in copies:
+        stores.append(pltpu.make_async_copy(pairs, out_ref.at[place], pair_sems.at[place]))
+        stores[-1].start()
+    for copy in gathers:
+        copy.wait()
+    joined = JOINED * SLICE
+    rest = blocks.shape[0] - joined
+    to = table_ref.at[pl.ds(count + 2 * strips, joined), :]
+    stores.append(pltpu.make_async_copy(blocks.at[pl.ds(0, joined), :], to, out_sems.at[2]))
+    stores[-1].start()
+    stores.append(pltpu.make_async_copy(blocks.at[pl.ds(joined, rest), :], block_ref, out_sems.at[3]))
+    stores[-1].start()
+    for copy in stores:
         copy.wait()
 
 
@@ -91,10 +113,10 @@
     def _():
         strips = at_ref.shape[1]
         split = 2 * VAL * 4
-        bands = own_ref.shape[0] - 2 * strips
+        bands = 2 * (VAL + CON) * 4
         at_ref[0] = own_ref[bands : bands + strips, :].astype(jnp.float32)
-        at_ref[1] = own_ref[bands + strips :, :].astype(jnp.float32)
-        both = jnp.concatenate([own_ref[...], partner_ref[...]], 1)
+        at_ref[1] = own_ref[bands + strips : bands + 2 * strips, :].astype(jnp.float32)
+        both = jnp.concatenate([own_ref[0:bands, :], partner_ref[0:bands, :]], 1)
         for parity in range(2):
             lanes = pl.ds(parity * 2 * SLICE, 2 * SLICE)
             table[0:KPAD, lanes] = pick(KPAD, parity, both[:split])
@@ -113,7 +135,7 @@
     density_ref[...] = jnp.concatenate(densities(*picked), 1).astype(jnp.bfloat16)
 
 
-def screened_kernel(pairs_ref, own_ref, re_ref, im_ref, out_ref, held, sems):
+def screened_kernel(pairs_ref, own_ref, joined_ref, block_ref, out_ref, held, sems):
     core = core_of()
     copies = []
     for place, chip in enumerate(RING):
@@ -123,13 +145,17 @@
     for copy in copies:
         copy.start()
     pairs = pairs_ref[...].reshape(-1, 2 * WIDTH)
+    chips = len(RING)
+    start = joined_ref.shape[0] - JOINED * SLICE
+    blocks = [joined_ref[start + i * SLICE : start + (i + 1) * SLICE, :] for i in range(JOINED)]
+    blocks += [block_ref[i * SLICE : (i + 1) * SLICE, :] for i in range(2 * chips - JOINED)]
     for half in (1, 0):
         if half == 0:
             for copy in copies:
                 copy.wait()
         parts = []
         for part in range(2):
-            w = (re_ref, im_ref)[part][...] if half else held[part]
+            w = jnp.concatenate(blocks[part * chips : (part + 1) * chips], 1) if half else held[part]
             parts.append(jnp.dot(w, pairs, preferred_element_type=jnp.float32))
         out_ref[half, :, :WIDTH] = parts[0][:, :WIDTH] - parts[1][:, WIDTH:]
         out_ref[half, :, WIDTH:] = parts[0][:, WIDTH:] + parts[1][:, :WIDTH]
@@ -180,25 +206,34 @@
     valence = valence_orbitals.reshape(-1, SLICE)
     conduction = conduction_orbitals.reshape(-1, SLICE)
     raw = (valence, conduction, *index)
-    shapes = (
-        jax.ShapeDtypeStruct((valence.shape[0] + conduction.shape[0] + 2 * strips, SLICE), bf16),
-        jax.ShapeDtypeStruct((chips, SLICE, 2 * WIDTH), bf16),
-    )
-    half_w = jax.ShapeDtypeStruct((SLICE, chips * SLICE), bf16)
-    tables, pairs, w_re, w_im = pl.pallas_call(
+    bands = valence.shape[0] + conduction.shape[0]
+    dma = pltpu.SemaphoreType.DMA
+    tables, pairs, blocks = pl.pallas_call(
         columns_kernel,
-        out_shape=(*shapes, half_w, half_w),
-        grid=(1,),
-        in_specs=[whole(array) for array in raw] + [anywhere],
-        out_specs=tuple(whole(array) for array in (*shapes, half_w, half_w)),
-        scratch_shapes=[pltpu.SemaphoreType.DMA((2, chips))],
+        out_shape=(
+            jax.ShapeDtypeStruct((bands + 2 * strips + JOINED * SLICE, SLICE), bf16),
+            jax.ShapeDtypeStruct((chips, SLICE, 2 * WIDTH), bf16),
+            jax.ShapeDtypeStruct(((2 * chips - JOINED) * SLICE, SLICE), bf16),
+        ),
+        in_specs=[anywhere] * 6,
+        out_specs=(anywhere,) * 3,
+        scratch_shapes=[
+            pltpu.VMEM((bands, SLICE), bf16),
+            pltpu.VMEM((3, strips, 128), jnp.int32),
+            pltpu.VMEM((2 * strips, 128), bf16),
+            pltpu.VMEM((SLICE, 2 * WIDTH), bf16),
+            pltpu.VMEM((2 * chips * SLICE, SLICE), bf16),
+            dma((5,)),
+            dma((2, chips)),
+            dma((4,)),
+            dma((chips,)),
+        ],
         compiler_params=ALL,
         name="columns",
     )(*raw, screened)
     pairs = lax.all_to_all(pairs, "row", 0, 0, axis_index_groups=same_core, tiled=True)
     partner_tables = lax.ppermute(tables, "row", swap)
-    w_re = lax.ppermute(w_re, "row", swap)
-    w_im = lax.ppermute(w_im, "row", swap)
+    blocks = lax.ppermute(blocks, "row", swap)
     density = pl.pallas_call(
         rows_kernel,
         out_shape=jax.ShapeDtypeStruct((strips * 64, 4 * SLICE), bf16),
@@ -208,7 +243,7 @@
         scratch_shapes=[pltpu.VMEM((2 * KPAD, 4 * SLICE), bf16), pltpu.VMEM((2, strips, 128), f32)],
         compiler_params=LITTLE,
         cost_estimate=pl.CostEstimate(
-            flops=4 * strips * 64 * KPAD * 4 * SLICE, bytes_accessed=3 << 20, transcendentals=0
+            flops=2 * strips * 64 * KPAD * 4 * SLICE, bytes_accessed=1 << 20, transcendentals=0
         ),
         name="rows",
     )(tables, partner_tables)
@@ -220,7 +255,7 @@
         scratch_shapes=[pltpu.VMEM((2, SLICE, chips * SLICE), bf16), pltpu.SemaphoreType.DMA((chips,))],
         compiler_params=MUCH,
         name="screened",
-    )(pairs, screened, w_re, w_im)
+    )(pairs, screened, partner_tables, blocks)
     other = lax.ppermute(mine, "row", swap)
     partial = pl.pallas_call(
         direct_kernel,

time: 49.6 us -> 48.6 us (0.980)
  starting transfers between devices: 18.6 us -> 16.3 us
  waiting for transfers between devices: 1.5 us -> 3.15 us
    ppermute x1, starting transfers between devices: 6.42 us -> 1.92 us  [shards(): partner_tables = lax.ppermute(tables, 'row', swap)]
    ppermute x2 -> x1, starting transfers between devices: 4.33 us -> 6.42 us  [shards(): blocks = lax.ppermute(blocks, 'row', swap)]
    ppermute x1, waiting for transfers between devices: 0.01 us -> 1.78 us  [shards(): partner_tables = lax.ppermute(tables, 'row', swap)]
  transfers between devices with their start and end apart: 5 -> 4, of which waited for: 1 -> 2; matrix products, arithmetic and copies ran while one was open for 0% -> 0% of each run, Pallas kernels for 4% -> 4%
where the time goes in v7:
time: 48.6 us; the launch traced here: 48.1 us
  blocking collectives  19.5 us (40%)
  starting transfers between devices  16.3 us (34%)
  Pallas kernels  8.17 us (17%)
  waiting for transfers between devices  3.15 us (6%)
  local copies, waits for them, and re-layouts  0.97 us (2%)
    all_to_all x1, blocking collectives, shards(): lax.all_to_all(partial, 'row', 0, 0, axis_index_groups=same_core, tiled=T...  19.5 us
    ppermute x1, starting transfers between devices, shards(): blocks = lax.ppermute(blocks, 'row', swap)  6.42 us
    all_to_all x1, starting transfers between devices, shards(): lax.all_to_all(pairs, 'row', 0, 0, axis_index_groups=same_core, tiled=True)  5.88 us
    pallas_call x1, Pallas kernels, shards(): pl.pallas_call(columns_kernel, out_shape=(jax.ShapeDtypeStruct((bands + 2...  2.88 us
    pallas_call x1, Pallas kernels, shards(): pl.pallas_call(rows_kernel, out_shape=jax.ShapeDtypeStruct((strips * 64,...  2.08 us
    ppermute x1, starting transfers between devices, shards(): other = lax.ppermute(mine, 'row', swap)  2.06 us
    ppermute x1, starting transfers between devices, shards(): partner_tables = lax.ppermute(tables, 'row', swap)  1.92 us
    ppermute x1, waiting for transfers between devices, shards(): partner_tables = lax.ppermute(tables, 'row', swap)  1.78 us
  transfers between devices with their start and end apart: 4, of which 2 were waited for; matrix products, arithmetic and copies ran while one was open for 0% of the time, Pallas kernels for 4%

profile of v7, /device:TPU:1, one launch (start us, length us, event | category | flops | bytes accessed | tf_op | source)
XLA Modules:
  0.0 48.1 jit_solution(12538781476502910060)
XLA Ops:
  0.0 2.9 %columns.1 = (bf16[1216,128]{1,0:T(8,128)(2,1)}, bf16[8,128,256]{2,1,0:T(8,128)(2,1)}, bf16[1792,128]{1,0:T(8,128)(2,1)}) custom-call(bf16[384,128]{1,0:T(8,128)(2,1)} %bitcast.7, bf16[512,128]{1,0:T(8,128)(2,1)} %bitcast.6, s32[32,128]{1,0:T(8,128)} %bitcast.8, s32[32,128]{1,0:T(8,128)} %bitcast.9, s32[32,128]{1,0:T(8,128)} %bitcast.10, ...), custom_call_target="tpu_custom_call" | custom-call | tf_op jit(solution)/shard_map/columns/pallas_call | solution.py:211
  2.9 5.9 %all-to-all-start = ((bf16[8,128,256]{2,1,0:T(8,128)(2,1)}), bf16[8,128,256]{2,1,0:T(8,128)(2,1)S(1)}, u32[]{:S(2)}, u32[]{:S(2)}) async-start(bf16[8,128,256]{2,1,0:T(8,128)(2,1)} %get-tuple-element.10), calls=%async_computation | async-start | bytes 1048576 | tf_op jit(solution)/shard_map/all_to_all | solution.py:234
  8.8 6.4 %collective-permute-start.1 = (bf16[1792,128]{1,0:T(8,128)(2,1)}, bf16[1792,128]{1,0:T(8,128)(2,1)S(1)}, u32[]{:S(2)}, u32[]{:S(2)}) collective-permute-start(bf16[1792,128]{1,0:T(8,128)(2,1)} %get-tuple-element.13), channel_id=1, source_target_pairs={{0,32},{32,0},{64,96},{96,64},{128,160},{160,128},{192,224},{224,1... | collective-permute-start | bytes 1376264 | tf_op jit(solution)/shard_map/ppermute | solution.py:236
  15.2 1.9 %collective-permute-start = (bf16[1216,128]{1,0:T(8,128)(2,1)}, bf16[1216,128]{1,0:T(8,128)(2,1)S(1)}, u32[]{:S(2)}, u32[]{:S(2)}) collective-permute-start(bf16[1216,128]{1,0:T(8,128)(2,1)} %get-tuple-element.11.own_ref), channel_id=1, source_target_pairs={{0,32},{32,0},{64,96},{96,64},{128,160},{160,128},{192,224},{224,1... | collective-permute-start | bytes 933896 | tf_op jit(solution)/shard_map/ppermute | solution.py:235
  17.1 1.8 %collective-permute-done.partner_ref.joined_ref = bf16[1216,128]{1,0:T(8,128)(2,1)S(1)} collective-permute-done((bf16[1216,128]{1,0:T(8,128)(2,1)}, bf16[1216,128]{1,0:T(8,128)(2,1)S(1)}, u32[]{:S(2)}, u32[]{:S(2)}) %collective-permute-start) | collective-permute-done | bytes 311328 | tf_op jit(solution)/shard_map/ppermute | solution.py:235
  18.9 0.0 copy-start
  18.9 1.0 %copy-done = bf16[1216,128]{1,0:T(8,128)(2,1)S(1)} copy-done((bf16[1216,128]{1,0:T(8,128)(2,1)S(1)}, bf16[1216,128]{1,0:T(8,128)(2,1)}, u32[]{:S(2)}) %copy-start) | copy-done | bytes 311320
  19.9 2.1 %rows.1.density_ref = bf16[2048,512]{1,0:T(8,128)(2,1)S(1)} custom-call(bf16[1216,128]{1,0:T(8,128)(2,1)S(1)} %copy-done, bf16[1216,128]{1,0:T(8,128)(2,1)S(1)} %collective-permute-done.partner_ref.joined_ref), custom_call_target="tpu_custom_call" | custom-call | flops 536870912 | bytes 1048576 | tf_op jit(solution)/shard_map/rows/pallas_call | solution.py:237
  22.0 0.0 all-to-all-done.pairs_ref
  22.0 0.0 collective-permute-done.1.block_ref
  22.0 1.7 %screened.1.mine_ref = f32[2,128,256]{2,1,0:T(8,128)S(1)} custom-call(bf16[8,128,256]{2,1,0:T(8,128)(2,1)S(1)} %all-to-all-done.pairs_ref, bf16[2,128,2048]{2,1,0:T(8,128)(2,1)} %own_ref.1, bf16[1216,128]{1,0:T(8,128)(2,1)S(1)} %collective-permute-done.partner_ref.joined_ref, bf16[1792,128]{1,0:T(8,128)(2,1)S(1)} %collective-permute-done.1.block_ref), custom_call_target="tpu_custom_call" | custom-call | tf_op jit(solution)/shard_map/screened/pallas_call | solution.py:251
  23.6 2.1 %collective-permute-start.2 = (f32[2,128,256]{2,1,0:T(8,128)S(1)}, f32[2,128,256]{2,1,0:T(8,128)S(1)}, u32[]{:S(2)}, u32[]{:S(2)}) collective-permute-start(f32[2,128,256]{2,1,0:T(8,128)S(1)} %screened.1.mine_ref), channel_id=1, source_target_pairs={{0,32},{32,0},{64,96},{96,64},{128,160},{160,128},{192,224},{224,1... | collective-permute-start | bytes 786440 | tf_op jit(solution)/shard_map/ppermute | solution.py:259
  25.7 1.4 %collective-permute-done.2.other_ref = f32[2,128,256]{2,1,0:T(8,128)S(1)} collective-permute-done((f32[2,128,256]{2,1,0:T(8,128)S(1)}, f32[2,128,256]{2,1,0:T(8,128)S(1)}, u32[]{:S(2)}, u32[]{:S(2)}) %collective-permute-start.2) | collective-permute-done | bytes 262176 | tf_op jit(solution)/shard_map/ppermute | solution.py:259
  27.1 0.7 %direct.1 = bf16[8,256,256]{2,1,0:T(8,128)(2,1)S(1)} custom-call(f32[2,128,256]{2,1,0:T(8,128)S(1)} %screened.1.mine_ref, f32[2,128,256]{2,1,0:T(8,128)S(1)} %collective-permute-done.2.other_ref, bf16[2048,512]{1,0:T(8,128)(2,1)S(1)} %rows.1.density_ref), custom_call_target="tpu_custom_call" | custom-call | tf_op jit(solution)/shard_map/direct/pallas_call | solution.py:260
  27.8 19.5 %all_to_all.10.in_ref = bf16[8,256,256]{2,1,0:T(8,128)(2,1)S(1)} all-to-all(bf16[8,256,256]{2,1,0:T(8,128)(2,1)S(1)} %direct.1), channel_id=1, replica_groups={{0,64,128,192,448,384,320,256},{32,96,160,224,480,416,352,288},{1,65,12..., dimensions={0} | all-to-all | bytes 2097152 | tf_op jit(solution)/shard_map/all_to_all | solution.py:267
  47.3 0.8 %total.1 = f32[2,256,128]{2,1,0:T(8,128)} custom-call(bf16[8,256,256]{2,1,0:T(8,128)(2,1)S(1)} %all_to_all.10.in_ref), custom_call_target="tpu_custom_call" | custom-call | tf_op jit(solution)/shard_map/total/pallas_call | solution.py:268
Async XLA Ops:
  2.9 19.1 %all-to-all-start = ((bf16[8,128,256]{2,1,0:T(8,128)(2,1)}), bf16[8,128,256]{2,1,0:T(8,128)(2,1)S(1)}, u32[]{:S(2)}, u32[]{:S(2)}) async-start(bf16[8,128,256]{2,1,0:T(8,128)(2,1)} %get-tuple-element.10), calls=%async_computation | async-start | bytes 1048576 | tf_op jit(solution)/shard_map/all_to_all | solution.py:234
  8.8 13.2 %collective-permute-start.1 = (bf16[1792,128]{1,0:T(8,128)(2,1)}, bf16[1792,128]{1,0:T(8,128)(2,1)S(1)}, u32[]{:S(2)}, u32[]{:S(2)}) collective-permute-start(bf16[1792,128]{1,0:T(8,128)(2,1)} %get-tuple-element.13), channel_id=1, source_target_pairs={{0,32},{32,0},{64,96},{96,64},{128,160},{160,128},{192,224},{224,1... | collective-permute-start | bytes 1376264 | tf_op jit(solution)/shard_map/ppermute | solution.py:236
  15.2 3.7 %collective-permute-start = (bf16[1216,128]{1,0:T(8,128)(2,1)}, bf16[1216,128]{1,0:T(8,128)(2,1)S(1)}, u32[]{:S(2)}, u32[]{:S(2)}) collective-permute-start(bf16[1216,128]{1,0:T(8,128)(2,1)} %get-tuple-element.11.own_ref), channel_id=1, source_target_pairs={{0,32},{32,0},{64,96},{96,64},{128,160},{160,128},{192,224},{224,1... | collective-permute-start | bytes 933896 | tf_op jit(solution)/shard_map/ppermute | solution.py:235
  18.9 1.0 %copy-start = (bf16[1216,128]{1,0:T(8,128)(2,1)S(1)}, bf16[1216,128]{1,0:T(8,128)(2,1)}, u32[]{:S(2)}) copy-start(bf16[1216,128]{1,0:T(8,128)(2,1)} %get-tuple-element.11.own_ref) | copy-start | bytes 933892
  23.6 3.4 %collective-permute-start.2 = (f32[2,128,256]{2,1,0:T(8,128)S(1)}, f32[2,128,256]{2,1,0:T(8,128)S(1)}, u32[]{:S(2)}, u32[]{:S(2)}) collective-permute-start(f32[2,128,256]{2,1,0:T(8,128)S(1)} %screened.1.mine_ref), channel_id=1, source_target_pairs={{0,32},{32,0},{64,96},{96,64},{128,160},{160,128},{192,224},{224,1... | collective-permute-start | bytes 786440 | tf_op jit(solution)/shard_map/ppermute | solution.py:259

commit v8 on v7

--- a/solution.py
+++ b/solution.py
@@ -13,7 +13,7 @@
 KPAD = 256
 RING = (0, 1, 2, 3, 7, 6, 5, 4)
 STRIPS = 16
-JOINED = 2
+JOINED = 5
 MIB = 1024 * 1024
 LITTLE = pltpu.CompilerParams(vmem_limit_bytes=16 * MIB)
 MUCH = pltpu.CompilerParams(vmem_limit_bytes=52 * MIB)
@@ -242,9 +242,7 @@
         out_specs=pl.BlockSpec((STRIPS * 64, 4 * SLICE), lambda m: (m, 0)),
         scratch_shapes=[pltpu.VMEM((2 * KPAD, 4 * SLICE), bf16), pltpu.VMEM((2, strips, 128), f32)],
         compiler_params=LITTLE,
-        cost_estimate=pl.CostEstimate(
-            flops=2 * strips * 64 * KPAD * 4 * SLICE, bytes_accessed=1 << 20, transcendentals=0
-        ),
+        cost_estimate=pl.CostEstimate(flops=0, bytes_accessed=0, transcendentals=0),
         name="rows",
     )(tables, partner_tables)
     pairs, density = lax.optimization_barrier((pairs, density))

time: 48.6 us -> 47 us (0.967)
  waiting for transfers between devices: 3.15 us -> 1.15 us
  starting transfers between devices: 16.3 us -> 17.1 us
  blocking collectives: 19.5 us -> 18.8 us
    ppermute x1, starting transfers between devices: 6.42 us -> 1.92 us  [shards(): blocks = lax.ppermute(blocks, 'row', swap)]
    ppermute x1, starting transfers between devices: 1.92 us -> 6.42 us  [shards(): partner_tables = lax.ppermute(tables, 'row', swap)]
    ppermute x1, waiting for transfers between devices: 1.78 us -> 0.01 us  [shards(): partner_tables = lax.ppermute(tables, 'row', swap)]
    ppermute x1, starting transfers between devices: 2.06 us -> 2.84 us  [shards(): other = lax.ppermute(mine, 'row', swap)]
    all_to_all x1, blocking collectives: 19.5 us -> 18.8 us  [shards(): lax.all_to_all(partial, 'row', 0, 0, axis_index_groups=same_core, tiled=T...]
  transfers between devices with their start and end apart: 4 -> 4, of which waited for: 2 -> 1; matrix products, arithmetic and copies ran while one was open for 0% -> 0% of each run, Pallas kernels for 4% -> 5%
where the time goes in v8:
time: 47 us; the launch traced here: 46.2 us
  blocking collectives  18.8 us (40%)
  starting transfers between devices  17.1 us (36%)
  Pallas kernels  8.16 us (17%)
  waiting for transfers between devices  1.15 us (2%)
  local copies, waits for them, and re-layouts  0.99 us (2%)
    all_to_all x1, blocking collectives, shards(): lax.all_to_all(partial, 'row', 0, 0, axis_index_groups=same_core, tiled=T...  18.8 us
    ppermute x1, starting transfers between devices, shards(): partner_tables = lax.ppermute(tables, 'row', swap)  6.42 us
    all_to_all x1, starting transfers between devices, shards(): lax.all_to_all(pairs, 'row', 0, 0, axis_index_groups=same_core, tiled=True)  5.88 us
    pallas_call x1, Pallas kernels, shards(): pl.pallas_call(columns_kernel, out_shape=(jax.ShapeDtypeStruct((bands + 2...  2.86 us
    ppermute x1, starting transfers between devices, shards(): other = lax.ppermute(mine, 'row', swap)  2.84 us
    pallas_call x1, Pallas kernels, shards(): pl.pallas_call(rows_kernel, out_shape=jax.ShapeDtypeStruct((strips * 64,...  2.08 us
    ppermute x1, starting transfers between devices, shards(): blocks = lax.ppermute(blocks, 'row', swap)  1.92 us
    pallas_call x1, Pallas kernels, shards(): pl.pallas_call(screened_kernel, out_shape=jax.ShapeDtypeStruct((2, SLICE,...  1.65 us
  transfers between devices with their start and end apart: 4, of which 1 were waited for; matrix products, arithmetic and copies ran while one was open for 0% of the time, Pallas kernels for 5%

profile of v8, /device:TPU:1, one launch (start us, length us, event | category | flops | bytes accessed | tf_op | source)
XLA Modules:
  0.0 46.2 jit_solution(105857816921302848)
XLA Ops:
  0.0 2.9 %columns.1 = (bf16[1600,128]{1,0:T(8,128)(2,1)}, bf16[8,128,256]{2,1,0:T(8,128)(2,1)}, bf16[1408,128]{1,0:T(8,128)(2,1)}) custom-call(bf16[384,128]{1,0:T(8,128)(2,1)} %bitcast.7, bf16[512,128]{1,0:T(8,128)(2,1)} %bitcast.6, s32[32,128]{1,0:T(8,128)} %bitcast.8, s32[32,128]{1,0:T(8,128)} %bitcast.9, s32[32,128]{1,0:T(8,128)} %bitcast.10, ...), custom_call_target="tpu_custom_call" | custom-call | tf_op jit(solution)/shard_map/columns/pallas_call | solution.py:211
  2.9 5.9 %all-to-all-start = ((bf16[8,128,256]{2,1,0:T(8,128)(2,1)}), bf16[8,128,256]{2,1,0:T(8,128)(2,1)S(1)}, u32[]{:S(2)}, u32[]{:S(2)}) async-start(bf16[8,128,256]{2,1,0:T(8,128)(2,1)} %get-tuple-element.10), calls=%async_computation | async-start | bytes 1048576 | tf_op jit(solution)/shard_map/all_to_all | solution.py:234
  8.7 6.4 %collective-permute-start = (bf16[1600,128]{1,0:T(8,128)(2,1)}, bf16[1600,128]{1,0:T(8,128)(2,1)S(1)}, u32[]{:S(2)}, u32[]{:S(2)}) collective-permute-start(bf16[1600,128]{1,0:T(8,128)(2,1)} %get-tuple-element.11.own_ref), channel_id=1, source_target_pairs={{0,32},{32,0},{64,96},{96,64},{128,160},{160,128},{192,224},{224,1... | collective-permute-start | bytes 1228808 | tf_op jit(solution)/shard_map/ppermute | solution.py:235
  15.2 1.9 %collective-permute-start.1 = (bf16[1408,128]{1,0:T(8,128)(2,1)}, bf16[1408,128]{1,0:T(8,128)(2,1)S(1)}, u32[]{:S(2)}, u32[]{:S(2)}) collective-permute-start(bf16[1408,128]{1,0:T(8,128)(2,1)} %get-tuple-element.13), channel_id=1, source_target_pairs={{0,32},{32,0},{64,96},{96,64},{128,160},{160,128},{192,224},{224,1... | collective-permute-start | bytes 1081352 | tf_op jit(solution)/shard_map/ppermute | solution.py:236
  17.1 0.0 collective-permute-done.partner_ref.joined_ref
  17.1 0.0 copy-start
  17.1 1.0 %copy-done = bf16[1600,128]{1,0:T(8,128)(2,1)S(1)} copy-done((bf16[1600,128]{1,0:T(8,128)(2,1)S(1)}, bf16[1600,128]{1,0:T(8,128)(2,1)}, u32[]{:S(2)}) %copy-start) | copy-done | bytes 409624
  18.1 2.1 %rows.1.density_ref = bf16[2048,512]{1,0:T(8,128)(2,1)S(1)} custom-call(bf16[1600,128]{1,0:T(8,128)(2,1)S(1)} %copy-done, bf16[1600,128]{1,0:T(8,128)(2,1)S(1)} %collective-permute-done.partner_ref.joined_ref), custom_call_target="tpu_custom_call" | custom-call | tf_op jit(solution)/shard_map/rows/pallas_call | solution.py:237
  20.2 0.0 all-to-all-done.pairs_ref
  20.2 0.0 collective-permute-done.1.block_ref
  20.2 1.7 %screened.1.mine_ref = f32[2,128,256]{2,1,0:T(8,128)S(1)} custom-call(bf16[8,128,256]{2,1,0:T(8,128)(2,1)S(1)} %all-to-all-done.pairs_ref, bf16[2,128,2048]{2,1,0:T(8,128)(2,1)} %own_ref.1, bf16[1600,128]{1,0:T(8,128)(2,1)S(1)} %collective-permute-done.partner_ref.joined_ref, bf16[1408,128]{1,0:T(8,128)(2,1)S(1)} %collective-permute-done.1.block_ref), custom_call_target="tpu_custom_call" | custom-call | tf_op jit(solution)/shard_map/screened/pallas_call | solution.py:249
  21.9 2.8 %collective-permute-start.2 = (f32[2,128,256]{2,1,0:T(8,128)S(1)}, f32[2,128,256]{2,1,0:T(8,128)S(1)}, u32[]{:S(2)}, u32[]{:S(2)}) collective-permute-start(f32[2,128,256]{2,1,0:T(8,128)S(1)} %screened.1.mine_ref), channel_id=1, source_target_pairs={{0,32},{32,0},{64,96},{96,64},{128,160},{160,128},{192,224},{224,1... | collective-permute-start | bytes 786440 | tf_op jit(solution)/shard_map/ppermute | solution.py:257
  24.7 1.1 %collective-permute-done.2.other_ref = f32[2,128,256]{2,1,0:T(8,128)S(1)} collective-permute-done((f32[2,128,256]{2,1,0:T(8,128)S(1)}, f32[2,128,256]{2,1,0:T(8,128)S(1)}, u32[]{:S(2)}, u32[]{:S(2)}) %collective-permute-start.2) | collective-permute-done | bytes 262176 | tf_op jit(solution)/shard_map/ppermute | solution.py:257
  25.9 0.7 %direct.1 = bf16[8,256,256]{2,1,0:T(8,128)(2,1)S(1)} custom-call(f32[2,128,256]{2,1,0:T(8,128)S(1)} %screened.1.mine_ref, f32[2,128,256]{2,1,0:T(8,128)S(1)} %collective-permute-done.2.other_ref, bf16[2048,512]{1,0:T(8,128)(2,1)S(1)} %rows.1.density_ref), custom_call_target="tpu_custom_call" | custom-call | tf_op jit(solution)/shard_map/direct/pallas_call | solution.py:258
  26.6 18.8 %all_to_all.10.in_ref = bf16[8,256,256]{2,1,0:T(8,128)(2,1)S(1)} all-to-all(bf16[8,256,256]{2,1,0:T(8,128)(2,1)S(1)} %direct.1), channel_id=1, replica_groups={{0,64,128,192,448,384,320,256},{32,96,160,224,480,416,352,288},{1,65,12..., dimensions={0} | all-to-all | bytes 2097152 | tf_op jit(solution)/shard_map/all_to_all | solution.py:265
  45.4 0.8 %total.1 = f32[2,256,128]{2,1,0:T(8,128)} custom-call(bf16[8,256,256]{2,1,0:T(8,128)(2,1)S(1)} %all_to_all.10.in_ref), custom_call_target="tpu_custom_call" | custom-call | tf_op jit(solution)/shard_map/total/pallas_call | solution.py:266
Async XLA Ops:
  2.9 17.3 %all-to-all-start = ((bf16[8,128,256]{2,1,0:T(8,128)(2,1)}), bf16[8,128,256]{2,1,0:T(8,128)(2,1)S(1)}, u32[]{:S(2)}, u32[]{:S(2)}) async-start(bf16[8,128,256]{2,1,0:T(8,128)(2,1)} %get-tuple-element.10), calls=%async_computation | async-start | bytes 1048576 | tf_op jit(solution)/shard_map/all_to_all | solution.py:234
  8.7 8.4 %collective-permute-start = (bf16[1600,128]{1,0:T(8,128)(2,1)}, bf16[1600,128]{1,0:T(8,128)(2,1)S(1)}, u32[]{:S(2)}, u32[]{:S(2)}) collective-permute-start(bf16[1600,128]{1,0:T(8,128)(2,1)} %get-tuple-element.11.own_ref), channel_id=1, source_target_pairs={{0,32},{32,0},{64,96},{96,64},{128,160},{160,128},{192,224},{224,1... | collective-permute-start | bytes 1228808 | tf_op jit(solution)/shard_map/ppermute | solution.py:235
  15.2 5.0 %collective-permute-start.1 = (bf16[1408,128]{1,0:T(8,128)(2,1)}, bf16[1408,128]{1,0:T(8,128)(2,1)S(1)}, u32[]{:S(2)}, u32[]{:S(2)}) collective-permute-start(bf16[1408,128]{1,0:T(8,128)(2,1)} %get-tuple-element.13), channel_id=1, source_target_pairs={{0,32},{32,0},{64,96},{96,64},{128,160},{160,128},{192,224},{224,1... | collective-permute-start | bytes 1081352 | tf_op jit(solution)/shard_map/ppermute | solution.py:236
  17.1 1.0 %copy-start = (bf16[1600,128]{1,0:T(8,128)(2,1)S(1)}, bf16[1600,128]{1,0:T(8,128)(2,1)}, u32[]{:S(2)}) copy-start(bf16[1600,128]{1,0:T(8,128)(2,1)} %get-tuple-element.11.own_ref) | copy-start | bytes 1228804
  21.9 4.0 %collective-permute-start.2 = (f32[2,128,256]{2,1,0:T(8,128)S(1)}, f32[2,128,256]{2,1,0:T(8,128)S(1)}, u32[]{:S(2)}, u32[]{:S(2)}) collective-permute-start(f32[2,128,256]{2,1,0:T(8,128)S(1)} %screened.1.mine_ref), channel_id=1, source_target_pairs={{0,32},{32,0},{64,96},{96,64},{128,160},{160,128},{192,224},{224,1... | collective-permute-start | bytes 786440 | tf_op jit(solution)/shard_map/ppermute | solution.py:257

commit v9 on v8

--- a/solution.py
+++ b/solution.py
@@ -12,7 +12,7 @@
 WIDTH = 128
 KPAD = 256
 RING = (0, 1, 2, 3, 7, 6, 5, 4)
-STRIPS = 16
+STRIPS = 8
 JOINED = 5
 MIB = 1024 * 1024
 LITTLE = pltpu.CompilerParams(vmem_limit_bytes=16 * MIB)
@@ -74,6 +74,15 @@
         copy.wait()
     stores = [pltpu.make_async_copy(bands, table_ref.at[pl.ds(0, count), :], out_sems.at[0])]
     stores[0].start()
+    for copy in gathers:
+        copy.wait()
+    joined = JOINED * SLICE
+    rest = blocks.shape[0] - joined
+    to = table_ref.at[pl.ds(count + 2 * strips, joined), :]
+    stores.append(pltpu.make_async_copy(blocks.at[pl.ds(0, joined), :], to, out_sems.at[2]))
+    stores[-1].start()
+    stores.append(pltpu.make_async_copy(blocks.at[pl.ds(joined, rest), :], block_ref, out_sems.at[3]))
+    stores[-1].start()
     own = pl.ds(lax.axis_index("col"), 1)
     picked = []
     for which, (width, start, stop) in enumerate(((VAL, 0, split), (CON, split, count))):
@@ -93,21 +102,12 @@
     for place in range(out_ref.shape[0]):
         stores.append(pltpu.make_async_copy(pairs, out_ref.at[place], pair_sems.at[place]))
         stores[-1].start()
-    for copy in gathers:
-        copy.wait()
-    joined = JOINED * SLICE
-    rest = blocks.shape[0] - joined
-    to = table_ref.at[pl.ds(count + 2 * strips, joined), :]
-    stores.append(pltpu.make_async_copy(blocks.at[pl.ds(0, joined), :], to, out_sems.at[2]))
-    stores[-1].start()
-    stores.append(pltpu.make_async_copy(blocks.at[pl.ds(joined, rest), :], block_ref, out_sems.at[3]))
-    stores[-1].start()
     for copy in stores:
         copy.wait()
 
 
 def rows_kernel(own_ref, partner_ref, density_ref, table, at_ref):
-    core = core_of()
+    first = core_of() * (at_ref.shape[1] // 2) + pl.program_id(0) * STRIPS
 
     @pl.when(pl.program_id(0) == 0)
     def _():
@@ -124,10 +124,7 @@
 
     picked = []
     for which in range(2):
-        index = []
-        for s in range(STRIPS):
-            strip = lane_matrix(at_ref[which, pl.ds(pl.program_id(0) * STRIPS + s, 1), :]).reshape(-1, 2, FINE, 128)
-            index.append(jnp.where(core == 0, strip[:, 0], strip[:, 1]).reshape(-1, 128))
+        index = [lane_matrix(at_ref[which, pl.ds(first + s, 1), :]) for s in range(STRIPS)]
         hot = one_hot(jnp.concatenate(index, 0), KPAD)
         picked.append(
             jnp.dot(hot, table[which * KPAD : (which + 1) * KPAD, :], preferred_element_type=jnp.float32)
@@ -169,24 +166,25 @@
         screened[(2 + half) * SLICE : (3 + half) * SLICE, WIDTH:] = -x[:, :WIDTH]
     parts = 4
     rows = density_ref.shape[0] // parts
-    strips = rows // 64
+    strips = rows // 128
     for m in range(parts):
         direct = jnp.dot(
             density_ref[m * rows : (m + 1) * rows, :], screened[...], preferred_element_type=jnp.float32
         )
         direct = direct.reshape(strips, -1, FINE, 2 * WIDTH)
         direct = jnp.concatenate([direct[s] for s in range(strips)], 1).astype(jnp.bfloat16)
-        for place, chip in enumerate(RING):
-            out_ref[place, m * strips * FINE : (m + 1) * strips * FINE, :] = direct[chip]
+        out_ref[:, m * strips * FINE : (m + 1) * strips * FINE, :] = direct
 
 
 def total_kernel(in_ref, out_ref):
-    for part in range(2):
-        lanes = slice(part * WIDTH, (part + 1) * WIDTH)
-        total = in_ref[0, :, lanes].astype(jnp.float32)
-        for chip in range(1, in_ref.shape[0]):
-            total += in_ref[chip, :, lanes].astype(jnp.float32)
-        out_ref[part] = total
+    rows = in_ref.shape[1]
+    for core in range(2):
+        for part in range(2):
+            lanes = slice(part * WIDTH, (part + 1) * WIDTH)
+            total = in_ref[core, :, lanes].astype(jnp.float32)
+            for chip in range(1, in_ref.shape[0] // 2):
+                total += in_ref[2 * chip + core, :, lanes].astype(jnp.float32)
+            out_ref[part, core * rows : (core + 1) * rows, :] = total
 
 
 def whole(array):
@@ -237,9 +235,9 @@
     density = pl.pallas_call(
         rows_kernel,
         out_shape=jax.ShapeDtypeStruct((strips * 64, 4 * SLICE), bf16),
-        grid=(strips // STRIPS,),
+        grid=(strips // 2 // STRIPS,),
         in_specs=[whole(tables), whole(partner_tables)],
-        out_specs=pl.BlockSpec((STRIPS * 64, 4 * SLICE), lambda m: (m, 0)),
+        out_specs=pl.BlockSpec((STRIPS * 128, 4 * SLICE), lambda m: (m, 0)),
         scratch_shapes=[pltpu.VMEM((2 * KPAD, 4 * SLICE), bf16), pltpu.VMEM((2, strips, 128), f32)],
         compiler_params=LITTLE,
         cost_estimate=pl.CostEstimate(flops=0, bytes_accessed=0, transcendentals=0),
@@ -257,12 +255,12 @@
     other = lax.ppermute(mine, "row", swap)
     partial = pl.pallas_call(
         direct_kernel,
-        out_shape=jax.ShapeDtypeStruct((chips, strips * FINE, 2 * WIDTH), bf16),
+        out_shape=jax.ShapeDtypeStruct((rows, strips // 2 * FINE, 2 * WIDTH), bf16),
         scratch_shapes=[pltpu.VMEM((4 * SLICE, 2 * WIDTH), bf16)],
         compiler_params=LITTLE,
         name="direct",
     )(mine, other, density)
-    partial = lax.all_to_all(partial, "row", 0, 0, axis_index_groups=same_core, tiled=True)
+    partial = lax.all_to_all(partial, "row", 0, 0, tiled=True)
     out = pl.pallas_call(
         total_kernel,
         out_shape=jax.ShapeDtypeStruct((2, strips * FINE, WIDTH), f32),

time: 47 us -> 48.5 us (1.032)
  blocking collectives: 18.8 us -> 20.8 us
    all_to_all x1, blocking collectives: 18.8 us -> 20.8 us  [shards(): partial = lax.all_to_all(partial, 'row', 0, 0, tiled=True)]
  transfers between devices with their start and end apart: 4 -> 4, of which waited for: 1 -> 1; matrix products, arithmetic and copies ran while one was open for 0% -> 0% of each run, Pallas kernels for 5% -> 4%
where the time goes in v9:
time: 48.5 us; the launch traced here: 48.1 us
  blocking collectives  20.8 us (43%)
  starting transfers between devices  17.1 us (35%)
  Pallas kernels  7.94 us (16%)
  waiting for transfers between devices  1.15 us (2%)
  local copies, waits for them, and re-layouts  0.99 us (2%)
    all_to_all x1, blocking collectives, shards(): partial = lax.all_to_all(partial, 'row', 0, 0, tiled=True)  20.8 us
    ppermute x1, starting transfers between devices, shards(): partner_tables = lax.ppermute(tables, 'row', swap)  6.42 us
    all_to_all x1, starting transfers between devices, shards(): lax.all_to_all(pairs, 'row', 0, 0, axis_index_groups=same_core, tiled=True)  5.88 us
    ppermute x1, starting transfers between devices, shards(): other = lax.ppermute(mine, 'row', swap)  2.9 us
    pallas_call x1, Pallas kernels, shards(): pl.pallas_call(columns_kernel, out_shape=(jax.ShapeDtypeStruct((bands + 2...  2.71 us
    pallas_call x1, Pallas kernels, shards(): pl.pallas_call(rows_kernel, out_shape=jax.ShapeDtypeStruct((strips * 64,...  2.03 us
    ppermute x1, starting transfers between devices, shards(): blocks = lax.ppermute(blocks, 'row', swap)  1.92 us
    pallas_call x1, Pallas kernels, shards(): pl.pallas_call(screened_kernel, out_shape=jax.ShapeDtypeStruct((2, SLICE,...  1.65 us
  transfers between devices with their start and end apart: 4, of which 1 were waited for; matrix products, arithmetic and copies ran while one was open for 0% of the time, Pallas kernels for 4%

profile of v9, /device:TPU:1, one launch (start us, length us, event | category | flops | bytes accessed | tf_op | source)
XLA Modules:
  0.0 48.1 jit_solution(16462761782591612046)
XLA Ops:
  0.0 2.7 %columns.1 = (bf16[1600,128]{1,0:T(8,128)(2,1)}, bf16[8,128,256]{2,1,0:T(8,128)(2,1)}, bf16[1408,128]{1,0:T(8,128)(2,1)}) custom-call(bf16[384,128]{1,0:T(8,128)(2,1)} %bitcast.7, bf16[512,128]{1,0:T(8,128)(2,1)} %bitcast.6, s32[32,128]{1,0:T(8,128)} %bitcast.8, s32[32,128]{1,0:T(8,128)} %bitcast.9, s32[32,128]{1,0:T(8,128)} %bitcast.10, ...), custom_call_target="tpu_custom_call" | custom-call | tf_op jit(solution)/shard_map/columns/pallas_call | solution.py:209
  2.7 5.9 %all-to-all-start = ((bf16[8,128,256]{2,1,0:T(8,128)(2,1)}), bf16[8,128,256]{2,1,0:T(8,128)(2,1)S(1)}, u32[]{:S(2)}, u32[]{:S(2)}) async-start(bf16[8,128,256]{2,1,0:T(8,128)(2,1)} %get-tuple-element.10), calls=%async_computation | async-start | bytes 1048576 | tf_op jit(solution)/shard_map/all_to_all | solution.py:232
  8.6 6.4 %collective-permute-start = (bf16[1600,128]{1,0:T(8,128)(2,1)}, bf16[1600,128]{1,0:T(8,128)(2,1)S(1)}, u32[]{:S(2)}, u32[]{:S(2)}) collective-permute-start(bf16[1600,128]{1,0:T(8,128)(2,1)} %get-tuple-element.11.own_ref), channel_id=1, source_target_pairs={{0,32},{32,0},{64,96},{96,64},{128,160},{160,128},{192,224},{224,1... | collective-permute-start | bytes 1228808 | tf_op jit(solution)/shard_map/ppermute | solution.py:233
  15.0 1.9 %collective-permute-start.1 = (bf16[1408,128]{1,0:T(8,128)(2,1)}, bf16[1408,128]{1,0:T(8,128)(2,1)S(1)}, u32[]{:S(2)}, u32[]{:S(2)}) collective-permute-start(bf16[1408,128]{1,0:T(8,128)(2,1)} %get-tuple-element.13), channel_id=1, source_target_pairs={{0,32},{32,0},{64,96},{96,64},{128,160},{160,128},{192,224},{224,1... | collective-permute-start | bytes 1081352 | tf_op jit(solution)/shard_map/ppermute | solution.py:234
  17.0 0.0 collective-permute-done.partner_ref.joined_ref
  17.0 0.0 copy-start
  17.0 1.0 %copy-done = bf16[1600,128]{1,0:T(8,128)(2,1)S(1)} copy-done((bf16[1600,128]{1,0:T(8,128)(2,1)S(1)}, bf16[1600,128]{1,0:T(8,128)(2,1)}, u32[]{:S(2)}) %copy-start) | copy-done | bytes 409624
  18.0 2.0 %rows.1.density_ref = bf16[2048,512]{1,0:T(8,128)(2,1)S(1)} custom-call(bf16[1600,128]{1,0:T(8,128)(2,1)S(1)} %copy-done, bf16[1600,128]{1,0:T(8,128)(2,1)S(1)} %collective-permute-done.partner_ref.joined_ref), custom_call_target="tpu_custom_call" | custom-call | tf_op jit(solution)/shard_map/rows/pallas_call | solution.py:235
  20.0 0.0 all-to-all-done.pairs_ref
  20.0 0.0 collective-permute-done.1.block_ref
  20.0 1.7 %screened.1.mine_ref = f32[2,128,256]{2,1,0:T(8,128)S(1)} custom-call(bf16[8,128,256]{2,1,0:T(8,128)(2,1)S(1)} %all-to-all-done.pairs_ref, bf16[2,128,2048]{2,1,0:T(8,128)(2,1)} %own_ref.1, bf16[1600,128]{1,0:T(8,128)(2,1)S(1)} %collective-permute-done.partner_ref.joined_ref, bf16[1408,128]{1,0:T(8,128)(2,1)S(1)} %collective-permute-done.1.block_ref), custom_call_target="tpu_custom_call" | custom-call | tf_op jit(solution)/shard_map/screened/pallas_call | solution.py:247
  21.7 2.9 %collective-permute-start.2 = (f32[2,128,256]{2,1,0:T(8,128)S(1)}, f32[2,128,256]{2,1,0:T(8,128)S(1)}, u32[]{:S(2)}, u32[]{:S(2)}) collective-permute-start(f32[2,128,256]{2,1,0:T(8,128)S(1)} %screened.1.mine_ref), channel_id=1, source_target_pairs={{0,32},{32,0},{64,96},{96,64},{128,160},{160,128},{192,224},{224,1... | collective-permute-start | bytes 786440 | tf_op jit(solution)/shard_map/ppermute | solution.py:255
  24.6 1.1 %collective-permute-done.2.other_ref = f32[2,128,256]{2,1,0:T(8,128)S(1)} collective-permute-done((f32[2,128,256]{2,1,0:T(8,128)S(1)}, f32[2,128,256]{2,1,0:T(8,128)S(1)}, u32[]{:S(2)}, u32[]{:S(2)}) %collective-permute-start.2) | collective-permute-done | bytes 262176 | tf_op jit(solution)/shard_map/ppermute | solution.py:255
  25.7 0.7 %direct.1 = bf16[16,128,256]{2,1,0:T(8,128)(2,1)S(1)} custom-call(f32[2,128,256]{2,1,0:T(8,128)S(1)} %screened.1.mine_ref, f32[2,128,256]{2,1,0:T(8,128)S(1)} %collective-permute-done.2.other_ref, bf16[2048,512]{1,0:T(8,128)(2,1)S(1)} %rows.1.density_ref), custom_call_target="tpu_custom_call" | custom-call | tf_op jit(solution)/shard_map/direct/pallas_call | solution.py:256
  26.5 20.8 %all_to_all.10.in_ref = bf16[16,128,256]{2,1,0:T(8,128)(2,1)S(1)} all-to-all(bf16[16,128,256]{2,1,0:T(8,128)(2,1)S(1)} %direct.1), channel_id=1, replica_groups=mesh['row'=16,'col'=32] {'row'}, dimensions={0} | all-to-all | bytes 2097152 | tf_op jit(solution)/shard_map/all_to_all | solution.py:263
  47.3 0.8 %total.1 = f32[2,256,128]{2,1,0:T(8,128)} custom-call(bf16[16,128,256]{2,1,0:T(8,128)(2,1)S(1)} %all_to_all.10.in_ref), custom_call_target="tpu_custom_call" | custom-call | tf_op jit(solution)/shard_map/total/pallas_call | solution.py:264
Async XLA Ops:
  2.7 17.3 %all-to-all-start = ((bf16[8,128,256]{2,1,0:T(8,128)(2,1)}), bf16[8,128,256]{2,1,0:T(8,128)(2,1)S(1)}, u32[]{:S(2)}, u32[]{:S(2)}) async-start(bf16[8,128,256]{2,1,0:T(8,128)(2,1)} %get-tuple-element.10), calls=%async_computation | async-start | bytes 1048576 | tf_op jit(solution)/shard_map/all_to_all | solution.py:232
  8.6 8.4 %collective-permute-start = (bf16[1600,128]{1,0:T(8,128)(2,1)}, bf16[1600,128]{1,0:T(8,128)(2,1)S(1)}, u32[]{:S(2)}, u32[]{:S(2)}) collective-permute-start(bf16[1600,128]{1,0:T(8,128)(2,1)} %get-tuple-element.11.own_ref), channel_id=1, source_target_pairs={{0,32},{32,0},{64,96},{96,64},{128,160},{160,128},{192,224},{224,1... | collective-permute-start | bytes 1228808 | tf_op jit(solution)/shard_map/ppermute | solution.py:233
  15.0 5.0 %collective-permute-start.1 = (bf16[1408,128]{1,0:T(8,128)(2,1)}, bf16[1408,128]{1,0:T(8,128)(2,1)S(1)}, u32[]{:S(2)}, u32[]{:S(2)}) collective-permute-start(bf16[1408,128]{1,0:T(8,128)(2,1)} %get-tuple-element.13), channel_id=1, source_target_pairs={{0,32},{32,0},{64,96},{96,64},{128,160},{160,128},{192,224},{224,1... | collective-permute-start | bytes 1081352 | tf_op jit(solution)/shard_map/ppermute | solution.py:234
  17.0 1.0 %copy-start = (bf16[1600,128]{1,0:T(8,128)(2,1)S(1)}, bf16[1600,128]{1,0:T(8,128)(2,1)}, u32[]{:S(2)}) copy-start(bf16[1600,128]{1,0:T(8,128)(2,1)} %get-tuple-element.11.own_ref) | copy-start | bytes 1228804
  21.7 4.0 %collective-permute-start.2 = (f32[2,128,256]{2,1,0:T(8,128)S(1)}, f32[2,128,256]{2,1,0:T(8,128)S(1)}, u32[]{:S(2)}, u32[]{:S(2)}) collective-permute-start(f32[2,128,256]{2,1,0:T(8,128)S(1)} %screened.1.mine_ref), channel_id=1, source_target_pairs={{0,32},{32,0},{64,96},{96,64},{128,160},{160,128},{192,224},{224,1... | collective-permute-start | bytes 786440 | tf_op jit(solution)/shard_map/ppermute | solution.py:255

commit v10 on v8

--- a/solution.py
+++ b/solution.py
@@ -74,6 +74,15 @@
         copy.wait()
     stores = [pltpu.make_async_copy(bands, table_ref.at[pl.ds(0, count), :], out_sems.at[0])]
     stores[0].start()
+    for copy in gathers:
+        copy.wait()
+    joined = JOINED * SLICE
+    rest = blocks.shape[0] - joined
+    to = table_ref.at[pl.ds(count + 2 * strips, joined), :]
+    stores.append(pltpu.make_async_copy(blocks.at[pl.ds(0, joined), :], to, out_sems.at[2]))
+    stores[-1].start()
+    stores.append(pltpu.make_async_copy(blocks.at[pl.ds(joined, rest), :], block_ref, out_sems.at[3]))
+    stores[-1].start()
     own = pl.ds(lax.axis_index("col"), 1)
     picked = []
     for which, (width, start, stop) in enumerate(((VAL, 0, split), (CON, split, count))):
@@ -93,15 +102,6 @@
     for place in range(out_ref.shape[0]):
         stores.append(pltpu.make_async_copy(pairs, out_ref.at[place], pair_sems.at[place]))
         stores[-1].start()
-    for copy in gathers:
-        copy.wait()
-    joined = JOINED * SLICE
-    rest = blocks.shape[0] - joined
-    to = table_ref.at[pl.ds(count + 2 * strips, joined), :]
-    stores.append(pltpu.make_async_copy(blocks.at[pl.ds(0, joined), :], to, out_sems.at[2]))
-    stores[-1].start()
-    stores.append(pltpu.make_async_copy(blocks.at[pl.ds(joined, rest), :], block_ref, out_sems.at[3]))
-    stores[-1].start()
     for copy in stores:
         copy.wait()
 
@@ -135,7 +135,7 @@
     density_ref[...] = jnp.concatenate(densities(*picked), 1).astype(jnp.bfloat16)
 
 
-def screened_kernel(pairs_ref, own_ref, joined_ref, block_ref, out_ref, held, sems):
+def screened_kernel(pairs_ref, own_ref, joined_ref, block_ref, out_ref, sent_ref, held, sems):
     core = core_of()
     copies = []
     for place, chip in enumerate(RING):
@@ -157,13 +157,16 @@
         for part in range(2):
             w = jnp.concatenate(blocks[part * chips : (part + 1) * chips], 1) if half else held[part]
             parts.append(jnp.dot(w, pairs, preferred_element_type=jnp.float32))
-        out_ref[half, :, :WIDTH] = parts[0][:, :WIDTH] - parts[1][:, WIDTH:]
-        out_ref[half, :, WIDTH:] = parts[0][:, WIDTH:] + parts[1][:, :WIDTH]
+        real = parts[0][:, :WIDTH] - parts[1][:, WIDTH:]
+        imag = parts[0][:, WIDTH:] + parts[1][:, :WIDTH]
+        both = jnp.concatenate([real, imag], 1)
+        out_ref[half] = both
+        sent_ref[half] = both.astype(jnp.bfloat16)
 
 
 def direct_kernel(mine_ref, other_ref, density_ref, out_ref, screened):
     for half in range(2):
-        x = (mine_ref[half] + other_ref[1 - half]).astype(jnp.bfloat16)
+        x = (mine_ref[half] + other_ref[1 - half].astype(jnp.float32)).astype(jnp.bfloat16)
         screened[half * SLICE : (half + 1) * SLICE, :] = x
         screened[(2 + half) * SLICE : (3 + half) * SLICE, :WIDTH] = x[:, WIDTH:]
         screened[(2 + half) * SLICE : (3 + half) * SLICE, WIDTH:] = -x[:, :WIDTH]
@@ -246,15 +249,15 @@
         name="rows",
     )(tables, partner_tables)
     pairs, density = lax.optimization_barrier((pairs, density))
-    mine = pl.pallas_call(
+    mine, other = pl.pallas_call(
         screened_kernel,
-        out_shape=jax.ShapeDtypeStruct((2, SLICE, 2 * WIDTH), f32),
+        out_shape=tuple(jax.ShapeDtypeStruct((2, SLICE, 2 * WIDTH), kind) for kind in (f32, bf16)),
         in_specs=[in_vmem, anywhere, in_vmem, in_vmem],
         scratch_shapes=[pltpu.VMEM((2, SLICE, chips * SLICE), bf16), pltpu.SemaphoreType.DMA((chips,))],
         compiler_params=MUCH,
         name="screened",
     )(pairs, screened, partner_tables, blocks)
-    other = lax.ppermute(mine, "row", swap)
+    other = lax.ppermute(other, "row", swap)
     partial = pl.pallas_call(
         direct_kernel,
         out_shape=jax.ShapeDtypeStruct((chips, strips * FINE, 2 * WIDTH), bf16),

time: 47 us -> 46.6 us (level)
  no operation moved by 1% of the time
where the time goes in v10:
time: 46.6 us; the launch traced here: 45.9 us
  blocking collectives  18.8 us (40%)
  starting transfers between devices  17.1 us (37%)
  Pallas kernels  7.99 us (17%)
  local copies, waits for them, and re-layouts  0.99 us (2%)
  waiting for transfers between devices  0.97 us (2%)
    all_to_all x1, blocking collectives, shards(): lax.all_to_all(partial, 'row', 0, 0, axis_index_groups=same_core, tiled=T...  18.8 us
    ppermute x1, starting transfers between devices, shards(): partner_tables = lax.ppermute(tables, 'row', swap)  6.42 us
    all_to_all x1, starting transfers between devices, shards(): lax.all_to_all(pairs, 'row', 0, 0, axis_index_groups=same_core, tiled=True)  5.88 us
    ppermute x1, starting transfers between devices, shards(): other = lax.ppermute(other, 'row', swap)  2.85 us
    pallas_call x1, Pallas kernels, shards(): pl.pallas_call(columns_kernel, out_shape=(jax.ShapeDtypeStruct((bands + 2...  2.71 us
    pallas_call x1, Pallas kernels, shards(): pl.pallas_call(rows_kernel, out_shape=jax.ShapeDtypeStruct((strips * 64,...  2.08 us
    ppermute x1, starting transfers between devices, shards(): blocks = lax.ppermute(blocks, 'row', swap)  1.92 us
    pallas_call x1, Pallas kernels, shards(): pl.pallas_call(screened_kernel, out_shape=tuple((jax.ShapeDtypeStruct((2,...  1.65 us
  transfers between devices with their start and end apart: 4, of which 1 were waited for; matrix products, arithmetic and copies ran while one was open for 0% of the time, Pallas kernels for 5%

profile of v10, /device:TPU:1, one launch (start us, length us, event | category | flops | bytes accessed | tf_op | source)
XLA Modules:
  0.0 45.9 jit_solution(13529574493098671764)
XLA Ops:
  0.0 2.7 %columns.1 = (bf16[1600,128]{1,0:T(8,128)(2,1)}, bf16[8,128,256]{2,1,0:T(8,128)(2,1)}, bf16[1408,128]{1,0:T(8,128)(2,1)}) custom-call(bf16[384,128]{1,0:T(8,128)(2,1)} %bitcast.7, bf16[512,128]{1,0:T(8,128)(2,1)} %bitcast.6, s32[32,128]{1,0:T(8,128)} %bitcast.8, s32[32,128]{1,0:T(8,128)} %bitcast.9, s32[32,128]{1,0:T(8,128)} %bitcast.10, ...), custom_call_target="tpu_custom_call" | custom-call | tf_op jit(solution)/shard_map/columns/pallas_call | solution.py:214
  2.7 5.9 %all-to-all-start = ((bf16[8,128,256]{2,1,0:T(8,128)(2,1)}), bf16[8,128,256]{2,1,0:T(8,128)(2,1)S(1)}, u32[]{:S(2)}, u32[]{:S(2)}) async-start(bf16[8,128,256]{2,1,0:T(8,128)(2,1)} %get-tuple-element.12), calls=%async_computation | async-start | bytes 1048576 | tf_op jit(solution)/shard_map/all_to_all | solution.py:237
  8.6 6.4 %collective-permute-start = (bf16[1600,128]{1,0:T(8,128)(2,1)}, bf16[1600,128]{1,0:T(8,128)(2,1)S(1)}, u32[]{:S(2)}, u32[]{:S(2)}) collective-permute-start(bf16[1600,128]{1,0:T(8,128)(2,1)} %get-tuple-element.13.own_ref), channel_id=1, source_target_pairs={{0,32},{32,0},{64,96},{96,64},{128,160},{160,128},{192,224},{224,1... | collective-permute-start | bytes 1228808 | tf_op jit(solution)/shard_map/ppermute | solution.py:238
  15.0 1.9 %collective-permute-start.1 = (bf16[1408,128]{1,0:T(8,128)(2,1)}, bf16[1408,128]{1,0:T(8,128)(2,1)S(1)}, u32[]{:S(2)}, u32[]{:S(2)}) collective-permute-start(bf16[1408,128]{1,0:T(8,128)(2,1)} %get-tuple-element.15), channel_id=1, source_target_pairs={{0,32},{32,0},{64,96},{96,64},{128,160},{160,128},{192,224},{224,1... | collective-permute-start | bytes 1081352 | tf_op jit(solution)/shard_map/ppermute | solution.py:239
  17.0 0.0 collective-permute-done.partner_ref.joined_ref
  17.0 0.0 copy-start
  17.0 1.0 %copy-done = bf16[1600,128]{1,0:T(8,128)(2,1)S(1)} copy-done((bf16[1600,128]{1,0:T(8,128)(2,1)S(1)}, bf16[1600,128]{1,0:T(8,128)(2,1)}, u32[]{:S(2)}) %copy-start) | copy-done | bytes 409624
  18.0 2.1 %rows.1.density_ref = bf16[2048,512]{1,0:T(8,128)(2,1)S(1)} custom-call(bf16[1600,128]{1,0:T(8,128)(2,1)S(1)} %copy-done, bf16[1600,128]{1,0:T(8,128)(2,1)S(1)} %collective-permute-done.partner_ref.joined_ref), custom_call_target="tpu_custom_call" | custom-call | tf_op jit(solution)/shard_map/rows/pallas_call | solution.py:240
  20.1 0.0 all-to-all-done.pairs_ref
  20.1 0.0 collective-permute-done.1.block_ref
  20.1 1.7 %screened.1 = (f32[2,128,256]{2,1,0:T(8,128)S(1)}, bf16[2,128,256]{2,1,0:T(8,128)(2,1)S(1)}) custom-call(bf16[8,128,256]{2,1,0:T(8,128)(2,1)S(1)} %all-to-all-done.pairs_ref, bf16[2,128,2048]{2,1,0:T(8,128)(2,1)} %own_ref.1, bf16[1600,128]{1,0:T(8,128)(2,1)S(1)} %collective-permute-done.partner_ref.joined_ref, ...), custom_call_target="tpu_custom_call" | custom-call | tf_op jit(solution)/shard_map/screened/pallas_call | solution.py:252
  21.7 2.8 %collective-permute-start.2 = (bf16[2,128,256]{2,1,0:T(8,128)(2,1)S(1)}, bf16[2,128,256]{2,1,0:T(8,128)(2,1)S(1)}, u32[]{:S(2)}, u32[]{:S(2)}) collective-permute-start(bf16[2,128,256]{2,1,0:T(8,128)(2,1)S(1)} %get-tuple-element.17), channel_id=1, source_target_pairs={{0,32},{32,0},{64,96},{96,64},{128,160},{160,128},{192,224},{224,1... | collective-permute-start | bytes 393224 | tf_op jit(solution)/shard_map/ppermute | solution.py:260
  24.6 1.0 %collective-permute-done.2.other_ref = bf16[2,128,256]{2,1,0:T(8,128)(2,1)S(1)} collective-permute-done((bf16[2,128,256]{2,1,0:T(8,128)(2,1)S(1)}, bf16[2,128,256]{2,1,0:T(8,128)(2,1)S(1)}, u32[]{:S(2)}, u32[]{:S(2)}) %collective-permute-start.2) | collective-permute-done | bytes 131104 | tf_op jit(solution)/shard_map/ppermute | solution.py:260
  25.6 0.7 %direct.1 = bf16[8,256,256]{2,1,0:T(8,128)(2,1)S(1)} custom-call(f32[2,128,256]{2,1,0:T(8,128)S(1)} %get-tuple-element.16.mine_ref, bf16[2,128,256]{2,1,0:T(8,128)(2,1)S(1)} %collective-permute-done.2.other_ref, bf16[2048,512]{1,0:T(8,128)(2,1)S(1)} %rows.1.density_ref), custom_call_target="tpu_custom_call" | custom-call | tf_op jit(solution)/shard_map/direct/pallas_call | solution.py:261
  26.3 18.8 %all_to_all.10.in_ref = bf16[8,256,256]{2,1,0:T(8,128)(2,1)S(1)} all-to-all(bf16[8,256,256]{2,1,0:T(8,128)(2,1)S(1)} %direct.1), channel_id=1, replica_groups={{0,64,128,192,448,384,320,256},{32,96,160,224,480,416,352,288},{1,65,12..., dimensions={0} | all-to-all | bytes 2097152 | tf_op jit(solution)/shard_map/all_to_all | solution.py:268
  45.1 0.8 %total.1 = f32[2,256,128]{2,1,0:T(8,128)} custom-call(bf16[8,256,256]{2,1,0:T(8,128)(2,1)S(1)} %all_to_all.10.in_ref), custom_call_target="tpu_custom_call" | custom-call | tf_op jit(solution)/shard_map/total/pallas_call | solution.py:269
Async XLA Ops:
  2.7 17.3 %all-to-all-start = ((bf16[8,128,256]{2,1,0:T(8,128)(2,1)}), bf16[8,128,256]{2,1,0:T(8,128)(2,1)S(1)}, u32[]{:S(2)}, u32[]{:S(2)}) async-start(bf16[8,128,256]{2,1,0:T(8,128)(2,1)} %get-tuple-element.12), calls=%async_computation | async-start | bytes 1048576 | tf_op jit(solution)/shard_map/all_to_all | solution.py:237
  8.6 8.4 %collective-permute-start = (bf16[1600,128]{1,0:T(8,128)(2,1)}, bf16[1600,128]{1,0:T(8,128)(2,1)S(1)}, u32[]{:S(2)}, u32[]{:S(2)}) collective-permute-start(bf16[1600,128]{1,0:T(8,128)(2,1)} %get-tuple-element.13.own_ref), channel_id=1, source_target_pairs={{0,32},{32,0},{64,96},{96,64},{128,160},{160,128},{192,224},{224,1... | collective-permute-start | bytes 1228808 | tf_op jit(solution)/shard_map/ppermute | solution.py:238
  15.0 5.0 %collective-permute-start.1 = (bf16[1408,128]{1,0:T(8,128)(2,1)}, bf16[1408,128]{1,0:T(8,128)(2,1)S(1)}, u32[]{:S(2)}, u32[]{:S(2)}) collective-permute-start(bf16[1408,128]{1,0:T(8,128)(2,1)} %get-tuple-element.15), channel_id=1, source_target_pairs={{0,32},{32,0},{64,96},{96,64},{128,160},{160,128},{192,224},{224,1... | collective-permute-start | bytes 1081352 | tf_op jit(solution)/shard_map/ppermute | solution.py:239
  17.0 1.0 %copy-start = (bf16[1600,128]{1,0:T(8,128)(2,1)S(1)}, bf16[1600,128]{1,0:T(8,128)(2,1)}, u32[]{:S(2)}) copy-start(bf16[1600,128]{1,0:T(8,128)(2,1)} %get-tuple-element.13.own_ref) | copy-start | bytes 1228804
  21.7 3.8 %collective-permute-start.2 = (bf16[2,128,256]{2,1,0:T(8,128)(2,1)S(1)}, bf16[2,128,256]{2,1,0:T(8,128)(2,1)S(1)}, u32[]{:S(2)}, u32[]{:S(2)}) collective-permute-start(bf16[2,128,256]{2,1,0:T(8,128)(2,1)S(1)} %get-tuple-element.17), channel_id=1, source_target_pairs={{0,32},{32,0},{64,96},{96,64},{128,160},{160,128},{192,224},{224,1... | collective-permute-start | bytes 393224 | tf_op jit(solution)/shard_map/ppermute | solution.py:260

commit v11 on v10

--- a/solution.py
+++ b/solution.py
@@ -12,7 +12,9 @@
 WIDTH = 128
 KPAD = 256
 RING = (0, 1, 2, 3, 7, 6, 5, 4)
-STRIPS = 16
+STRIPS = 8
+ROOM = 16384
+FAR = 512
 JOINED = 5
 MIB = 1024 * 1024
 LITTLE = pltpu.CompilerParams(vmem_limit_bytes=16 * MIB)
@@ -106,77 +108,85 @@
         copy.wait()
 
 
-def rows_kernel(own_ref, partner_ref, density_ref, table, at_ref):
-    core = core_of()
-
-    @pl.when(pl.program_id(0) == 0)
-    def _():
-        strips = at_ref.shape[1]
-        split = 2 * VAL * 4
-        bands = 2 * (VAL + CON) * 4
-        at_ref[0] = own_ref[bands : bands + strips, :].astype(jnp.float32)
-        at_ref[1] = own_ref[bands + strips : bands + 2 * strips, :].astype(jnp.float32)
-        both = jnp.concatenate([own_ref[0:bands, :], partner_ref[0:bands, :]], 1)
-        for parity in range(2):
-            lanes = pl.ds(parity * 2 * SLICE, 2 * SLICE)
-            table[0:KPAD, lanes] = pick(KPAD, parity, both[:split])
-            table[KPAD:, lanes] = pick(KPAD, parity, both[split:bands])
-
-    picked = []
-    for which in range(2):
-        index = []
-        for s in range(STRIPS):
-            strip = lane_matrix(at_ref[which, pl.ds(pl.program_id(0) * STRIPS + s, 1), :]).reshape(-1, 2, FINE, 128)
-            index.append(jnp.where(core == 0, strip[:, 0], strip[:, 1]).reshape(-1, 128))
-        hot = one_hot(jnp.concatenate(index, 0), KPAD)
-        picked.append(
-            jnp.dot(hot, table[which * KPAD : (which + 1) * KPAD, :], preferred_element_type=jnp.float32)
-        )
-    density_ref[...] = jnp.concatenate(densities(*picked), 1).astype(jnp.bfloat16)
-
-
-def screened_kernel(pairs_ref, own_ref, joined_ref, block_ref, out_ref, sent_ref, held, sems):
-    core = core_of()
+def own_blocks(w_ref, to_ref, sems):
     copies = []
     for place, chip in enumerate(RING):
-        lanes = pl.ds(pl.multiple_of((2 * chip + core) * SLICE, SLICE), SLICE)
-        to = held.at[:, :, place * SLICE : (place + 1) * SLICE]
-        copies.append(pltpu.make_async_copy(own_ref.at[:, :, lanes], to, sems.at[place]))
+        lanes = pl.ds(pl.multiple_of((2 * chip + core_of()) * SLICE, SLICE), SLICE)
+        to = to_ref.at[:, :, pl.ds(place * SLICE, SLICE)]
+        copies.append(pltpu.make_async_copy(w_ref.at[:, :, lanes], to, sems.at[place]))
+    return copies
+
+
+def rows_kernel(own_ref, partner_ref, w_ref, near_ref, far_ref, kept_ref, table, at_ref, held, sems, out_sems):
+    core = core_of()
+    copies = own_blocks(w_ref, kept_ref, sems)
     for copy in copies:
         copy.start()
+    strips = at_ref.shape[1]
+    split = 2 * VAL * 4
+    bands = 2 * (VAL + CON) * 4
+    at_ref[0] = own_ref[bands : bands + strips, :].astype(jnp.float32)
+    at_ref[1] = own_ref[bands + strips : bands + 2 * strips, :].astype(jnp.float32)
+    both = jnp.concatenate([own_ref[0:bands, :], partner_ref[0:bands, :]], 1)
+    for parity in range(2):
+        lanes = pl.ds(parity * 2 * SLICE, 2 * SLICE)
+        table[0:KPAD, lanes] = pick(KPAD, parity, both[:split])
+        table[KPAD:, lanes] = pick(KPAD, parity, both[split:bands])
+    rows = STRIPS * 64
+    stores = []
+    near = near_ref.shape[0] // rows
+    for m in range(held.shape[0]):
+        picked = []
+        for which in range(2):
+            index = []
+            for s in range(m * STRIPS, (m + 1) * STRIPS):
+                strip = lane_matrix(at_ref[which, s : s + 1, :]).reshape(-1, 2, FINE, 128)
+                index.append(jnp.where(core == 0, strip[:, 0], strip[:, 1]).reshape(-1, 128))
+            hot = one_hot(jnp.concatenate(index, 0), KPAD)
+            picked.append(
+                jnp.dot(hot, table[which * KPAD : (which + 1) * KPAD, :], preferred_element_type=jnp.float32)
+            )
+        held[m] = jnp.concatenate(densities(*picked), 1).astype(jnp.bfloat16)
+        ref, at = (near_ref, m) if m < near else (far_ref, m - near)
+        stores.append(pltpu.make_async_copy(held.at[m], ref.at[pl.ds(at * rows, rows), :], out_sems.at[m]))
+        stores[-1].start()
+    for copy in stores + copies:
+        copy.wait()
+
+
+def screened_kernel(pairs_ref, kept_ref, joined_ref, block_ref, far_ref, out_ref, sent_ref, back_ref, sem):
+    copy = pltpu.make_async_copy(far_ref.at[pl.ds(0, FAR), :], back_ref, sem)
+    copy.start()
     pairs = pairs_ref[...].reshape(-1, 2 * WIDTH)
     chips = len(RING)
     start = joined_ref.shape[0] - JOINED * SLICE
     blocks = [joined_ref[start + i * SLICE : start + (i + 1) * SLICE, :] for i in range(JOINED)]
     blocks += [block_ref[i * SLICE : (i + 1) * SLICE, :] for i in range(2 * chips - JOINED)]
-    for half in (1, 0):
-        if half == 0:
-            for copy in copies:
-                copy.wait()
+    for half in range(2):
         parts = []
         for part in range(2):
-            w = jnp.concatenate(blocks[part * chips : (part + 1) * chips], 1) if half else held[part]
+            w = jnp.concatenate(blocks[part * chips : (part + 1) * chips], 1) if half else kept_ref[part]
             parts.append(jnp.dot(w, pairs, preferred_element_type=jnp.float32))
         real = parts[0][:, :WIDTH] - parts[1][:, WIDTH:]
         imag = parts[0][:, WIDTH:] + parts[1][:, :WIDTH]
         both = jnp.concatenate([real, imag], 1)
         out_ref[half] = both
         sent_ref[half] = both.astype(jnp.bfloat16)
-
-
-def direct_kernel(mine_ref, other_ref, density_ref, out_ref, screened):
+    copy.wait()
+
+
+def direct_kernel(mine_ref, other_ref, near_ref, far_ref, out_ref, screened):
     for half in range(2):
         x = (mine_ref[half] + other_ref[1 - half].astype(jnp.float32)).astype(jnp.bfloat16)
         screened[half * SLICE : (half + 1) * SLICE, :] = x
         screened[(2 + half) * SLICE : (3 + half) * SLICE, :WIDTH] = x[:, WIDTH:]
         screened[(2 + half) * SLICE : (3 + half) * SLICE, WIDTH:] = -x[:, :WIDTH]
-    parts = 4
-    rows = density_ref.shape[0] // parts
+    rows = 512
     strips = rows // 64
-    for m in range(parts):
-        direct = jnp.dot(
-            density_ref[m * rows : (m + 1) * rows, :], screened[...], preferred_element_type=jnp.float32
-        )
+    near = near_ref.shape[0] // rows
+    for m in range(near + far_ref.shape[0] // rows):
+        ref, at = (near_ref, m * rows) if m < near else (far_ref, (m - near) * rows)
+        direct = jnp.dot(ref[at : at + rows, :], screened[...], preferred_element_type=jnp.float32)
         direct = direct.reshape(strips, -1, FINE, 2 * WIDTH)
         direct = jnp.concatenate([direct[s] for s in range(strips)], 1).astype(jnp.bfloat16)
         for place, chip in enumerate(RING):
@@ -237,26 +247,37 @@
     pairs = lax.all_to_all(pairs, "row", 0, 0, axis_index_groups=same_core, tiled=True)
     partner_tables = lax.ppermute(tables, "row", swap)
     blocks = lax.ppermute(blocks, "row", swap)
-    density = pl.pallas_call(
+    near = jax.ShapeDtypeStruct((strips * 64 - FAR, 4 * SLICE), bf16)
+    far = jax.ShapeDtypeStruct((ROOM, 4 * SLICE), bf16)
+    kept = jax.ShapeDtypeStruct((2, SLICE, chips * SLICE), bf16)
+    near, far, kept = pl.pallas_call(
         rows_kernel,
-        out_shape=jax.ShapeDtypeStruct((strips * 64, 4 * SLICE), bf16),
-        grid=(strips // STRIPS,),
-        in_specs=[whole(tables), whole(partner_tables)],
-        out_specs=pl.BlockSpec((STRIPS * 64, 4 * SLICE), lambda m: (m, 0)),
-        scratch_shapes=[pltpu.VMEM((2 * KPAD, 4 * SLICE), bf16), pltpu.VMEM((2, strips, 128), f32)],
-        compiler_params=LITTLE,
+        out_shape=(near, far, kept),
+        in_specs=[in_vmem, in_vmem, anywhere],
+        out_specs=(anywhere, anywhere, in_vmem),
+        scratch_shapes=[
+            pltpu.VMEM((2 * KPAD, 4 * SLICE), bf16),
+            pltpu.VMEM((2, strips, 128), f32),
+            pltpu.VMEM((strips // STRIPS, STRIPS * 64, 4 * SLICE), bf16),
+            dma((chips,)),
+            dma((strips // STRIPS,)),
+        ],
+        compiler_params=pltpu.CompilerParams(vmem_limit_bytes=52 * MIB),
         cost_estimate=pl.CostEstimate(flops=0, bytes_accessed=0, transcendentals=0),
         name="rows",
-    )(tables, partner_tables)
-    pairs, density = lax.optimization_barrier((pairs, density))
-    mine, other = pl.pallas_call(
+    )(tables, partner_tables, screened)
+    pairs, near = lax.optimization_barrier((pairs, near))
+    mine, other, back = pl.pallas_call(
         screened_kernel,
-        out_shape=tuple(jax.ShapeDtypeStruct((2, SLICE, 2 * WIDTH), kind) for kind in (f32, bf16)),
-        in_specs=[in_vmem, anywhere, in_vmem, in_vmem],
-        scratch_shapes=[pltpu.VMEM((2, SLICE, chips * SLICE), bf16), pltpu.SemaphoreType.DMA((chips,))],
-        compiler_params=MUCH,
+        out_shape=(
+            *[jax.ShapeDtypeStruct((2, SLICE, 2 * WIDTH), kind) for kind in (f32, bf16)],
+            jax.ShapeDtypeStruct((FAR, 4 * SLICE), bf16),
+        ),
+        in_specs=[in_vmem] * 4 + [anywhere],
+        scratch_shapes=[dma],
+        compiler_params=pltpu.CompilerParams(vmem_limit_bytes=46 * MIB),
         name="screened",
-    )(pairs, screened, partner_tables, blocks)
+    )(pairs, kept, partner_tables, blocks, far)
     other = lax.ppermute(other, "row", swap)
     partial = pl.pallas_call(
         direct_kernel,
@@ -264,7 +285,7 @@
         scratch_shapes=[pltpu.VMEM((4 * SLICE, 2 * WIDTH), bf16)],
         compiler_params=LITTLE,
         name="direct",
-    )(mine, other, density)
+    )(mine, other, near, back)
     partial = lax.all_to_all(partial, "row", 0, 0, axis_index_groups=same_core, tiled=True)
     out = pl.pallas_call(
         total_kernel,

time: 46.6 us -> 47.2 us (1.013)
  starting transfers between devices: 17.1 us -> 16.6 us
    pallas_call x2, Pallas kernels: 3.74 us -> 4.21 us  [the longest x1 3.04 us: shards(): pl.pallas_call(rows_kernel, out_shape=(near, far, kept), in_specs=[in_vme...]
    unnamed x2 -> x4, local copies, waits for them, and re-layouts: 0.99 us -> 1 us
  transfers between devices with their start and end apart: 4 -> 4, of which waited for: 1 -> 1; matrix products, arithmetic and copies ran while one was open for 0% -> 0% of each run, Pallas kernels for 5% -> 7%
where the time goes in v11:
time: 47.2 us; the launch traced here: 46.4 us
  blocking collectives  19.2 us (41%)
  starting transfers between devices  16.6 us (35%)
  Pallas kernels  8.46 us (18%)
  local copies, waits for them, and re-layouts  1 us (2%)
  waiting for transfers between devices  0.97 us (2%)
    all_to_all x1, blocking collectives, shards(): lax.all_to_all(partial, 'row', 0, 0, axis_index_groups=same_core, tiled=T...  19.2 us
    ppermute x1, starting transfers between devices, shards(): partner_tables = lax.ppermute(tables, 'row', swap)  6.43 us
    all_to_all x1, starting transfers between devices, shards(): lax.all_to_all(pairs, 'row', 0, 0, axis_index_groups=same_core, tiled=True)  5.87 us
    pallas_call x1, Pallas kernels, shards(): pl.pallas_call(rows_kernel, out_shape=(near, far, kept), in_specs=[in_vme...  3.04 us
    pallas_call x1, Pallas kernels, shards(): pl.pallas_call(columns_kernel, out_shape=(jax.ShapeDtypeStruct((bands + 2...  2.69 us
    ppermute x1, starting transfers between devices, shards(): other = lax.ppermute(other, 'row', swap)  2.41 us
    ppermute x1, starting transfers between devices, shards(): blocks = lax.ppermute(blocks, 'row', swap)  1.92 us
    pallas_call x1, Pallas kernels, shards(): pl.pallas_call(screened_kernel, out_shape=(*[jax.ShapeDtypeStruct((2, SLI...  1.17 us
  transfers between devices with their start and end apart: 4, of which 1 were waited for; matrix products, arithmetic and copies ran while one was open for 0% of the time, Pallas kernels for 7%

profile of v11, /device:TPU:1, one launch (start us, length us, event | category | flops | bytes accessed | tf_op | source)
XLA Modules:
  0.0 46.4 jit_solution(17642454600314703241)
XLA Ops:
  0.0 2.7 %columns.1 = (bf16[1600,128]{1,0:T(8,128)(2,1)}, bf16[8,128,256]{2,1,0:T(8,128)(2,1)}, bf16[1408,128]{1,0:T(8,128)(2,1)}) custom-call(bf16[384,128]{1,0:T(8,128)(2,1)} %bitcast.7, bf16[512,128]{1,0:T(8,128)(2,1)} %bitcast.6, s32[32,128]{1,0:T(8,128)} %bitcast.8, s32[32,128]{1,0:T(8,128)} %bitcast.9, s32[32,128]{1,0:T(8,128)} %bitcast.10, ...), custom_call_target="tpu_custom_call" | custom-call | tf_op jit(solution)/shard_map/columns/pallas_call | solution.py:224
  2.7 5.9 %all-to-all-start = ((bf16[8,128,256]{2,1,0:T(8,128)(2,1)}), bf16[8,128,256]{2,1,0:T(8,128)(2,1)S(1)}, u32[]{:S(2)}, u32[]{:S(2)}) async-start(bf16[8,128,256]{2,1,0:T(8,128)(2,1)} %get-tuple-element.16), calls=%async_computation | async-start | bytes 1048576 | tf_op jit(solution)/shard_map/all_to_all | solution.py:247
  8.6 6.4 %collective-permute-start = (bf16[1600,128]{1,0:T(8,128)(2,1)}, bf16[1600,128]{1,0:T(8,128)(2,1)S(1)}, u32[]{:S(2)}, u32[]{:S(2)}) collective-permute-start(bf16[1600,128]{1,0:T(8,128)(2,1)} %get-tuple-element.17.own_ref), channel_id=1, source_target_pairs={{0,32},{32,0},{64,96},{96,64},{128,160},{160,128},{192,224},{224,1... | collective-permute-start | bytes 1228808 | tf_op jit(solution)/shard_map/ppermute | solution.py:248
  15.0 1.9 %collective-permute-start.1 = (bf16[1408,128]{1,0:T(8,128)(2,1)}, bf16[1408,128]{1,0:T(8,128)(2,1)S(1)}, u32[]{:S(2)}, u32[]{:S(2)}) collective-permute-start(bf16[1408,128]{1,0:T(8,128)(2,1)} %get-tuple-element.21), channel_id=1, source_target_pairs={{0,32},{32,0},{64,96},{96,64},{128,160},{160,128},{192,224},{224,1... | collective-permute-start | bytes 1081352 | tf_op jit(solution)/shard_map/ppermute | solution.py:249
  16.9 0.0 collective-permute-done.partner_ref.joined_ref
  17.0 0.0 copy-start.1
  17.0 1.0 %copy-done.1 = bf16[1600,128]{1,0:T(8,128)(2,1)S(1)} copy-done((bf16[1600,128]{1,0:T(8,128)(2,1)S(1)}, bf16[1600,128]{1,0:T(8,128)(2,1)}, u32[]{:S(2)}) %copy-start.1) | copy-done | bytes 409624
  18.0 3.0 %rows.1 = (bf16[1536,512]{1,0:T(8,128)(2,1)}, bf16[16384,512]{1,0:T(8,128)(2,1)}, bf16[2,128,1024]{2,1,0:T(8,128)(2,1)S(1)}) custom-call(bf16[1600,128]{1,0:T(8,128)(2,1)S(1)} %copy-done.1, bf16[1600,128]{1,0:T(8,128)(2,1)S(1)} %collective-permute-done.partner_ref.joined_ref, bf16[2,128,2048]{2,1,0:T(8,128)(2,1)} %w_ref.3), custom_call_target="tpu_custom_call" | custom-call | tf_op jit(solution)/shard_map/rows/pallas_call | solution.py:253
  21.0 0.0 copy-start
  21.0 0.0 all-to-all-done.pairs_ref
  21.0 0.0 collective-permute-done.1.block_ref
  21.0 1.2 %screened.1 = (f32[2,128,256]{2,1,0:T(8,128)S(1)}, bf16[2,128,256]{2,1,0:T(8,128)(2,1)S(1)}, bf16[512,512]{1,0:T(8,128)(2,1)S(1)}) custom-call(bf16[8,128,256]{2,1,0:T(8,128)(2,1)S(1)} %all-to-all-done.pairs_ref, bf16[2,128,1024]{2,1,0:T(8,128)(2,1)S(1)} %get-tuple-element.20.kept_ref, bf16[1600,128]{1,0:T(8,128)(2,1)S(1)} %collective-permute-done.partner_ref.joined_ref, ...), custom_call_target="tpu_custom_call" | custom-call | tf_op jit(solution)/shard_map/screened/pallas_call | solution.py:270
  22.2 2.4 %collective-permute-start.2 = (bf16[2,128,256]{2,1,0:T(8,128)(2,1)S(1)}, bf16[2,128,256]{2,1,0:T(8,128)(2,1)S(1)}, u32[]{:S(2)}, u32[]{:S(2)}) collective-permute-start(bf16[2,128,256]{2,1,0:T(8,128)(2,1)S(1)} %get-tuple-element.24), channel_id=1, source_target_pairs={{0,32},{32,0},{64,96},{96,64},{128,160},{160,128},{192,224},{224,1... | collective-permute-start | bytes 393224 | tf_op jit(solution)/shard_map/ppermute | solution.py:281
  24.6 1.0 %collective-permute-done.2.other_ref = bf16[2,128,256]{2,1,0:T(8,128)(2,1)S(1)} collective-permute-done((bf16[2,128,256]{2,1,0:T(8,128)(2,1)S(1)}, bf16[2,128,256]{2,1,0:T(8,128)(2,1)S(1)}, u32[]{:S(2)}, u32[]{:S(2)}) %collective-permute-start.2) | collective-permute-done | bytes 131104 | tf_op jit(solution)/shard_map/ppermute | solution.py:281
  25.6 0.0 copy-done
  25.6 0.7 %direct.1 = bf16[8,256,256]{2,1,0:T(8,128)(2,1)S(1)} custom-call(f32[2,128,256]{2,1,0:T(8,128)S(1)} %get-tuple-element.23.mine_ref, bf16[2,128,256]{2,1,0:T(8,128)(2,1)S(1)} %collective-permute-done.2.other_ref, bf16[1536,512]{1,0:T(8,128)(2,1)S(1)} %copy-done, bf16[512,512]{1,0:T(8,128)(2,1)S(1)} %get-tuple-element.26.far_ref), custom_call_target="tpu_custom_call" | custom-call | tf_op jit(solution)/shard_map/direct/pallas_call | solution.py:282
  26.3 19.2 %all_to_all.10.in_ref = bf16[8,256,256]{2,1,0:T(8,128)(2,1)S(1)} all-to-all(bf16[8,256,256]{2,1,0:T(8,128)(2,1)S(1)} %direct.1), channel_id=1, replica_groups={{0,64,128,192,448,384,320,256},{32,96,160,224,480,416,352,288},{1,65,12..., dimensions={0} | all-to-all | bytes 2097152 | tf_op jit(solution)/shard_map/all_to_all | solution.py:289
  45.5 0.8 %total.1 = f32[2,256,128]{2,1,0:T(8,128)} custom-call(bf16[8,256,256]{2,1,0:T(8,128)(2,1)S(1)} %all_to_all.10.in_ref), custom_call_target="tpu_custom_call" | custom-call | tf_op jit(solution)/shard_map/total/pallas_call | solution.py:290
Async XLA Ops:
  2.7 18.3 %all-to-all-start = ((bf16[8,128,256]{2,1,0:T(8,128)(2,1)}), bf16[8,128,256]{2,1,0:T(8,128)(2,1)S(1)}, u32[]{:S(2)}, u32[]{:S(2)}) async-start(bf16[8,128,256]{2,1,0:T(8,128)(2,1)} %get-tuple-element.16), calls=%async_computation | async-start | bytes 1048576 | tf_op jit(solution)/shard_map/all_to_all | solution.py:247
  8.6 8.4 %collective-permute-start = (bf16[1600,128]{1,0:T(8,128)(2,1)}, bf16[1600,128]{1,0:T(8,128)(2,1)S(1)}, u32[]{:S(2)}, u32[]{:S(2)}) collective-permute-start(bf16[1600,128]{1,0:T(8,128)(2,1)} %get-tuple-element.17.own_ref), channel_id=1, source_target_pairs={{0,32},{32,0},{64,96},{96,64},{128,160},{160,128},{192,224},{224,1... | collective-permute-start | bytes 1228808 | tf_op jit(solution)/shard_map/ppermute | solution.py:248
  15.0 6.0 %collective-permute-start.1 = (bf16[1408,128]{1,0:T(8,128)(2,1)}, bf16[1408,128]{1,0:T(8,128)(2,1)S(1)}, u32[]{:S(2)}, u32[]{:S(2)}) collective-permute-start(bf16[1408,128]{1,0:T(8,128)(2,1)} %get-tuple-element.21), channel_id=1, source_target_pairs={{0,32},{32,0},{64,96},{96,64},{128,160},{160,128},{192,224},{224,1... | collective-permute-start | bytes 1081352 | tf_op jit(solution)/shard_map/ppermute | solution.py:249
  17.0 1.0 %copy-start.1 = (bf16[1600,128]{1,0:T(8,128)(2,1)S(1)}, bf16[1600,128]{1,0:T(8,128)(2,1)}, u32[]{:S(2)}) copy-start(bf16[1600,128]{1,0:T(8,128)(2,1)} %get-tuple-element.17.own_ref) | copy-start | bytes 1228804
  21.0 4.6 %copy-start = (bf16[1536,512]{1,0:T(8,128)(2,1)S(1)}, bf16[1536,512]{1,0:T(8,128)(2,1)}, u32[]{:S(2)}) copy-start(bf16[1536,512]{1,0:T(8,128)(2,1)} %get-tuple-element.25.near_ref) | copy-start | bytes 4718596
  22.2 3.4 %collective-permute-start.2 = (bf16[2,128,256]{2,1,0:T(8,128)(2,1)S(1)}, bf16[2,128,256]{2,1,0:T(8,128)(2,1)S(1)}, u32[]{:S(2)}, u32[]{:S(2)}) collective-permute-start(bf16[2,128,256]{2,1,0:T(8,128)(2,1)S(1)} %get-tuple-element.24), channel_id=1, source_target_pairs={{0,32},{32,0},{64,96},{96,64},{128,160},{160,128},{192,224},{224,1... | collective-permute-start | bytes 393224 | tf_op jit(solution)/shard_map/ppermute | solution.py:281

commit v12 on v10

--- a/solution.py
+++ b/solution.py
@@ -11,7 +11,7 @@
 SLICE = 128
 WIDTH = 128
 KPAD = 256
-RING = (0, 1, 2, 3, 7, 6, 5, 4)
+RING = (0, 4, 1, 5, 2, 6, 3, 7)
 STRIPS = 16
 JOINED = 5
 MIB = 1024 * 1024

time: 46.6 us -> 46.6 us (level)
  no operation moved by 1% of the time
where the time goes in v12:
time: 46.6 us; the launch traced here: 46.1 us
  blocking collectives  18.8 us (40%)
  starting transfers between devices  17.3 us (37%)
  Pallas kernels  8 us (17%)
  local copies, waits for them, and re-layouts  0.99 us (2%)
  waiting for transfers between devices  0.97 us (2%)
    all_to_all x1, blocking collectives, shards(): lax.all_to_all(partial, 'row', 0, 0, axis_index_groups=same_core, tiled=T...  18.8 us
    ppermute x1, starting transfers between devices, shards(): partner_tables = lax.ppermute(tables, 'row', swap)  6.42 us
    all_to_all x1, starting transfers between devices, shards(): lax.all_to_all(pairs, 'row', 0, 0, axis_index_groups=same_core, tiled=True)  5.88 us
    ppermute x1, starting transfers between devices, shards(): other = lax.ppermute(other, 'row', swap)  3.04 us
    pallas_call x1, Pallas kernels, shards(): pl.pallas_call(columns_kernel, out_shape=(jax.ShapeDtypeStruct((bands + 2...  2.71 us
    pallas_call x1, Pallas kernels, shards(): pl.pallas_call(rows_kernel, out_shape=jax.ShapeDtypeStruct((strips * 64,...  2.08 us
    ppermute x1, starting transfers between devices, shards(): blocks = lax.ppermute(blocks, 'row', swap)  1.92 us
    pallas_call x1, Pallas kernels, shards(): pl.pallas_call(screened_kernel, out_shape=tuple((jax.ShapeDtypeStruct((2,...  1.65 us
  transfers between devices with their start and end apart: 4, of which 1 were waited for; matrix products, arithmetic and copies ran while one was open for 0% of the time, Pallas kernels for 5%

profile of v12, /device:TPU:1, one launch (start us, length us, event | category | flops | bytes accessed | tf_op | source)
XLA Modules:
  0.0 46.1 jit_solution(10055632287562631447)
XLA Ops:
  0.0 2.7 %columns.1 = (bf16[1600,128]{1,0:T(8,128)(2,1)}, bf16[8,128,256]{2,1,0:T(8,128)(2,1)}, bf16[1408,128]{1,0:T(8,128)(2,1)}) custom-call(bf16[384,128]{1,0:T(8,128)(2,1)} %bitcast.7, bf16[512,128]{1,0:T(8,128)(2,1)} %bitcast.6, s32[32,128]{1,0:T(8,128)} %bitcast.8, s32[32,128]{1,0:T(8,128)} %bitcast.9, s32[32,128]{1,0:T(8,128)} %bitcast.10, ...), custom_call_target="tpu_custom_call" | custom-call | tf_op jit(solution)/shard_map/columns/pallas_call | solution.py:214
  2.7 5.9 %all-to-all-start = ((bf16[8,128,256]{2,1,0:T(8,128)(2,1)}), bf16[8,128,256]{2,1,0:T(8,128)(2,1)S(1)}, u32[]{:S(2)}, u32[]{:S(2)}) async-start(bf16[8,128,256]{2,1,0:T(8,128)(2,1)} %get-tuple-element.12), calls=%async_computation | async-start | bytes 1048576 | tf_op jit(solution)/shard_map/all_to_all | solution.py:237
  8.6 6.4 %collective-permute-start = (bf16[1600,128]{1,0:T(8,128)(2,1)}, bf16[1600,128]{1,0:T(8,128)(2,1)S(1)}, u32[]{:S(2)}, u32[]{:S(2)}) collective-permute-start(bf16[1600,128]{1,0:T(8,128)(2,1)} %get-tuple-element.13.own_ref), channel_id=1, source_target_pairs={{0,32},{32,0},{64,96},{96,64},{128,160},{160,128},{192,224},{224,1... | collective-permute-start | bytes 1228808 | tf_op jit(solution)/shard_map/ppermute | solution.py:238
  15.0 1.9 %collective-permute-start.1 = (bf16[1408,128]{1,0:T(8,128)(2,1)}, bf16[1408,128]{1,0:T(8,128)(2,1)S(1)}, u32[]{:S(2)}, u32[]{:S(2)}) collective-permute-start(bf16[1408,128]{1,0:T(8,128)(2,1)} %get-tuple-element.15), channel_id=1, source_target_pairs={{0,32},{32,0},{64,96},{96,64},{128,160},{160,128},{192,224},{224,1... | collective-permute-start | bytes 1081352 | tf_op jit(solution)/shard_map/ppermute | solution.py:239
  17.0 0.0 collective-permute-done.partner_ref.joined_ref
  17.0 0.0 copy-start
  17.0 1.0 %copy-done = bf16[1600,128]{1,0:T(8,128)(2,1)S(1)} copy-done((bf16[1600,128]{1,0:T(8,128)(2,1)S(1)}, bf16[1600,128]{1,0:T(8,128)(2,1)}, u32[]{:S(2)}) %copy-start) | copy-done | bytes 409624
  18.0 2.1 %rows.1.density_ref = bf16[2048,512]{1,0:T(8,128)(2,1)S(1)} custom-call(bf16[1600,128]{1,0:T(8,128)(2,1)S(1)} %copy-done, bf16[1600,128]{1,0:T(8,128)(2,1)S(1)} %collective-permute-done.partner_ref.joined_ref), custom_call_target="tpu_custom_call" | custom-call | tf_op jit(solution)/shard_map/rows/pallas_call | solution.py:240
  20.1 0.0 all-to-all-done.pairs_ref
  20.1 0.0 collective-permute-done.1.block_ref
  20.1 1.7 %screened.1 = (f32[2,128,256]{2,1,0:T(8,128)S(1)}, bf16[2,128,256]{2,1,0:T(8,128)(2,1)S(1)}) custom-call(bf16[8,128,256]{2,1,0:T(8,128)(2,1)S(1)} %all-to-all-done.pairs_ref, bf16[2,128,2048]{2,1,0:T(8,128)(2,1)} %own_ref.1, bf16[1600,128]{1,0:T(8,128)(2,1)S(1)} %collective-permute-done.partner_ref.joined_ref, ...), custom_call_target="tpu_custom_call" | custom-call | tf_op jit(solution)/shard_map/screened/pallas_call | solution.py:252
  21.7 3.0 %collective-permute-start.2 = (bf16[2,128,256]{2,1,0:T(8,128)(2,1)S(1)}, bf16[2,128,256]{2,1,0:T(8,128)(2,1)S(1)}, u32[]{:S(2)}, u32[]{:S(2)}) collective-permute-start(bf16[2,128,256]{2,1,0:T(8,128)(2,1)S(1)} %get-tuple-element.17), channel_id=1, source_target_pairs={{0,32},{32,0},{64,96},{96,64},{128,160},{160,128},{192,224},{224,1... | collective-permute-start | bytes 393224 | tf_op jit(solution)/shard_map/ppermute | solution.py:260
  24.8 1.0 %collective-permute-done.2.other_ref = bf16[2,128,256]{2,1,0:T(8,128)(2,1)S(1)} collective-permute-done((bf16[2,128,256]{2,1,0:T(8,128)(2,1)S(1)}, bf16[2,128,256]{2,1,0:T(8,128)(2,1)S(1)}, u32[]{:S(2)}, u32[]{:S(2)}) %collective-permute-start.2) | collective-permute-done | bytes 131104 | tf_op jit(solution)/shard_map/ppermute | solution.py:260
  25.7 0.7 %direct.1 = bf16[8,256,256]{2,1,0:T(8,128)(2,1)S(1)} custom-call(f32[2,128,256]{2,1,0:T(8,128)S(1)} %get-tuple-element.16.mine_ref, bf16[2,128,256]{2,1,0:T(8,128)(2,1)S(1)} %collective-permute-done.2.other_ref, bf16[2048,512]{1,0:T(8,128)(2,1)S(1)} %rows.1.density_ref), custom_call_target="tpu_custom_call" | custom-call | tf_op jit(solution)/shard_map/direct/pallas_call | solution.py:261
  26.5 18.8 %all_to_all.10.in_ref = bf16[8,256,256]{2,1,0:T(8,128)(2,1)S(1)} all-to-all(bf16[8,256,256]{2,1,0:T(8,128)(2,1)S(1)} %direct.1), channel_id=1, replica_groups={{0,256,64,320,128,384,192,448},{32,288,96,352,160,416,224,480},{1,257,6..., dimensions={0} | all-to-all | bytes 2097152 | tf_op jit(solution)/shard_map/all_to_all | solution.py:268
  45.2 0.8 %total.1 = f32[2,256,128]{2,1,0:T(8,128)} custom-call(bf16[8,256,256]{2,1,0:T(8,128)(2,1)S(1)} %all_to_all.10.in_ref), custom_call_target="tpu_custom_call" | custom-call | tf_op jit(solution)/shard_map/total/pallas_call | solution.py:269
Async XLA Ops:
  2.7 17.3 %all-to-all-start = ((bf16[8,128,256]{2,1,0:T(8,128)(2,1)}), bf16[8,128,256]{2,1,0:T(8,128)(2,1)S(1)}, u32[]{:S(2)}, u32[]{:S(2)}) async-start(bf16[8,128,256]{2,1,0:T(8,128)(2,1)} %get-tuple-element.12), calls=%async_computation | async-start | bytes 1048576 | tf_op jit(solution)/shard_map/all_to_all | solution.py:237
  8.6 8.4 %collective-permute-start = (bf16[1600,128]{1,0:T(8,128)(2,1)}, bf16[1600,128]{1,0:T(8,128)(2,1)S(1)}, u32[]{:S(2)}, u32[]{:S(2)}) collective-permute-start(bf16[1600,128]{1,0:T(8,128)(2,1)} %get-tuple-element.13.own_ref), channel_id=1, source_target_pairs={{0,32},{32,0},{64,96},{96,64},{128,160},{160,128},{192,224},{224,1... | collective-permute-start | bytes 1228808 | tf_op jit(solution)/shard_map/ppermute | solution.py:238
  15.0 5.0 %collective-permute-start.1 = (bf16[1408,128]{1,0:T(8,128)(2,1)}, bf16[1408,128]{1,0:T(8,128)(2,1)S(1)}, u32[]{:S(2)}, u32[]{:S(2)}) collective-permute-start(bf16[1408,128]{1,0:T(8,128)(2,1)} %get-tuple-element.15), channel_id=1, source_target_pairs={{0,32},{32,0},{64,96},{96,64},{128,160},{160,128},{192,224},{224,1... | collective-permute-start | bytes 1081352 | tf_op jit(solution)/shard_map/ppermute | solution.py:239
  17.0 1.0 %copy-start = (bf16[1600,128]{1,0:T(8,128)(2,1)S(1)}, bf16[1600,128]{1,0:T(8,128)(2,1)}, u32[]{:S(2)}) copy-start(bf16[1600,128]{1,0:T(8,128)(2,1)} %get-tuple-element.13.own_ref) | copy-start | bytes 1228804
  21.7 4.0 %collective-permute-start.2 = (bf16[2,128,256]{2,1,0:T(8,128)(2,1)S(1)}, bf16[2,128,256]{2,1,0:T(8,128)(2,1)S(1)}, u32[]{:S(2)}, u32[]{:S(2)}) collective-permute-start(bf16[2,128,256]{2,1,0:T(8,128)(2,1)S(1)} %get-tuple-element.17), channel_id=1, source_target_pairs={{0,32},{32,0},{64,96},{96,64},{128,160},{160,128},{192,224},{224,1... | collective-permute-start | bytes 393224 | tf_op jit(solution)/shard_map/ppermute | solution.py:260

commit v13 on v12

--- a/solution.py
+++ b/solution.py
@@ -12,7 +12,7 @@
 WIDTH = 128
 KPAD = 256
 RING = (0, 4, 1, 5, 2, 6, 3, 7)
-STRIPS = 16
+STRIPS = 32
 JOINED = 5
 MIB = 1024 * 1024
 LITTLE = pltpu.CompilerParams(vmem_limit_bytes=16 * MIB)
@@ -41,11 +41,19 @@
     return v_re * c_re + v_im * c_im, v_re * c_im - v_im * c_re
 
 
-def pick(rows, parity, table):
-    i = lax.broadcasted_iota(jnp.int32, (rows, table.shape[0]), 0)
-    j = lax.broadcasted_iota(jnp.int32, (rows, table.shape[0]), 1)
+def pick(parity, table):
+    i = lax.broadcasted_iota(jnp.int32, (128, 256), 0)
+    j = lax.broadcasted_iota(jnp.int32, (128, 256), 1)
     mask = jnp.where(j == 2 * i + parity, 1.0, 0.0).astype(jnp.bfloat16)
-    return jnp.dot(mask, table, preferred_element_type=jnp.float32).astype(jnp.bfloat16)
+    parts = []
+    for start in range(0, table.shape[0], 256):
+        count = min(256, table.shape[0] - start)
+        part = table[start : start + count]
+        parts.append(jnp.dot(mask[: count // 2, :count], part, preferred_element_type=jnp.float32))
+    missing = KPAD - table.shape[0] // 2
+    if missing:
+        parts.append(jnp.zeros((missing, table.shape[1]), jnp.float32))
+    return jnp.concatenate(parts, 0).astype(jnp.bfloat16)
 
 
 def columns_kernel(
@@ -119,8 +127,8 @@
         both = jnp.concatenate([own_ref[0:bands, :], partner_ref[0:bands, :]], 1)
         for parity in range(2):
             lanes = pl.ds(parity * 2 * SLICE, 2 * SLICE)
-            table[0:KPAD, lanes] = pick(KPAD, parity, both[:split])
-            table[KPAD:, lanes] = pick(KPAD, parity, both[split:bands])
+            table[0:KPAD, lanes] = pick(parity, both[:split])
+            table[KPAD:, lanes] = pick(parity, both[split:bands])
 
     picked = []
     for which in range(2):

time: 46.6 us -> 46.2 us (level)
  blocking collectives: 18.8 us -> 18.3 us
  transfers between devices with their start and end apart: 4 -> 4, of which waited for: 1 -> 1; matrix products, arithmetic and copies ran while one was open for 0% -> 0% of each run, Pallas kernels for 5% -> 4%
where the time goes in v13:
time: 46.2 us; the launch traced here: 45.6 us
  blocking collectives  18.3 us (40%)
  starting transfers between devices  17.7 us (38%)
  Pallas kernels  7.57 us (16%)
  local copies, waits for them, and re-layouts  0.99 us (2%)
  waiting for transfers between devices  0.97 us (2%)
    all_to_all x1, blocking collectives, shards(): lax.all_to_all(partial, 'row', 0, 0, axis_index_groups=same_core, tiled=T...  18.3 us
    ppermute x1, starting transfers between devices, shards(): partner_tables = lax.ppermute(tables, 'row', swap)  6.42 us
    all_to_all x1, starting transfers between devices, shards(): lax.all_to_all(pairs, 'row', 0, 0, axis_index_groups=same_core, tiled=True)  5.88 us
    ppermute x1, starting transfers between devices, shards(): other = lax.ppermute(other, 'row', swap)  3.47 us
    pallas_call x1, Pallas kernels, shards(): pl.pallas_call(columns_kernel, out_shape=(jax.ShapeDtypeStruct((bands + 2...  2.71 us
    ppermute x1, starting transfers between devices, shards(): blocks = lax.ppermute(blocks, 'row', swap)  1.92 us
    pallas_call x1, Pallas kernels, shards(): pl.pallas_call(screened_kernel, out_shape=tuple((jax.ShapeDtypeStruct((2,...  1.66 us
    pallas_call x1, Pallas kernels, shards(): pl.pallas_call(rows_kernel, out_shape=jax.ShapeDtypeStruct((strips * 64,...  1.65 us
  transfers between devices with their start and end apart: 4, of which 1 were waited for; matrix products, arithmetic and copies ran while one was open for 0% of the time, Pallas kernels for 4%

profile of v13, /device:TPU:1, one launch (start us, length us, event | category | flops | bytes accessed | tf_op | source)
XLA Modules:
  0.0 45.6 jit_solution(15195451451450755021)
XLA Ops:
  0.0 2.7 %columns.1 = (bf16[1600,128]{1,0:T(8,128)(2,1)}, bf16[8,128,256]{2,1,0:T(8,128)(2,1)}, bf16[1408,128]{1,0:T(8,128)(2,1)}) custom-call(bf16[384,128]{1,0:T(8,128)(2,1)} %bitcast.7, bf16[512,128]{1,0:T(8,128)(2,1)} %bitcast.6, s32[32,128]{1,0:T(8,128)} %bitcast.8, s32[32,128]{1,0:T(8,128)} %bitcast.9, s32[32,128]{1,0:T(8,128)} %bitcast.10, ...), custom_call_target="tpu_custom_call" | custom-call | tf_op jit(solution)/shard_map/columns/pallas_call | solution.py:222
  2.7 5.9 %all-to-all-start = ((bf16[8,128,256]{2,1,0:T(8,128)(2,1)}), bf16[8,128,256]{2,1,0:T(8,128)(2,1)S(1)}, u32[]{:S(2)}, u32[]{:S(2)}) async-start(bf16[8,128,256]{2,1,0:T(8,128)(2,1)} %get-tuple-element.12), calls=%async_computation | async-start | bytes 1048576 | tf_op jit(solution)/shard_map/all_to_all | solution.py:245
  8.6 6.4 %collective-permute-start = (bf16[1600,128]{1,0:T(8,128)(2,1)}, bf16[1600,128]{1,0:T(8,128)(2,1)S(1)}, u32[]{:S(2)}, u32[]{:S(2)}) collective-permute-start(bf16[1600,128]{1,0:T(8,128)(2,1)} %get-tuple-element.13.own_ref), channel_id=1, source_target_pairs={{0,32},{32,0},{64,96},{96,64},{128,160},{160,128},{192,224},{224,1... | collective-permute-start | bytes 1228808 | tf_op jit(solution)/shard_map/ppermute | solution.py:246
  15.0 1.9 %collective-permute-start.1 = (bf16[1408,128]{1,0:T(8,128)(2,1)}, bf16[1408,128]{1,0:T(8,128)(2,1)S(1)}, u32[]{:S(2)}, u32[]{:S(2)}) collective-permute-start(bf16[1408,128]{1,0:T(8,128)(2,1)} %get-tuple-element.15), channel_id=1, source_target_pairs={{0,32},{32,0},{64,96},{96,64},{128,160},{160,128},{192,224},{224,1... | collective-permute-start | bytes 1081352 | tf_op jit(solution)/shard_map/ppermute | solution.py:247
  17.0 0.0 collective-permute-done.partner_ref.joined_ref
  17.0 0.0 copy-start
  17.0 1.0 %copy-done = bf16[1600,128]{1,0:T(8,128)(2,1)S(1)} copy-done((bf16[1600,128]{1,0:T(8,128)(2,1)S(1)}, bf16[1600,128]{1,0:T(8,128)(2,1)}, u32[]{:S(2)}) %copy-start) | copy-done | bytes 409624
  18.0 1.6 %rows.1.density_ref = bf16[2048,512]{1,0:T(8,128)(2,1)S(1)} custom-call(bf16[1600,128]{1,0:T(8,128)(2,1)S(1)} %copy-done, bf16[1600,128]{1,0:T(8,128)(2,1)S(1)} %collective-permute-done.partner_ref.joined_ref), custom_call_target="tpu_custom_call" | custom-call | tf_op jit(solution)/shard_map/rows/pallas_call | solution.py:248
  19.6 0.0 all-to-all-done.pairs_ref
  19.6 0.0 collective-permute-done.1.block_ref
  19.6 1.7 %screened.1 = (f32[2,128,256]{2,1,0:T(8,128)S(1)}, bf16[2,128,256]{2,1,0:T(8,128)(2,1)S(1)}) custom-call(bf16[8,128,256]{2,1,0:T(8,128)(2,1)S(1)} %all-to-all-done.pairs_ref, bf16[2,128,2048]{2,1,0:T(8,128)(2,1)} %own_ref.1, bf16[1600,128]{1,0:T(8,128)(2,1)S(1)} %collective-permute-done.partner_ref.joined_ref, ...), custom_call_target="tpu_custom_call" | custom-call | tf_op jit(solution)/shard_map/screened/pallas_call | solution.py:260
  21.3 3.5 %collective-permute-start.2 = (bf16[2,128,256]{2,1,0:T(8,128)(2,1)S(1)}, bf16[2,128,256]{2,1,0:T(8,128)(2,1)S(1)}, u32[]{:S(2)}, u32[]{:S(2)}) collective-permute-start(bf16[2,128,256]{2,1,0:T(8,128)(2,1)S(1)} %get-tuple-element.17), channel_id=1, source_target_pairs={{0,32},{32,0},{64,96},{96,64},{128,160},{160,128},{192,224},{224,1... | collective-permute-start | bytes 393224 | tf_op jit(solution)/shard_map/ppermute | solution.py:268
  24.8 1.0 %collective-permute-done.2.other_ref = bf16[2,128,256]{2,1,0:T(8,128)(2,1)S(1)} collective-permute-done((bf16[2,128,256]{2,1,0:T(8,128)(2,1)S(1)}, bf16[2,128,256]{2,1,0:T(8,128)(2,1)S(1)}, u32[]{:S(2)}, u32[]{:S(2)}) %collective-permute-start.2) | collective-permute-done | bytes 131104 | tf_op jit(solution)/shard_map/ppermute | solution.py:268
  25.7 0.7 %direct.1 = bf16[8,256,256]{2,1,0:T(8,128)(2,1)S(1)} custom-call(f32[2,128,256]{2,1,0:T(8,128)S(1)} %get-tuple-element.16.mine_ref, bf16[2,128,256]{2,1,0:T(8,128)(2,1)S(1)} %collective-permute-done.2.other_ref, bf16[2048,512]{1,0:T(8,128)(2,1)S(1)} %rows.1.density_ref), custom_call_target="tpu_custom_call" | custom-call | tf_op jit(solution)/shard_map/direct/pallas_call | solution.py:269
  26.5 18.3 %all_to_all.10.in_ref = bf16[8,256,256]{2,1,0:T(8,128)(2,1)S(1)} all-to-all(bf16[8,256,256]{2,1,0:T(8,128)(2,1)S(1)} %direct.1), channel_id=1, replica_groups={{0,256,64,320,128,384,192,448},{32,288,96,352,160,416,224,480},{1,257,6..., dimensions={0} | all-to-all | bytes 2097152 | tf_op jit(solution)/shard_map/all_to_all | solution.py:276
  44.8 0.8 %total.1 = f32[2,256,128]{2,1,0:T(8,128)} custom-call(bf16[8,256,256]{2,1,0:T(8,128)(2,1)S(1)} %all_to_all.10.in_ref), custom_call_target="tpu_custom_call" | custom-call | tf_op jit(solution)/shard_map/total/pallas_call | solution.py:277
Async XLA Ops:
  2.7 16.9 %all-to-all-start = ((bf16[8,128,256]{2,1,0:T(8,128)(2,1)}), bf16[8,128,256]{2,1,0:T(8,128)(2,1)S(1)}, u32[]{:S(2)}, u32[]{:S(2)}) async-start(bf16[8,128,256]{2,1,0:T(8,128)(2,1)} %get-tuple-element.12), calls=%async_computation | async-start | bytes 1048576 | tf_op jit(solution)/shard_map/all_to_all | solution.py:245
  8.6 8.4 %collective-permute-start = (bf16[1600,128]{1,0:T(8,128)(2,1)}, bf16[1600,128]{1,0:T(8,128)(2,1)S(1)}, u32[]{:S(2)}, u32[]{:S(2)}) collective-permute-start(bf16[1600,128]{1,0:T(8,128)(2,1)} %get-tuple-element.13.own_ref), channel_id=1, source_target_pairs={{0,32},{32,0},{64,96},{96,64},{128,160},{160,128},{192,224},{224,1... | collective-permute-start | bytes 1228808 | tf_op jit(solution)/shard_map/ppermute | solution.py:246
  15.0 4.6 %collective-permute-start.1 = (bf16[1408,128]{1,0:T(8,128)(2,1)}, bf16[1408,128]{1,0:T(8,128)(2,1)S(1)}, u32[]{:S(2)}, u32[]{:S(2)}) collective-permute-start(bf16[1408,128]{1,0:T(8,128)(2,1)} %get-tuple-element.15), channel_id=1, source_target_pairs={{0,32},{32,0},{64,96},{96,64},{128,160},{160,128},{192,224},{224,1... | collective-permute-start | bytes 1081352 | tf_op jit(solution)/shard_map/ppermute | solution.py:247
  17.0 1.0 %copy-start = (bf16[1600,128]{1,0:T(8,128)(2,1)S(1)}, bf16[1600,128]{1,0:T(8,128)(2,1)}, u32[]{:S(2)}) copy-start(bf16[1600,128]{1,0:T(8,128)(2,1)} %get-tuple-element.13.own_ref) | copy-start | bytes 1228804
  21.3 4.4 %collective-permute-start.2 = (bf16[2,128,256]{2,1,0:T(8,128)(2,1)S(1)}, bf16[2,128,256]{2,1,0:T(8,128)(2,1)S(1)}, u32[]{:S(2)}, u32[]{:S(2)}) collective-permute-start(bf16[2,128,256]{2,1,0:T(8,128)(2,1)S(1)} %get-tuple-element.17), channel_id=1, source_target_pairs={{0,32},{32,0},{64,96},{96,64},{128,160},{160,128},{192,224},{224,1... | collective-permute-start | bytes 393224 | tf_op jit(solution)/shard_map/ppermute | solution.py:268

commit v14 on v13

--- a/solution.py
+++ b/solution.py
@@ -14,6 +14,7 @@
 RING = (0, 4, 1, 5, 2, 6, 3, 7)
 STRIPS = 32
 JOINED = 5
+ROOM = 65536
 MIB = 1024 * 1024
 LITTLE = pltpu.CompilerParams(vmem_limit_bytes=16 * MIB)
 MUCH = pltpu.CompilerParams(vmem_limit_bytes=52 * MIB)
@@ -58,7 +59,7 @@
 
 def columns_kernel(
     valence_ref, conduction_ref, v_ref, n_ref, k_ref, w_ref,
-    table_ref, out_ref, block_ref,
+    table_ref, out_ref, block_ref, own_ref,
     bands, index, sums, pairs, blocks, in_sems, w_sems, out_sems, pair_sems,
 ):
     core = core_of()
@@ -80,8 +81,12 @@
         copy.start()
     for copy in loads:
         copy.wait()
-    stores = [pltpu.make_async_copy(bands, table_ref.at[pl.ds(0, count), :], out_sems.at[0])]
+    stores = [
+        pltpu.make_async_copy(bands, table_ref.at[pl.ds(0, count), :], out_sems.at[0]),
+        pltpu.make_async_copy(bands, own_ref.at[pl.ds(0, count), :], out_sems.at[4]),
+    ]
     stores[0].start()
+    stores[1].start()
     for copy in gathers:
         copy.wait()
     joined = JOINED * SLICE
@@ -103,8 +108,9 @@
             hot = one_hot(2.0 * here + parity, stop - start)
             parts.append(jnp.dot(hot, bands[start:stop, :], preferred_element_type=jnp.float32))
         picked.append(jnp.concatenate(parts, 1))
-    stores.append(pltpu.make_async_copy(sums, table_ref.at[pl.ds(count, 2 * strips), :], out_sems.at[1]))
-    stores[-1].start()
+    for i, ref in ((1, table_ref), (5, own_ref)):
+        stores.append(pltpu.make_async_copy(sums, ref.at[pl.ds(count, 2 * strips), :], out_sems.at[i]))
+        stores[-1].start()
     real, imag = densities(*picked)
     pairs[...] = jnp.concatenate([real.T, imag.T], 1).astype(jnp.bfloat16)
     for place in range(out_ref.shape[0]):
@@ -114,22 +120,23 @@
         copy.wait()
 
 
-def rows_kernel(own_ref, partner_ref, density_ref, table, at_ref):
+def rows_kernel(own_ref, partner_ref, density_ref, table, at_ref, held, sem):
     core = core_of()
 
-    @pl.when(pl.program_id(0) == 0)
-    def _():
-        strips = at_ref.shape[1]
-        split = 2 * VAL * 4
-        bands = 2 * (VAL + CON) * 4
-        at_ref[0] = own_ref[bands : bands + strips, :].astype(jnp.float32)
-        at_ref[1] = own_ref[bands + strips : bands + 2 * strips, :].astype(jnp.float32)
-        both = jnp.concatenate([own_ref[0:bands, :], partner_ref[0:bands, :]], 1)
+    copy = pltpu.make_async_copy(own_ref.at[pl.ds(0, held.shape[0]), :], held, sem)
+    copy.start()
+    strips = at_ref.shape[1]
+    split = 2 * VAL * 4
+    bands = 2 * (VAL + CON) * 4
+    for place, ref in ((1, partner_ref), (0, held)):
+        if place == 0:
+            copy.wait()
         for parity in range(2):
-            lanes = pl.ds(parity * 2 * SLICE, 2 * SLICE)
-            table[0:KPAD, lanes] = pick(parity, both[:split])
-            table[KPAD:, lanes] = pick(parity, both[split:bands])
-
+            lanes = slice((2 * parity + place) * SLICE, (2 * parity + place + 1) * SLICE)
+            table[0:KPAD, lanes] = pick(parity, ref[0:split, :])
+            table[KPAD:, lanes] = pick(parity, ref[split:bands, :])
+    at_ref[0] = held[bands : bands + strips, :].astype(jnp.float32)
+    at_ref[1] = held[bands + strips : bands + 2 * strips, :].astype(jnp.float32)
     picked = []
     for which in range(2):
         index = []
@@ -219,15 +226,16 @@
     raw = (valence, conduction, *index)
     bands = valence.shape[0] + conduction.shape[0]
     dma = pltpu.SemaphoreType.DMA
-    tables, pairs, blocks = pl.pallas_call(
+    tables, pairs, blocks, own_tables = pl.pallas_call(
         columns_kernel,
         out_shape=(
             jax.ShapeDtypeStruct((bands + 2 * strips + JOINED * SLICE, SLICE), bf16),
             jax.ShapeDtypeStruct((chips, SLICE, 2 * WIDTH), bf16),
             jax.ShapeDtypeStruct(((2 * chips - JOINED) * SLICE, SLICE), bf16),
+            jax.ShapeDtypeStruct((ROOM, SLICE), bf16),
         ),
         in_specs=[anywhere] * 6,
-        out_specs=(anywhere,) * 3,
+        out_specs=(anywhere,) * 4,
         scratch_shapes=[
             pltpu.VMEM((bands, SLICE), bf16),
             pltpu.VMEM((3, strips, 128), jnp.int32),
@@ -236,7 +244,7 @@
             pltpu.VMEM((2 * chips * SLICE, SLICE), bf16),
             dma((5,)),
             dma((2, chips)),
-            dma((4,)),
+            dma((6,)),
             dma((chips,)),
         ],
         compiler_params=ALL,
@@ -249,13 +257,18 @@
         rows_kernel,
         out_shape=jax.ShapeDtypeStruct((strips * 64, 4 * SLICE), bf16),
         grid=(strips // STRIPS,),
-        in_specs=[whole(tables), whole(partner_tables)],
+        in_specs=[anywhere, whole(partner_tables)],
         out_specs=pl.BlockSpec((STRIPS * 64, 4 * SLICE), lambda m: (m, 0)),
-        scratch_shapes=[pltpu.VMEM((2 * KPAD, 4 * SLICE), bf16), pltpu.VMEM((2, strips, 128), f32)],
-        compiler_params=LITTLE,
+        scratch_shapes=[
+            pltpu.VMEM((2 * KPAD, 4 * SLICE), bf16),
+            pltpu.VMEM((2, strips, 128), f32),
+            pltpu.VMEM((bands + 2 * strips, SLICE), bf16),
+            dma,
+        ],
+        compiler_params=pltpu.CompilerParams(vmem_limit_bytes=48 * MIB),
         cost_estimate=pl.CostEstimate(flops=0, bytes_accessed=0, transcendentals=0),
         name="rows",
-    )(tables, partner_tables)
+    )(own_tables, partner_tables)
     pairs, density = lax.optimization_barrier((pairs, density))
     mine, other = pl.pallas_call(
         screened_kernel,

time: 46.2 us -> 46.3 us (level)
  Pallas kernels: 7.57 us -> 8.64 us
  local copies, waits for them, and re-layouts: 0.99 us -> 0 us
    pallas_call x1, Pallas kernels: 1.65 us -> 2.7 us  [shards(): pl.pallas_call(rows_kernel, out_shape=jax.ShapeDtypeStruct((strips * 64,...]
    unnamed x2 -> x0, local copies, waits for them, and re-layouts: 0.99 us -> none
  transfers between devices with their start and end apart: 4 -> 4, of which waited for: 1 -> 1; matrix products, arithmetic and copies ran while one was open for 0% -> 0% of each run, Pallas kernels for 4% -> 6%
where the time goes in v14:
time: 46.3 us; the launch traced here: 45.7 us
  blocking collectives  18.4 us (40%)
  starting transfers between devices  17.6 us (38%)
  Pallas kernels  8.64 us (19%)
  waiting for transfers between devices  0.97 us (2%)
    all_to_all x1, blocking collectives, shards(): lax.all_to_all(partial, 'row', 0, 0, axis_index_groups=same_core, tiled=T...  18.4 us
    ppermute x1, starting transfers between devices, shards(): partner_tables = lax.ppermute(tables, 'row', swap)  6.42 us
    all_to_all x1, starting transfers between devices, shards(): lax.all_to_all(pairs, 'row', 0, 0, axis_index_groups=same_core, tiled=True)  5.88 us
    ppermute x1, starting transfers between devices, shards(): other = lax.ppermute(other, 'row', swap)  3.42 us
    pallas_call x1, Pallas kernels, shards(): pl.pallas_call(columns_kernel, out_shape=(jax.ShapeDtypeStruct((bands + 2...  2.73 us
    pallas_call x1, Pallas kernels, shards(): pl.pallas_call(rows_kernel, out_shape=jax.ShapeDtypeStruct((strips * 64,...  2.7 us
    ppermute x1, starting transfers between devices, shards(): blocks = lax.ppermute(blocks, 'row', swap)  1.92 us
    pallas_call x1, Pallas kernels, shards(): pl.pallas_call(screened_kernel, out_shape=tuple((jax.ShapeDtypeStruct((2,...  1.66 us
  transfers between devices with their start and end apart: 4, of which 1 were waited for; matrix products, arithmetic and copies ran while one was open for 0% of the time, Pallas kernels for 6%

profile of v14, /device:TPU:1, one launch (start us, length us, event | category | flops | bytes accessed | tf_op | source)
XLA Modules:
  0.0 45.7 jit_solution(379357958956088324)
XLA Ops:
  0.0 2.7 %columns.1 = (bf16[1600,128]{1,0:T(8,128)(2,1)}, bf16[8,128,256]{2,1,0:T(8,128)(2,1)}, bf16[1408,128]{1,0:T(8,128)(2,1)}, bf16[65536,128]{1,0:T(8,128)(2,1)}) custom-call(bf16[384,128]{1,0:T(8,128)(2,1)} %bitcast.7, bf16[512,128]{1,0:T(8,128)(2,1)} %bitcast.6, s32[32,128]{1,0:T(8,128)} %bitcast.8, s32[32,128]{1,0:T(8,128)} %bitcast.9, s32[32,128]{1,0:T(8,128)} %bitcast.10, ...), custom_call_target="tpu_custom_call" | custom-call | tf_op jit(solution)/shard_map/columns/pallas_call | solution.py:229
  2.7 5.9 %all-to-all-start = ((bf16[8,128,256]{2,1,0:T(8,128)(2,1)}), bf16[8,128,256]{2,1,0:T(8,128)(2,1)S(1)}, u32[]{:S(2)}, u32[]{:S(2)}) async-start(bf16[8,128,256]{2,1,0:T(8,128)(2,1)} %get-tuple-element.13), calls=%async_computation | async-start | bytes 1048576 | tf_op jit(solution)/shard_map/all_to_all | solution.py:253
  8.6 6.4 %collective-permute-start = (bf16[1600,128]{1,0:T(8,128)(2,1)}, bf16[1600,128]{1,0:T(8,128)(2,1)S(1)}, u32[]{:S(2)}, u32[]{:S(2)}) collective-permute-start(bf16[1600,128]{1,0:T(8,128)(2,1)} %get-tuple-element.15), channel_id=1, source_target_pairs={{0,32},{32,0},{64,96},{96,64},{128,160},{160,128},{192,224},{224,1... | collective-permute-start | bytes 1228808 | tf_op jit(solution)/shard_map/ppermute | solution.py:254
  15.0 1.9 %collective-permute-start.1 = (bf16[1408,128]{1,0:T(8,128)(2,1)}, bf16[1408,128]{1,0:T(8,128)(2,1)S(1)}, u32[]{:S(2)}, u32[]{:S(2)}) collective-permute-start(bf16[1408,128]{1,0:T(8,128)(2,1)} %get-tuple-element.17), channel_id=1, source_target_pairs={{0,32},{32,0},{64,96},{96,64},{128,160},{160,128},{192,224},{224,1... | collective-permute-start | bytes 1081352 | tf_op jit(solution)/shard_map/ppermute | solution.py:255
  17.0 0.0 collective-permute-done.partner_ref.joined_ref
  17.0 2.7 %rows.1.density_ref = bf16[2048,512]{1,0:T(8,128)(2,1)S(1)} custom-call(bf16[65536,128]{1,0:T(8,128)(2,1)} %get-tuple-element.14.own_ref, bf16[1600,128]{1,0:T(8,128)(2,1)S(1)} %collective-permute-done.partner_ref.joined_ref), custom_call_target="tpu_custom_call" | custom-call | tf_op jit(solution)/shard_map/rows/pallas_call | solution.py:256
  19.7 0.0 all-to-all-done.pairs_ref
  19.7 0.0 collective-permute-done.1.block_ref
  19.7 1.7 %screened.1 = (f32[2,128,256]{2,1,0:T(8,128)S(1)}, bf16[2,128,256]{2,1,0:T(8,128)(2,1)S(1)}) custom-call(bf16[8,128,256]{2,1,0:T(8,128)(2,1)S(1)} %all-to-all-done.pairs_ref, bf16[2,128,2048]{2,1,0:T(8,128)(2,1)} %own_ref.1, bf16[1600,128]{1,0:T(8,128)(2,1)S(1)} %collective-permute-done.partner_ref.joined_ref, ...), custom_call_target="tpu_custom_call" | custom-call | tf_op jit(solution)/shard_map/screened/pallas_call | solution.py:273
  21.4 3.4 %collective-permute-start.2 = (bf16[2,128,256]{2,1,0:T(8,128)(2,1)S(1)}, bf16[2,128,256]{2,1,0:T(8,128)(2,1)S(1)}, u32[]{:S(2)}, u32[]{:S(2)}) collective-permute-start(bf16[2,128,256]{2,1,0:T(8,128)(2,1)S(1)} %get-tuple-element.19), channel_id=1, source_target_pairs={{0,32},{32,0},{64,96},{96,64},{128,160},{160,128},{192,224},{224,1... | collective-permute-start | bytes 393224 | tf_op jit(solution)/shard_map/ppermute | solution.py:281
  24.8 1.0 %collective-permute-done.2.other_ref = bf16[2,128,256]{2,1,0:T(8,128)(2,1)S(1)} collective-permute-done((bf16[2,128,256]{2,1,0:T(8,128)(2,1)S(1)}, bf16[2,128,256]{2,1,0:T(8,128)(2,1)S(1)}, u32[]{:S(2)}, u32[]{:S(2)}) %collective-permute-start.2) | collective-permute-done | bytes 131104 | tf_op jit(solution)/shard_map/ppermute | solution.py:281
  25.8 0.7 %direct.1 = bf16[8,256,256]{2,1,0:T(8,128)(2,1)S(1)} custom-call(f32[2,128,256]{2,1,0:T(8,128)S(1)} %get-tuple-element.18.mine_ref, bf16[2,128,256]{2,1,0:T(8,128)(2,1)S(1)} %collective-permute-done.2.other_ref, bf16[2048,512]{1,0:T(8,128)(2,1)S(1)} %rows.1.density_ref), custom_call_target="tpu_custom_call" | custom-call | tf_op jit(solution)/shard_map/direct/pallas_call | solution.py:282
  26.5 18.4 %all_to_all.10.in_ref = bf16[8,256,256]{2,1,0:T(8,128)(2,1)S(1)} all-to-all(bf16[8,256,256]{2,1,0:T(8,128)(2,1)S(1)} %direct.1), channel_id=1, replica_groups={{0,256,64,320,128,384,192,448},{32,288,96,352,160,416,224,480},{1,257,6..., dimensions={0} | all-to-all | bytes 2097152 | tf_op jit(solution)/shard_map/all_to_all | solution.py:289
  44.9 0.8 %total.1 = f32[2,256,128]{2,1,0:T(8,128)} custom-call(bf16[8,256,256]{2,1,0:T(8,128)(2,1)S(1)} %all_to_all.10.in_ref), custom_call_target="tpu_custom_call" | custom-call | tf_op jit(solution)/shard_map/total/pallas_call | solution.py:290
Async XLA Ops:
  2.7 17.0 %all-to-all-start = ((bf16[8,128,256]{2,1,0:T(8,128)(2,1)}), bf16[8,128,256]{2,1,0:T(8,128)(2,1)S(1)}, u32[]{:S(2)}, u32[]{:S(2)}) async-start(bf16[8,128,256]{2,1,0:T(8,128)(2,1)} %get-tuple-element.13), calls=%async_computation | async-start | bytes 1048576 | tf_op jit(solution)/shard_map/all_to_all | solution.py:253
  8.6 8.4 %collective-permute-start = (bf16[1600,128]{1,0:T(8,128)(2,1)}, bf16[1600,128]{1,0:T(8,128)(2,1)S(1)}, u32[]{:S(2)}, u32[]{:S(2)}) collective-permute-start(bf16[1600,128]{1,0:T(8,128)(2,1)} %get-tuple-element.15), channel_id=1, source_target_pairs={{0,32},{32,0},{64,96},{96,64},{128,160},{160,128},{192,224},{224,1... | collective-permute-start | bytes 1228808 | tf_op jit(solution)/shard_map/ppermute | solution.py:254
  15.0 4.7 %collective-permute-start.1 = (bf16[1408,128]{1,0:T(8,128)(2,1)}, bf16[1408,128]{1,0:T(8,128)(2,1)S(1)}, u32[]{:S(2)}, u32[]{:S(2)}) collective-permute-start(bf16[1408,128]{1,0:T(8,128)(2,1)} %get-tuple-element.17), channel_id=1, source_target_pairs={{0,32},{32,0},{64,96},{96,64},{128,160},{160,128},{192,224},{224,1... | collective-permute-start | bytes 1081352 | tf_op jit(solution)/shard_map/ppermute | solution.py:255
  21.4 4.4 %collective-permute-start.2 = (bf16[2,128,256]{2,1,0:T(8,128)(2,1)S(1)}, bf16[2,128,256]{2,1,0:T(8,128)(2,1)S(1)}, u32[]{:S(2)}, u32[]{:S(2)}) collective-permute-start(bf16[2,128,256]{2,1,0:T(8,128)(2,1)S(1)} %get-tuple-element.19), channel_id=1, source_target_pairs={{0,32},{32,0},{64,96},{96,64},{128,160},{160,128},{192,224},{224,1... | collective-permute-start | bytes 393224 | tf_op jit(solution)/shard_map/ppermute | solution.py:281

commit v15 on v13

--- a/solution.py
+++ b/solution.py
@@ -12,7 +12,6 @@
 WIDTH = 128
 KPAD = 256
 RING = (0, 4, 1, 5, 2, 6, 3, 7)
-STRIPS = 32
 JOINED = 5
 MIB = 1024 * 1024
 LITTLE = pltpu.CompilerParams(vmem_limit_bytes=16 * MIB)
@@ -117,25 +116,26 @@
 def rows_kernel(own_ref, partner_ref, density_ref, table, at_ref):
     core = core_of()
 
-    @pl.when(pl.program_id(0) == 0)
-    def _():
-        strips = at_ref.shape[1]
-        split = 2 * VAL * 4
-        bands = 2 * (VAL + CON) * 4
-        at_ref[0] = own_ref[bands : bands + strips, :].astype(jnp.float32)
-        at_ref[1] = own_ref[bands + strips : bands + 2 * strips, :].astype(jnp.float32)
-        both = jnp.concatenate([own_ref[0:bands, :], partner_ref[0:bands, :]], 1)
-        for parity in range(2):
-            lanes = pl.ds(parity * 2 * SLICE, 2 * SLICE)
-            table[0:KPAD, lanes] = pick(parity, both[:split])
-            table[KPAD:, lanes] = pick(parity, both[split:bands])
-
+    strips = at_ref.shape[1]
+    split = 2 * VAL * 4
+    bands = 2 * (VAL + CON) * 4
+    at_ref[0] = own_ref[bands : bands + strips, :].astype(jnp.float32)
+    at_ref[1] = own_ref[bands + strips : bands + 2 * strips, :].astype(jnp.float32)
+    both = jnp.concatenate([own_ref[0:bands, :], partner_ref[0:bands, :]], 1)
+    for parity in range(2):
+        lanes = pl.ds(parity * 2 * SLICE, 2 * SLICE)
+        table[0:KPAD, lanes] = pick(parity, both[:split])
+        table[KPAD:, lanes] = pick(parity, both[split:bands])
+    lane = lax.broadcasted_iota(jnp.int32, (strips // 2, 128), 1)
+    low = lane // FINE % 2 == 0
     picked = []
     for which in range(2):
-        index = []
-        for s in range(STRIPS):
-            strip = lane_matrix(at_ref[which, pl.ds(pl.program_id(0) * STRIPS + s, 1), :]).reshape(-1, 2, FINE, 128)
-            index.append(jnp.where(core == 0, strip[:, 0], strip[:, 1]).reshape(-1, 128))
+        even = at_ref[which, pl.ds(0, strips // 2, stride=2), :]
+        odd = at_ref[which, pl.ds(1, strips // 2, stride=2), :]
+        first = jnp.where(low, even, pltpu.roll(odd, FINE, 1))
+        second = jnp.where(low, pltpu.roll(even, 128 - FINE, 1), odd)
+        pairs = jnp.where(core == 0, first, second)
+        index = [lane_matrix(pairs[p : p + 1, :]) for p in range(strips // 2)]
         hot = one_hot(jnp.concatenate(index, 0), KPAD)
         picked.append(
             jnp.dot(hot, table[which * KPAD : (which + 1) * KPAD, :], preferred_element_type=jnp.float32)
@@ -185,8 +185,8 @@
         direct = jnp.dot(
             density_ref[m * rows : (m + 1) * rows, :], screened[...], preferred_element_type=jnp.float32
         )
-        direct = direct.reshape(strips, -1, FINE, 2 * WIDTH)
-        direct = jnp.concatenate([direct[s] for s in range(strips)], 1).astype(jnp.bfloat16)
+        direct = direct.reshape(strips // 2, -1, 2 * FINE, 2 * WIDTH)
+        direct = jnp.concatenate([direct[s] for s in range(strips // 2)], 1).astype(jnp.bfloat16)
         for place, chip in enumerate(RING):
             out_ref[place, m * strips * FINE : (m + 1) * strips * FINE, :] = direct[chip]
 
@@ -245,12 +245,13 @@
     pairs = lax.all_to_all(pairs, "row", 0, 0, axis_index_groups=same_core, tiled=True)
     partner_tables = lax.ppermute(tables, "row", swap)
     blocks = lax.ppermute(blocks, "row", swap)
+    density = jax.ShapeDtypeStruct((strips * 64, 4 * SLICE), bf16)
     density = pl.pallas_call(
         rows_kernel,
-        out_shape=jax.ShapeDtypeStruct((strips * 64, 4 * SLICE), bf16),
-        grid=(strips // STRIPS,),
+        out_shape=density,
+        grid=(1,),
         in_specs=[whole(tables), whole(partner_tables)],
-        out_specs=pl.BlockSpec((STRIPS * 64, 4 * SLICE), lambda m: (m, 0)),
+        out_specs=whole(density),
         scratch_shapes=[pltpu.VMEM((2 * KPAD, 4 * SLICE), bf16), pltpu.VMEM((2, strips, 128), f32)],
         compiler_params=LITTLE,
         cost_estimate=pl.CostEstimate(flops=0, bytes_accessed=0, transcendentals=0),

time: 46.2 us -> 46.2 us (level)
  no operation moved by 1% of the time
where the time goes in v15:
time: 46.2 us; the launch traced here: 45.6 us
  blocking collectives  18.3 us (40%)
  starting transfers between devices  17.7 us (38%)
  Pallas kernels  7.59 us (16%)
  local copies, waits for them, and re-layouts  0.99 us (2%)
  waiting for transfers between devices  0.97 us (2%)
    all_to_all x1, blocking collectives, shards(): lax.all_to_all(partial, 'row', 0, 0, axis_index_groups=same_core, tiled=T...  18.3 us
    ppermute x1, starting transfers between devices, shards(): partner_tables = lax.ppermute(tables, 'row', swap)  6.42 us
    all_to_all x1, starting transfers between devices, shards(): lax.all_to_all(pairs, 'row', 0, 0, axis_index_groups=same_core, tiled=True)  5.88 us
    ppermute x1, starting transfers between devices, shards(): other = lax.ppermute(other, 'row', swap)  3.45 us
    pallas_call x1, Pallas kernels, shards(): pl.pallas_call(columns_kernel, out_shape=(jax.ShapeDtypeStruct((bands + 2...  2.71 us
    ppermute x1, starting transfers between devices, shards(): blocks = lax.ppermute(blocks, 'row', swap)  1.92 us
    pallas_call x1, Pallas kernels, shards(): pl.pallas_call(rows_kernel, out_shape=density, grid=(1,), in_specs=[whole...  1.67 us
    pallas_call x1, Pallas kernels, shards(): pl.pallas_call(screened_kernel, out_shape=tuple((jax.ShapeDtypeStruct((2,...  1.66 us
  transfers between devices with their start and end apart: 4, of which 1 were waited for; matrix products, arithmetic and copies ran while one was open for 0% of the time, Pallas kernels for 4%

profile of v15, /device:TPU:1, one launch (start us, length us, event | category | flops | bytes accessed | tf_op | source)
XLA Modules:
  0.0 45.6 jit_solution(15738641237655784727)
XLA Ops:
  0.0 2.7 %columns.1 = (bf16[1600,128]{1,0:T(8,128)(2,1)}, bf16[8,128,256]{2,1,0:T(8,128)(2,1)}, bf16[1408,128]{1,0:T(8,128)(2,1)}) custom-call(bf16[384,128]{1,0:T(8,128)(2,1)} %bitcast.7, bf16[512,128]{1,0:T(8,128)(2,1)} %bitcast.6, s32[32,128]{1,0:T(8,128)} %bitcast.8, s32[32,128]{1,0:T(8,128)} %bitcast.9, s32[32,128]{1,0:T(8,128)} %bitcast.10, ...), custom_call_target="tpu_custom_call" | custom-call | tf_op jit(solution)/shard_map/columns/pallas_call | solution.py:222
  2.7 5.9 %all-to-all-start = ((bf16[8,128,256]{2,1,0:T(8,128)(2,1)}), bf16[8,128,256]{2,1,0:T(8,128)(2,1)S(1)}, u32[]{:S(2)}, u32[]{:S(2)}) async-start(bf16[8,128,256]{2,1,0:T(8,128)(2,1)} %get-tuple-element.12), calls=%async_computation | async-start | bytes 1048576 | tf_op jit(solution)/shard_map/all_to_all | solution.py:245
  8.6 6.4 %collective-permute-start = (bf16[1600,128]{1,0:T(8,128)(2,1)}, bf16[1600,128]{1,0:T(8,128)(2,1)S(1)}, u32[]{:S(2)}, u32[]{:S(2)}) collective-permute-start(bf16[1600,128]{1,0:T(8,128)(2,1)} %get-tuple-element.13.own_ref), channel_id=1, source_target_pairs={{0,32},{32,0},{64,96},{96,64},{128,160},{160,128},{192,224},{224,1... | collective-permute-start | bytes 1228808 | tf_op jit(solution)/shard_map/ppermute | solution.py:246
  15.0 1.9 %collective-permute-start.1 = (bf16[1408,128]{1,0:T(8,128)(2,1)}, bf16[1408,128]{1,0:T(8,128)(2,1)S(1)}, u32[]{:S(2)}, u32[]{:S(2)}) collective-permute-start(bf16[1408,128]{1,0:T(8,128)(2,1)} %get-tuple-element.15), channel_id=1, source_target_pairs={{0,32},{32,0},{64,96},{96,64},{128,160},{160,128},{192,224},{224,1... | collective-permute-start | bytes 1081352 | tf_op jit(solution)/shard_map/ppermute | solution.py:247
  17.0 0.0 collective-permute-done.partner_ref.joined_ref
  17.0 0.0 copy-start
  17.0 1.0 %copy-done = bf16[1600,128]{1,0:T(8,128)(2,1)S(1)} copy-done((bf16[1600,128]{1,0:T(8,128)(2,1)S(1)}, bf16[1600,128]{1,0:T(8,128)(2,1)}, u32[]{:S(2)}) %copy-start) | copy-done | bytes 409624
  18.0 1.7 %rows.1.density_ref = bf16[2048,512]{1,0:T(8,128)(2,1)S(1)} custom-call(bf16[1600,128]{1,0:T(8,128)(2,1)S(1)} %copy-done, bf16[1600,128]{1,0:T(8,128)(2,1)S(1)} %collective-permute-done.partner_ref.joined_ref), custom_call_target="tpu_custom_call" | custom-call | tf_op jit(solution)/shard_map/rows/pallas_call | solution.py:249
  19.6 0.0 all-to-all-done.pairs_ref
  19.7 0.0 collective-permute-done.1.block_ref
  19.7 1.7 %screened.1 = (f32[2,128,256]{2,1,0:T(8,128)S(1)}, bf16[2,128,256]{2,1,0:T(8,128)(2,1)S(1)}) custom-call(bf16[8,128,256]{2,1,0:T(8,128)(2,1)S(1)} %all-to-all-done.pairs_ref, bf16[2,128,2048]{2,1,0:T(8,128)(2,1)} %own_ref.1, bf16[1600,128]{1,0:T(8,128)(2,1)S(1)} %collective-permute-done.partner_ref.joined_ref, ...), custom_call_target="tpu_custom_call" | custom-call | tf_op jit(solution)/shard_map/screened/pallas_call | solution.py:261
  21.3 3.4 %collective-permute-start.2 = (bf16[2,128,256]{2,1,0:T(8,128)(2,1)S(1)}, bf16[2,128,256]{2,1,0:T(8,128)(2,1)S(1)}, u32[]{:S(2)}, u32[]{:S(2)}) collective-permute-start(bf16[2,128,256]{2,1,0:T(8,128)(2,1)S(1)} %get-tuple-element.17), channel_id=1, source_target_pairs={{0,32},{32,0},{64,96},{96,64},{128,160},{160,128},{192,224},{224,1... | collective-permute-start | bytes 393224 | tf_op jit(solution)/shard_map/ppermute | solution.py:269
  24.8 1.0 %collective-permute-done.2.other_ref = bf16[2,128,256]{2,1,0:T(8,128)(2,1)S(1)} collective-permute-done((bf16[2,128,256]{2,1,0:T(8,128)(2,1)S(1)}, bf16[2,128,256]{2,1,0:T(8,128)(2,1)S(1)}, u32[]{:S(2)}, u32[]{:S(2)}) %collective-permute-start.2) | collective-permute-done | bytes 131104 | tf_op jit(solution)/shard_map/ppermute | solution.py:269
  25.7 0.7 %direct.1 = bf16[8,256,256]{2,1,0:T(8,128)(2,1)S(1)} custom-call(f32[2,128,256]{2,1,0:T(8,128)S(1)} %get-tuple-element.16.mine_ref, bf16[2,128,256]{2,1,0:T(8,128)(2,1)S(1)} %collective-permute-done.2.other_ref, bf16[2048,512]{1,0:T(8,128)(2,1)S(1)} %rows.1.density_ref), custom_call_target="tpu_custom_call" | custom-call | tf_op jit(solution)/shard_map/direct/pallas_call | solution.py:270
  26.5 18.3 %all_to_all.10.in_ref = bf16[8,256,256]{2,1,0:T(8,128)(2,1)S(1)} all-to-all(bf16[8,256,256]{2,1,0:T(8,128)(2,1)S(1)} %direct.1), channel_id=1, replica_groups={{0,256,64,320,128,384,192,448},{32,288,96,352,160,416,224,480},{1,257,6..., dimensions={0} | all-to-all | bytes 2097152 | tf_op jit(solution)/shard_map/all_to_all | solution.py:277
  44.8 0.8 %total.1 = f32[2,256,128]{2,1,0:T(8,128)} custom-call(bf16[8,256,256]{2,1,0:T(8,128)(2,1)S(1)} %all_to_all.10.in_ref), custom_call_target="tpu_custom_call" | custom-call | tf_op jit(solution)/shard_map/total/pallas_call | solution.py:278
Async XLA Ops:
  2.7 16.9 %all-to-all-start = ((bf16[8,128,256]{2,1,0:T(8,128)(2,1)}), bf16[8,128,256]{2,1,0:T(8,128)(2,1)S(1)}, u32[]{:S(2)}, u32[]{:S(2)}) async-start(bf16[8,128,256]{2,1,0:T(8,128)(2,1)} %get-tuple-element.12), calls=%async_computation | async-start | bytes 1048576 | tf_op jit(solution)/shard_map/all_to_all | solution.py:245
  8.6 8.4 %collective-permute-start = (bf16[1600,128]{1,0:T(8,128)(2,1)}, bf16[1600,128]{1,0:T(8,128)(2,1)S(1)}, u32[]{:S(2)}, u32[]{:S(2)}) collective-permute-start(bf16[1600,128]{1,0:T(8,128)(2,1)} %get-tuple-element.13.own_ref), channel_id=1, source_target_pairs={{0,32},{32,0},{64,96},{96,64},{128,160},{160,128},{192,224},{224,1... | collective-permute-start | bytes 1228808 | tf_op jit(solution)/shard_map/ppermute | solution.py:246
  15.0 4.6 %collective-permute-start.1 = (bf16[1408,128]{1,0:T(8,128)(2,1)}, bf16[1408,128]{1,0:T(8,128)(2,1)S(1)}, u32[]{:S(2)}, u32[]{:S(2)}) collective-permute-start(bf16[1408,128]{1,0:T(8,128)(2,1)} %get-tuple-element.15), channel_id=1, source_target_pairs={{0,32},{32,0},{64,96},{96,64},{128,160},{160,128},{192,224},{224,1... | collective-permute-start | bytes 1081352 | tf_op jit(solution)/shard_map/ppermute | solution.py:247
  17.0 1.0 %copy-start = (bf16[1600,128]{1,0:T(8,128)(2,1)S(1)}, bf16[1600,128]{1,0:T(8,128)(2,1)}, u32[]{:S(2)}) copy-start(bf16[1600,128]{1,0:T(8,128)(2,1)} %get-tuple-element.13.own_ref) | copy-start | bytes 1228804
  21.3 4.4 %collective-permute-start.2 = (bf16[2,128,256]{2,1,0:T(8,128)(2,1)S(1)}, bf16[2,128,256]{2,1,0:T(8,128)(2,1)S(1)}, u32[]{:S(2)}, u32[]{:S(2)}) collective-permute-start(bf16[2,128,256]{2,1,0:T(8,128)(2,1)S(1)} %get-tuple-element.17), channel_id=1, source_target_pairs={{0,32},{32,0},{64,96},{96,64},{128,160},{160,128},{192,224},{224,1... | collective-permute-start | bytes 393224 | tf_op jit(solution)/shard_map/ppermute | solution.py:269

commit v16 on v13

--- a/solution.py
+++ b/solution.py
@@ -68,7 +68,7 @@
     loads = []
     for i, (ref, place) in enumerate(zip((valence_ref, conduction_ref, v_ref, n_ref, k_ref), places)):
         loads.append(pltpu.make_async_copy(ref, place, in_sems.at[i]))
-    for copy in loads:
+    for copy in loads[2:] + loads[:2]:
         copy.start()
     gathers = []
     for part in range(2):
@@ -78,7 +78,17 @@
             gathers.append(pltpu.make_async_copy(w_ref.at[part, :, lanes], to, w_sems.at[part, place]))
     for copy in gathers:
         copy.start()
-    for copy in loads:
+    for copy in loads[2:]:
+        copy.wait()
+    own = pl.ds(lax.axis_index("col"), 1)
+    hots = []
+    for which, (width, size) in enumerate(((VAL, split), (CON, count - split))):
+        sums[which * strips : (which + 1) * strips, :] = (
+            (index[2] * width + index[which]).astype(jnp.float32).astype(jnp.bfloat16)
+        )
+        here = lane_matrix((index[2, own, :] * width + index[which, own, :]).astype(jnp.float32))
+        hots.append([one_hot(2.0 * here + parity, size) for parity in range(2)])
+    for copy in loads[:2]:
         copy.wait()
     stores = [pltpu.make_async_copy(bands, table_ref.at[pl.ds(0, count), :], out_sems.at[0])]
     stores[0].start()
@@ -91,17 +101,9 @@
     stores[-1].start()
     stores.append(pltpu.make_async_copy(blocks.at[pl.ds(joined, rest), :], block_ref, out_sems.at[3]))
     stores[-1].start()
-    own = pl.ds(lax.axis_index("col"), 1)
     picked = []
-    for which, (width, start, stop) in enumerate(((VAL, 0, split), (CON, split, count))):
-        sums[which * strips : (which + 1) * strips, :] = (
-            (index[2] * width + index[which]).astype(jnp.float32).astype(jnp.bfloat16)
-        )
-        here = lane_matrix((index[2, own, :] * width + index[which, own, :]).astype(jnp.float32))
-        parts = []
-        for parity in range(2):
-            hot = one_hot(2.0 * here + parity, stop - start)
-            parts.append(jnp.dot(hot, bands[start:stop, :], preferred_element_type=jnp.float32))
+    for pair, (start, stop) in zip(hots, ((0, split), (split, count))):
+        parts = [jnp.dot(hot, bands[start:stop, :], preferred_element_type=jnp.float32) for hot in pair]
         picked.append(jnp.concatenate(parts, 1))
     stores.append(pltpu.make_async_copy(sums, table_ref.at[pl.ds(count, 2 * strips), :], out_sems.at[1]))
     stores[-1].start()

time: 46.2 us -> 46.2 us (level)
  no operation moved by 1% of the time
where the time goes in v16:
time: 46.2 us; the launch traced here: 45.6 us
  blocking collectives  18.3 us (40%)
  starting transfers between devices  17.7 us (38%)
  Pallas kernels  7.53 us (16%)
  local copies, waits for them, and re-layouts  0.99 us (2%)
  waiting for transfers between devices  0.97 us (2%)
    all_to_all x1, blocking collectives, shards(): lax.all_to_all(partial, 'row', 0, 0, axis_index_groups=same_core, tiled=T...  18.3 us
    ppermute x1, starting transfers between devices, shards(): partner_tables = lax.ppermute(tables, 'row', swap)  6.42 us
    all_to_all x1, starting transfers between devices, shards(): lax.all_to_all(pairs, 'row', 0, 0, axis_index_groups=same_core, tiled=True)  5.87 us
    ppermute x1, starting transfers between devices, shards(): other = lax.ppermute(other, 'row', swap)  3.47 us
    pallas_call x1, Pallas kernels, shards(): pl.pallas_call(columns_kernel, out_shape=(jax.ShapeDtypeStruct((bands + 2...  2.69 us
    ppermute x1, starting transfers between devices, shards(): blocks = lax.ppermute(blocks, 'row', swap)  1.92 us
    pallas_call x1, Pallas kernels, shards(): pl.pallas_call(rows_kernel, out_shape=jax.ShapeDtypeStruct((strips * 64,...  1.65 us
    pallas_call x1, Pallas kernels, shards(): pl.pallas_call(screened_kernel, out_shape=tuple((jax.ShapeDtypeStruct((2,...  1.65 us
  transfers between devices with their start and end apart: 4, of which 1 were waited for; matrix products, arithmetic and copies ran while one was open for 0% of the time, Pallas kernels for 4%

profile of v16, /device:TPU:1, one launch (start us, length us, event | category | flops | bytes accessed | tf_op | source)
XLA Modules:
  0.0 45.6 jit_solution(14936761237088234512)
XLA Ops:
  0.0 2.7 %columns.1 = (bf16[1600,128]{1,0:T(8,128)(2,1)}, bf16[8,128,256]{2,1,0:T(8,128)(2,1)}, bf16[1408,128]{1,0:T(8,128)(2,1)}) custom-call(bf16[384,128]{1,0:T(8,128)(2,1)} %bitcast.7, bf16[512,128]{1,0:T(8,128)(2,1)} %bitcast.6, s32[32,128]{1,0:T(8,128)} %bitcast.8, s32[32,128]{1,0:T(8,128)} %bitcast.9, s32[32,128]{1,0:T(8,128)} %bitcast.10, ...), custom_call_target="tpu_custom_call" | custom-call | tf_op jit(solution)/shard_map/columns/pallas_call | solution.py:224
  2.7 5.9 %all-to-all-start = ((bf16[8,128,256]{2,1,0:T(8,128)(2,1)}), bf16[8,128,256]{2,1,0:T(8,128)(2,1)S(1)}, u32[]{:S(2)}, u32[]{:S(2)}) async-start(bf16[8,128,256]{2,1,0:T(8,128)(2,1)} %get-tuple-element.12), calls=%async_computation | async-start | bytes 1048576 | tf_op jit(solution)/shard_map/all_to_all | solution.py:247
  8.6 6.4 %collective-permute-start = (bf16[1600,128]{1,0:T(8,128)(2,1)}, bf16[1600,128]{1,0:T(8,128)(2,1)S(1)}, u32[]{:S(2)}, u32[]{:S(2)}) collective-permute-start(bf16[1600,128]{1,0:T(8,128)(2,1)} %get-tuple-element.13.own_ref), channel_id=1, source_target_pairs={{0,32},{32,0},{64,96},{96,64},{128,160},{160,128},{192,224},{224,1... | collective-permute-start | bytes 1228808 | tf_op jit(solution)/shard_map/ppermute | solution.py:248
  15.0 1.9 %collective-permute-start.1 = (bf16[1408,128]{1,0:T(8,128)(2,1)}, bf16[1408,128]{1,0:T(8,128)(2,1)S(1)}, u32[]{:S(2)}, u32[]{:S(2)}) collective-permute-start(bf16[1408,128]{1,0:T(8,128)(2,1)} %get-tuple-element.15), channel_id=1, source_target_pairs={{0,32},{32,0},{64,96},{96,64},{128,160},{160,128},{192,224},{224,1... | collective-permute-start | bytes 1081352 | tf_op jit(solution)/shard_map/ppermute | solution.py:249
  16.9 0.0 collective-permute-done.partner_ref.joined_ref
  16.9 0.0 copy-start
  17.0 1.0 %copy-done = bf16[1600,128]{1,0:T(8,128)(2,1)S(1)} copy-done((bf16[1600,128]{1,0:T(8,128)(2,1)S(1)}, bf16[1600,128]{1,0:T(8,128)(2,1)}, u32[]{:S(2)}) %copy-start) | copy-done | bytes 409624
  17.9 1.7 %rows.1.density_ref = bf16[2048,512]{1,0:T(8,128)(2,1)S(1)} custom-call(bf16[1600,128]{1,0:T(8,128)(2,1)S(1)} %copy-done, bf16[1600,128]{1,0:T(8,128)(2,1)S(1)} %collective-permute-done.partner_ref.joined_ref), custom_call_target="tpu_custom_call" | custom-call | tf_op jit(solution)/shard_map/rows/pallas_call | solution.py:250
  19.6 0.0 all-to-all-done.pairs_ref
  19.6 0.0 collective-permute-done.1.block_ref
  19.6 1.6 %screened.1 = (f32[2,128,256]{2,1,0:T(8,128)S(1)}, bf16[2,128,256]{2,1,0:T(8,128)(2,1)S(1)}) custom-call(bf16[8,128,256]{2,1,0:T(8,128)(2,1)S(1)} %all-to-all-done.pairs_ref, bf16[2,128,2048]{2,1,0:T(8,128)(2,1)} %own_ref.1, bf16[1600,128]{1,0:T(8,128)(2,1)S(1)} %collective-permute-done.partner_ref.joined_ref, ...), custom_call_target="tpu_custom_call" | custom-call | tf_op jit(solution)/shard_map/screened/pallas_call | solution.py:262
  21.3 3.5 %collective-permute-start.2 = (bf16[2,128,256]{2,1,0:T(8,128)(2,1)S(1)}, bf16[2,128,256]{2,1,0:T(8,128)(2,1)S(1)}, u32[]{:S(2)}, u32[]{:S(2)}) collective-permute-start(bf16[2,128,256]{2,1,0:T(8,128)(2,1)S(1)} %get-tuple-element.17), channel_id=1, source_target_pairs={{0,32},{32,0},{64,96},{96,64},{128,160},{160,128},{192,224},{224,1... | collective-permute-start | bytes 393224 | tf_op jit(solution)/shard_map/ppermute | solution.py:270
  24.8 1.0 %collective-permute-done.2.other_ref = bf16[2,128,256]{2,1,0:T(8,128)(2,1)S(1)} collective-permute-done((bf16[2,128,256]{2,1,0:T(8,128)(2,1)S(1)}, bf16[2,128,256]{2,1,0:T(8,128)(2,1)S(1)}, u32[]{:S(2)}, u32[]{:S(2)}) %collective-permute-start.2) | collective-permute-done | bytes 131104 | tf_op jit(solution)/shard_map/ppermute | solution.py:270
  25.7 0.7 %direct.1 = bf16[8,256,256]{2,1,0:T(8,128)(2,1)S(1)} custom-call(f32[2,128,256]{2,1,0:T(8,128)S(1)} %get-tuple-element.16.mine_ref, bf16[2,128,256]{2,1,0:T(8,128)(2,1)S(1)} %collective-permute-done.2.other_ref, bf16[2048,512]{1,0:T(8,128)(2,1)S(1)} %rows.1.density_ref), custom_call_target="tpu_custom_call" | custom-call | tf_op jit(solution)/shard_map/direct/pallas_call | solution.py:271
  26.4 18.3 %all_to_all.10.in_ref = bf16[8,256,256]{2,1,0:T(8,128)(2,1)S(1)} all-to-all(bf16[8,256,256]{2,1,0:T(8,128)(2,1)S(1)} %direct.1), channel_id=1, replica_groups={{0,256,64,320,128,384,192,448},{32,288,96,352,160,416,224,480},{1,257,6..., dimensions={0} | all-to-all | bytes 2097152 | tf_op jit(solution)/shard_map/all_to_all | solution.py:278
  44.8 0.8 %total.1 = f32[2,256,128]{2,1,0:T(8,128)} custom-call(bf16[8,256,256]{2,1,0:T(8,128)(2,1)S(1)} %all_to_all.10.in_ref), custom_call_target="tpu_custom_call" | custom-call | tf_op jit(solution)/shard_map/total/pallas_call | solution.py:279
Async XLA Ops:
  2.7 16.9 %all-to-all-start = ((bf16[8,128,256]{2,1,0:T(8,128)(2,1)}), bf16[8,128,256]{2,1,0:T(8,128)(2,1)S(1)}, u32[]{:S(2)}, u32[]{:S(2)}) async-start(bf16[8,128,256]{2,1,0:T(8,128)(2,1)} %get-tuple-element.12), calls=%async_computation | async-start | bytes 1048576 | tf_op jit(solution)/shard_map/all_to_all | solution.py:247
  8.6 8.4 %collective-permute-start = (bf16[1600,128]{1,0:T(8,128)(2,1)}, bf16[1600,128]{1,0:T(8,128)(2,1)S(1)}, u32[]{:S(2)}, u32[]{:S(2)}) collective-permute-start(bf16[1600,128]{1,0:T(8,128)(2,1)} %get-tuple-element.13.own_ref), channel_id=1, source_target_pairs={{0,32},{32,0},{64,96},{96,64},{128,160},{160,128},{192,224},{224,1... | collective-permute-start | bytes 1228808 | tf_op jit(solution)/shard_map/ppermute | solution.py:248
  15.0 4.6 %collective-permute-start.1 = (bf16[1408,128]{1,0:T(8,128)(2,1)}, bf16[1408,128]{1,0:T(8,128)(2,1)S(1)}, u32[]{:S(2)}, u32[]{:S(2)}) collective-permute-start(bf16[1408,128]{1,0:T(8,128)(2,1)} %get-tuple-element.15), channel_id=1, source_target_pairs={{0,32},{32,0},{64,96},{96,64},{128,160},{160,128},{192,224},{224,1... | collective-permute-start | bytes 1081352 | tf_op jit(solution)/shard_map/ppermute | solution.py:249
  16.9 1.0 %copy-start = (bf16[1600,128]{1,0:T(8,128)(2,1)S(1)}, bf16[1600,128]{1,0:T(8,128)(2,1)}, u32[]{:S(2)}) copy-start(bf16[1600,128]{1,0:T(8,128)(2,1)} %get-tuple-element.13.own_ref) | copy-start | bytes 1228804
  21.3 4.4 %collective-permute-start.2 = (bf16[2,128,256]{2,1,0:T(8,128)(2,1)S(1)}, bf16[2,128,256]{2,1,0:T(8,128)(2,1)S(1)}, u32[]{:S(2)}, u32[]{:S(2)}) collective-permute-start(bf16[2,128,256]{2,1,0:T(8,128)(2,1)S(1)} %get-tuple-element.17), channel_id=1, source_target_pairs={{0,32},{32,0},{64,96},{96,64},{128,160},{160,128},{192,224},{224,1... | collective-permute-start | bytes 393224 | tf_op jit(solution)/shard_map/ppermute | solution.py:270

commit v17 on v16

--- a/solution.py
+++ b/solution.py
@@ -163,10 +163,12 @@
         if half == 0:
             for copy in copies:
                 copy.wait()
-        parts = []
-        for part in range(2):
-            w = jnp.concatenate(blocks[part * chips : (part + 1) * chips], 1) if half else held[part]
-            parts.append(jnp.dot(w, pairs, preferred_element_type=jnp.float32))
+        if half:
+            w = jnp.concatenate([jnp.concatenate(blocks[part * chips : (part + 1) * chips], 1) for part in range(2)], 0)
+        else:
+            w = held[...].reshape(2 * SLICE, -1)
+        product = jnp.dot(w, pairs, preferred_element_type=jnp.float32)
+        parts = product[:SLICE], product[SLICE:]
         real = parts[0][:, :WIDTH] - parts[1][:, WIDTH:]
         imag = parts[0][:, WIDTH:] + parts[1][:, :WIDTH]
         both = jnp.concatenate([real, imag], 1)

time: 46.2 us -> 46.4 us (level)
  no operation moved by 1% of the time
where the time goes in v17:
time: 46.4 us; the launch traced here: 45.8 us
  blocking collectives  18.3 us (39%)
  starting transfers between devices  17.7 us (38%)
  Pallas kernels  7.74 us (17%)
  local copies, waits for them, and re-layouts  0.99 us (2%)
  waiting for transfers between devices  0.97 us (2%)
    all_to_all x1, blocking collectives, shards(): lax.all_to_all(partial, 'row', 0, 0, axis_index_groups=same_core, tiled=T...  18.3 us
    ppermute x1, starting transfers between devices, shards(): partner_tables = lax.ppermute(tables, 'row', swap)  6.42 us
    all_to_all x1, starting transfers between devices, shards(): lax.all_to_all(pairs, 'row', 0, 0, axis_index_groups=same_core, tiled=True)  5.87 us
    ppermute x1, starting transfers between devices, shards(): other = lax.ppermute(other, 'row', swap)  3.46 us
    pallas_call x1, Pallas kernels, shards(): pl.pallas_call(columns_kernel, out_shape=(jax.ShapeDtypeStruct((bands + 2...  2.69 us
    ppermute x1, starting transfers between devices, shards(): blocks = lax.ppermute(blocks, 'row', swap)  1.92 us
    pallas_call x1, Pallas kernels, shards(): pl.pallas_call(screened_kernel, out_shape=tuple((jax.ShapeDtypeStruct((2,...  1.86 us
    pallas_call x1, Pallas kernels, shards(): pl.pallas_call(rows_kernel, out_shape=jax.ShapeDtypeStruct((strips * 64,...  1.65 us
  transfers between devices with their start and end apart: 4, of which 1 were waited for; matrix products, arithmetic and copies ran while one was open for 0% of the time, Pallas kernels for 4%

profile of v17, /device:TPU:1, one launch (start us, length us, event | category | flops | bytes accessed | tf_op | source)
XLA Modules:
  0.0 45.8 jit_solution(16766665220990582590)
XLA Ops:
  0.0 2.7 %columns.1 = (bf16[1600,128]{1,0:T(8,128)(2,1)}, bf16[8,128,256]{2,1,0:T(8,128)(2,1)}, bf16[1408,128]{1,0:T(8,128)(2,1)}) custom-call(bf16[384,128]{1,0:T(8,128)(2,1)} %bitcast.7, bf16[512,128]{1,0:T(8,128)(2,1)} %bitcast.6, s32[32,128]{1,0:T(8,128)} %bitcast.8, s32[32,128]{1,0:T(8,128)} %bitcast.9, s32[32,128]{1,0:T(8,128)} %bitcast.10, ...), custom_call_target="tpu_custom_call" | custom-call | tf_op jit(solution)/shard_map/columns/pallas_call | solution.py:226
  2.7 5.9 %all-to-all-start = ((bf16[8,128,256]{2,1,0:T(8,128)(2,1)}), bf16[8,128,256]{2,1,0:T(8,128)(2,1)S(1)}, u32[]{:S(2)}, u32[]{:S(2)}) async-start(bf16[8,128,256]{2,1,0:T(8,128)(2,1)} %get-tuple-element.12), calls=%async_computation | async-start | bytes 1048576 | tf_op jit(solution)/shard_map/all_to_all | solution.py:249
  8.6 6.4 %collective-permute-start = (bf16[1600,128]{1,0:T(8,128)(2,1)}, bf16[1600,128]{1,0:T(8,128)(2,1)S(1)}, u32[]{:S(2)}, u32[]{:S(2)}) collective-permute-start(bf16[1600,128]{1,0:T(8,128)(2,1)} %get-tuple-element.13.own_ref), channel_id=1, source_target_pairs={{0,32},{32,0},{64,96},{96,64},{128,160},{160,128},{192,224},{224,1... | collective-permute-start | bytes 1228808 | tf_op jit(solution)/shard_map/ppermute | solution.py:250
  15.0 1.9 %collective-permute-start.1 = (bf16[1408,128]{1,0:T(8,128)(2,1)}, bf16[1408,128]{1,0:T(8,128)(2,1)S(1)}, u32[]{:S(2)}, u32[]{:S(2)}) collective-permute-start(bf16[1408,128]{1,0:T(8,128)(2,1)} %get-tuple-element.15), channel_id=1, source_target_pairs={{0,32},{32,0},{64,96},{96,64},{128,160},{160,128},{192,224},{224,1... | collective-permute-start | bytes 1081352 | tf_op jit(solution)/shard_map/ppermute | solution.py:251
  16.9 0.0 collective-permute-done.partner_ref.joined_ref
  16.9 0.0 copy-start
  17.0 1.0 %copy-done = bf16[1600,128]{1,0:T(8,128)(2,1)S(1)} copy-done((bf16[1600,128]{1,0:T(8,128)(2,1)S(1)}, bf16[1600,128]{1,0:T(8,128)(2,1)}, u32[]{:S(2)}) %copy-start) | copy-done | bytes 409624
  17.9 1.7 %rows.1.density_ref = bf16[2048,512]{1,0:T(8,128)(2,1)S(1)} custom-call(bf16[1600,128]{1,0:T(8,128)(2,1)S(1)} %copy-done, bf16[1600,128]{1,0:T(8,128)(2,1)S(1)} %collective-permute-done.partner_ref.joined_ref), custom_call_target="tpu_custom_call" | custom-call | tf_op jit(solution)/shard_map/rows/pallas_call | solution.py:252
  19.6 0.0 all-to-all-done.pairs_ref
  19.6 0.0 collective-permute-done.1.block_ref
  19.6 1.9 %screened.1 = (f32[2,128,256]{2,1,0:T(8,128)S(1)}, bf16[2,128,256]{2,1,0:T(8,128)(2,1)S(1)}) custom-call(bf16[8,128,256]{2,1,0:T(8,128)(2,1)S(1)} %all-to-all-done.pairs_ref, bf16[2,128,2048]{2,1,0:T(8,128)(2,1)} %own_ref.1, bf16[1600,128]{1,0:T(8,128)(2,1)S(1)} %collective-permute-done.partner_ref.joined_ref, ...), custom_call_target="tpu_custom_call" | custom-call | tf_op jit(solution)/shard_map/screened/pallas_call | solution.py:264
  21.5 3.5 %collective-permute-start.2 = (bf16[2,128,256]{2,1,0:T(8,128)(2,1)S(1)}, bf16[2,128,256]{2,1,0:T(8,128)(2,1)S(1)}, u32[]{:S(2)}, u32[]{:S(2)}) collective-permute-start(bf16[2,128,256]{2,1,0:T(8,128)(2,1)S(1)} %get-tuple-element.17), channel_id=1, source_target_pairs={{0,32},{32,0},{64,96},{96,64},{128,160},{160,128},{192,224},{224,1... | collective-permute-start | bytes 393224 | tf_op jit(solution)/shard_map/ppermute | solution.py:272
  25.0 1.0 %collective-permute-done.2.other_ref = bf16[2,128,256]{2,1,0:T(8,128)(2,1)S(1)} collective-permute-done((bf16[2,128,256]{2,1,0:T(8,128)(2,1)S(1)}, bf16[2,128,256]{2,1,0:T(8,128)(2,1)S(1)}, u32[]{:S(2)}, u32[]{:S(2)}) %collective-permute-start.2) | collective-permute-done | bytes 131104 | tf_op jit(solution)/shard_map/ppermute | solution.py:272
  25.9 0.7 %direct.1 = bf16[8,256,256]{2,1,0:T(8,128)(2,1)S(1)} custom-call(f32[2,128,256]{2,1,0:T(8,128)S(1)} %get-tuple-element.16.mine_ref, bf16[2,128,256]{2,1,0:T(8,128)(2,1)S(1)} %collective-permute-done.2.other_ref, bf16[2048,512]{1,0:T(8,128)(2,1)S(1)} %rows.1.density_ref), custom_call_target="tpu_custom_call" | custom-call | tf_op jit(solution)/shard_map/direct/pallas_call | solution.py:273
  26.6 18.3 %all_to_all.10.in_ref = bf16[8,256,256]{2,1,0:T(8,128)(2,1)S(1)} all-to-all(bf16[8,256,256]{2,1,0:T(8,128)(2,1)S(1)} %direct.1), channel_id=1, replica_groups={{0,256,64,320,128,384,192,448},{32,288,96,352,160,416,224,480},{1,257,6..., dimensions={0} | all-to-all | bytes 2097152 | tf_op jit(solution)/shard_map/all_to_all | solution.py:280
  45.0 0.8 %total.1 = f32[2,256,128]{2,1,0:T(8,128)} custom-call(bf16[8,256,256]{2,1,0:T(8,128)(2,1)S(1)} %all_to_all.10.in_ref), custom_call_target="tpu_custom_call" | custom-call | tf_op jit(solution)/shard_map/total/pallas_call | solution.py:281
Async XLA Ops:
  2.7 16.9 %all-to-all-start = ((bf16[8,128,256]{2,1,0:T(8,128)(2,1)}), bf16[8,128,256]{2,1,0:T(8,128)(2,1)S(1)}, u32[]{:S(2)}, u32[]{:S(2)}) async-start(bf16[8,128,256]{2,1,0:T(8,128)(2,1)} %get-tuple-element.12), calls=%async_computation | async-start | bytes 1048576 | tf_op jit(solution)/shard_map/all_to_all | solution.py:249
  8.6 8.4 %collective-permute-start = (bf16[1600,128]{1,0:T(8,128)(2,1)}, bf16[1600,128]{1,0:T(8,128)(2,1)S(1)}, u32[]{:S(2)}, u32[]{:S(2)}) collective-permute-start(bf16[1600,128]{1,0:T(8,128)(2,1)} %get-tuple-element.13.own_ref), channel_id=1, source_target_pairs={{0,32},{32,0},{64,96},{96,64},{128,160},{160,128},{192,224},{224,1... | collective-permute-start | bytes 1228808 | tf_op jit(solution)/shard_map/ppermute | solution.py:250
  15.0 4.6 %collective-permute-start.1 = (bf16[1408,128]{1,0:T(8,128)(2,1)}, bf16[1408,128]{1,0:T(8,128)(2,1)S(1)}, u32[]{:S(2)}, u32[]{:S(2)}) collective-permute-start(bf16[1408,128]{1,0:T(8,128)(2,1)} %get-tuple-element.15), channel_id=1, source_target_pairs={{0,32},{32,0},{64,96},{96,64},{128,160},{160,128},{192,224},{224,1... | collective-permute-start | bytes 1081352 | tf_op jit(solution)/shard_map/ppermute | solution.py:251
  16.9 1.0 %copy-start = (bf16[1600,128]{1,0:T(8,128)(2,1)S(1)}, bf16[1600,128]{1,0:T(8,128)(2,1)}, u32[]{:S(2)}) copy-start(bf16[1600,128]{1,0:T(8,128)(2,1)} %get-tuple-element.13.own_ref) | copy-start | bytes 1228804
  21.5 4.4 %collective-permute-start.2 = (bf16[2,128,256]{2,1,0:T(8,128)(2,1)S(1)}, bf16[2,128,256]{2,1,0:T(8,128)(2,1)S(1)}, u32[]{:S(2)}, u32[]{:S(2)}) collective-permute-start(bf16[2,128,256]{2,1,0:T(8,128)(2,1)S(1)} %get-tuple-element.17), channel_id=1, source_target_pairs={{0,32},{32,0},{64,96},{96,64},{128,160},{160,128},{192,224},{224,1... | collective-permute-start | bytes 393224 | tf_op jit(solution)/shard_map/ppermute | solution.py:272

commit v18 on v16

--- a/solution.py
+++ b/solution.py
@@ -148,10 +148,11 @@
 def screened_kernel(pairs_ref, own_ref, joined_ref, block_ref, out_ref, sent_ref, held, sems):
     core = core_of()
     copies = []
-    for place, chip in enumerate(RING):
-        lanes = pl.ds(pl.multiple_of((2 * chip + core) * SLICE, SLICE), SLICE)
-        to = held.at[:, :, place * SLICE : (place + 1) * SLICE]
-        copies.append(pltpu.make_async_copy(own_ref.at[:, :, lanes], to, sems.at[place]))
+    for part in range(2):
+        for place, chip in enumerate(RING):
+            lanes = pl.ds(pl.multiple_of((2 * chip + core) * SLICE, SLICE), SLICE)
+            to = held.at[part, :, pl.ds(place * SLICE, SLICE)]
+            copies.append(pltpu.make_async_copy(own_ref.at[part, :, lanes], to, sems.at[part, place]))
     for copy in copies:
         copy.start()
     pairs = pairs_ref[...].reshape(-1, 2 * WIDTH)
@@ -160,11 +161,11 @@
     blocks = [joined_ref[start + i * SLICE : start + (i + 1) * SLICE, :] for i in range(JOINED)]
     blocks += [block_ref[i * SLICE : (i + 1) * SLICE, :] for i in range(2 * chips - JOINED)]
     for half in (1, 0):
-        if half == 0:
-            for copy in copies:
-                copy.wait()
         parts = []
         for part in range(2):
+            if half == 0:
+                for copy in copies[part * chips : (part + 1) * chips]:
+                    copy.wait()
             w = jnp.concatenate(blocks[part * chips : (part + 1) * chips], 1) if half else held[part]
             parts.append(jnp.dot(w, pairs, preferred_element_type=jnp.float32))
         real = parts[0][:, :WIDTH] - parts[1][:, WIDTH:]
@@ -263,7 +264,7 @@
         screened_kernel,
         out_shape=tuple(jax.ShapeDtypeStruct((2, SLICE, 2 * WIDTH), kind) for kind in (f32, bf16)),
         in_specs=[in_vmem, anywhere, in_vmem, in_vmem],
-        scratch_shapes=[pltpu.VMEM((2, SLICE, chips * SLICE), bf16), pltpu.SemaphoreType.DMA((chips,))],
+        scratch_shapes=[pltpu.VMEM((2, SLICE, chips * SLICE), bf16), pltpu.SemaphoreType.DMA((2, chips))],
         compiler_params=MUCH,
         name="screened",
     )(pairs, screened, partner_tables, blocks)

time: 46.2 us -> 46.4 us (level)
  no operation moved by 1% of the time
where the time goes in v18:
time: 46.4 us; the launch traced here: 45.7 us
  blocking collectives  18.3 us (39%)
  starting transfers between devices  17.7 us (38%)
  Pallas kernels  7.69 us (17%)
  local copies, waits for them, and re-layouts  0.99 us (2%)
  waiting for transfers between devices  0.97 us (2%)
    all_to_all x1, blocking collectives, shards(): lax.all_to_all(partial, 'row', 0, 0, axis_index_groups=same_core, tiled=T...  18.3 us
    ppermute x1, starting transfers between devices, shards(): partner_tables = lax.ppermute(tables, 'row', swap)  6.42 us
    all_to_all x1, starting transfers between devices, shards(): lax.all_to_all(pairs, 'row', 0, 0, axis_index_groups=same_core, tiled=True)  5.87 us
    ppermute x1, starting transfers between devices, shards(): other = lax.ppermute(other, 'row', swap)  3.47 us
    pallas_call x1, Pallas kernels, shards(): pl.pallas_call(columns_kernel, out_shape=(jax.ShapeDtypeStruct((bands + 2...  2.69 us
    ppermute x1, starting transfers between devices, shards(): blocks = lax.ppermute(blocks, 'row', swap)  1.92 us
    pallas_call x1, Pallas kernels, shards(): pl.pallas_call(screened_kernel, out_shape=tuple((jax.ShapeDtypeStruct((2,...  1.79 us
    pallas_call x1, Pallas kernels, shards(): pl.pallas_call(rows_kernel, out_shape=jax.ShapeDtypeStruct((strips * 64,...  1.65 us
  transfers between devices with their start and end apart: 4, of which 1 were waited for; matrix products, arithmetic and copies ran while one was open for 0% of the time, Pallas kernels for 4%

profile of v18, /device:TPU:1, one launch (start us, length us, event | category | flops | bytes accessed | tf_op | source)
XLA Modules:
  0.0 45.7 jit_solution(4345147069601599725)
XLA Ops:
  0.0 2.7 %columns.1 = (bf16[1600,128]{1,0:T(8,128)(2,1)}, bf16[8,128,256]{2,1,0:T(8,128)(2,1)}, bf16[1408,128]{1,0:T(8,128)(2,1)}) custom-call(bf16[384,128]{1,0:T(8,128)(2,1)} %bitcast.7, bf16[512,128]{1,0:T(8,128)(2,1)} %bitcast.6, s32[32,128]{1,0:T(8,128)} %bitcast.8, s32[32,128]{1,0:T(8,128)} %bitcast.9, s32[32,128]{1,0:T(8,128)} %bitcast.10, ...), custom_call_target="tpu_custom_call" | custom-call | tf_op jit(solution)/shard_map/columns/pallas_call | solution.py:225
  2.7 5.9 %all-to-all-start = ((bf16[8,128,256]{2,1,0:T(8,128)(2,1)}), bf16[8,128,256]{2,1,0:T(8,128)(2,1)S(1)}, u32[]{:S(2)}, u32[]{:S(2)}) async-start(bf16[8,128,256]{2,1,0:T(8,128)(2,1)} %get-tuple-element.12), calls=%async_computation | async-start | bytes 1048576 | tf_op jit(solution)/shard_map/all_to_all | solution.py:248
  8.6 6.4 %collective-permute-start = (bf16[1600,128]{1,0:T(8,128)(2,1)}, bf16[1600,128]{1,0:T(8,128)(2,1)S(1)}, u32[]{:S(2)}, u32[]{:S(2)}) collective-permute-start(bf16[1600,128]{1,0:T(8,128)(2,1)} %get-tuple-element.13.own_ref), channel_id=1, source_target_pairs={{0,32},{32,0},{64,96},{96,64},{128,160},{160,128},{192,224},{224,1... | collective-permute-start | bytes 1228808 | tf_op jit(solution)/shard_map/ppermute | solution.py:249
  15.0 1.9 %collective-permute-start.1 = (bf16[1408,128]{1,0:T(8,128)(2,1)}, bf16[1408,128]{1,0:T(8,128)(2,1)S(1)}, u32[]{:S(2)}, u32[]{:S(2)}) collective-permute-start(bf16[1408,128]{1,0:T(8,128)(2,1)} %get-tuple-element.15), channel_id=1, source_target_pairs={{0,32},{32,0},{64,96},{96,64},{128,160},{160,128},{192,224},{224,1... | collective-permute-start | bytes 1081352 | tf_op jit(solution)/shard_map/ppermute | solution.py:250
  16.9 0.0 collective-permute-done.partner_ref.joined_ref
  16.9 0.0 copy-start
  17.0 1.0 %copy-done = bf16[1600,128]{1,0:T(8,128)(2,1)S(1)} copy-done((bf16[1600,128]{1,0:T(8,128)(2,1)S(1)}, bf16[1600,128]{1,0:T(8,128)(2,1)}, u32[]{:S(2)}) %copy-start) | copy-done | bytes 409624
  17.9 1.7 %rows.1.density_ref = bf16[2048,512]{1,0:T(8,128)(2,1)S(1)} custom-call(bf16[1600,128]{1,0:T(8,128)(2,1)S(1)} %copy-done, bf16[1600,128]{1,0:T(8,128)(2,1)S(1)} %collective-permute-done.partner_ref.joined_ref), custom_call_target="tpu_custom_call" | custom-call | tf_op jit(solution)/shard_map/rows/pallas_call | solution.py:251
  19.6 0.0 all-to-all-done.pairs_ref
  19.6 0.0 collective-permute-done.1.block_ref
  19.6 1.8 %screened.1 = (f32[2,128,256]{2,1,0:T(8,128)S(1)}, bf16[2,128,256]{2,1,0:T(8,128)(2,1)S(1)}) custom-call(bf16[8,128,256]{2,1,0:T(8,128)(2,1)S(1)} %all-to-all-done.pairs_ref, bf16[2,128,2048]{2,1,0:T(8,128)(2,1)} %own_ref.1, bf16[1600,128]{1,0:T(8,128)(2,1)S(1)} %collective-permute-done.partner_ref.joined_ref, ...), custom_call_target="tpu_custom_call" | custom-call | tf_op jit(solution)/shard_map/screened/pallas_call | solution.py:263
  21.4 3.5 %collective-permute-start.2 = (bf16[2,128,256]{2,1,0:T(8,128)(2,1)S(1)}, bf16[2,128,256]{2,1,0:T(8,128)(2,1)S(1)}, u32[]{:S(2)}, u32[]{:S(2)}) collective-permute-start(bf16[2,128,256]{2,1,0:T(8,128)(2,1)S(1)} %get-tuple-element.17), channel_id=1, source_target_pairs={{0,32},{32,0},{64,96},{96,64},{128,160},{160,128},{192,224},{224,1... | collective-permute-start | bytes 393224 | tf_op jit(solution)/shard_map/ppermute | solution.py:271
  24.9 1.0 %collective-permute-done.2.other_ref = bf16[2,128,256]{2,1,0:T(8,128)(2,1)S(1)} collective-permute-done((bf16[2,128,256]{2,1,0:T(8,128)(2,1)S(1)}, bf16[2,128,256]{2,1,0:T(8,128)(2,1)S(1)}, u32[]{:S(2)}, u32[]{:S(2)}) %collective-permute-start.2) | collective-permute-done | bytes 131104 | tf_op jit(solution)/shard_map/ppermute | solution.py:271
  25.9 0.7 %direct.1 = bf16[8,256,256]{2,1,0:T(8,128)(2,1)S(1)} custom-call(f32[2,128,256]{2,1,0:T(8,128)S(1)} %get-tuple-element.16.mine_ref, bf16[2,128,256]{2,1,0:T(8,128)(2,1)S(1)} %collective-permute-done.2.other_ref, bf16[2048,512]{1,0:T(8,128)(2,1)S(1)} %rows.1.density_ref), custom_call_target="tpu_custom_call" | custom-call | tf_op jit(solution)/shard_map/direct/pallas_call | solution.py:272
  26.6 18.3 %all_to_all.10.in_ref = bf16[8,256,256]{2,1,0:T(8,128)(2,1)S(1)} all-to-all(bf16[8,256,256]{2,1,0:T(8,128)(2,1)S(1)} %direct.1), channel_id=1, replica_groups={{0,256,64,320,128,384,192,448},{32,288,96,352,160,416,224,480},{1,257,6..., dimensions={0} | all-to-all | bytes 2097152 | tf_op jit(solution)/shard_map/all_to_all | solution.py:279
  44.9 0.8 %total.1 = f32[2,256,128]{2,1,0:T(8,128)} custom-call(bf16[8,256,256]{2,1,0:T(8,128)(2,1)S(1)} %all_to_all.10.in_ref), custom_call_target="tpu_custom_call" | custom-call | tf_op jit(solution)/shard_map/total/pallas_call | solution.py:280
Async XLA Ops:
  2.7 16.9 %all-to-all-start = ((bf16[8,128,256]{2,1,0:T(8,128)(2,1)}), bf16[8,128,256]{2,1,0:T(8,128)(2,1)S(1)}, u32[]{:S(2)}, u32[]{:S(2)}) async-start(bf16[8,128,256]{2,1,0:T(8,128)(2,1)} %get-tuple-element.12), calls=%async_computation | async-start | bytes 1048576 | tf_op jit(solution)/shard_map/all_to_all | solution.py:248
  8.6 8.4 %collective-permute-start = (bf16[1600,128]{1,0:T(8,128)(2,1)}, bf16[1600,128]{1,0:T(8,128)(2,1)S(1)}, u32[]{:S(2)}, u32[]{:S(2)}) collective-permute-start(bf16[1600,128]{1,0:T(8,128)(2,1)} %get-tuple-element.13.own_ref), channel_id=1, source_target_pairs={{0,32},{32,0},{64,96},{96,64},{128,160},{160,128},{192,224},{224,1... | collective-permute-start | bytes 1228808 | tf_op jit(solution)/shard_map/ppermute | solution.py:249
  15.0 4.6 %collective-permute-start.1 = (bf16[1408,128]{1,0:T(8,128)(2,1)}, bf16[1408,128]{1,0:T(8,128)(2,1)S(1)}, u32[]{:S(2)}, u32[]{:S(2)}) collective-permute-start(bf16[1408,128]{1,0:T(8,128)(2,1)} %get-tuple-element.15), channel_id=1, source_target_pairs={{0,32},{32,0},{64,96},{96,64},{128,160},{160,128},{192,224},{224,1... | collective-permute-start | bytes 1081352 | tf_op jit(solution)/shard_map/ppermute | solution.py:250
  16.9 1.0 %copy-start = (bf16[1600,128]{1,0:T(8,128)(2,1)S(1)}, bf16[1600,128]{1,0:T(8,128)(2,1)}, u32[]{:S(2)}) copy-start(bf16[1600,128]{1,0:T(8,128)(2,1)} %get-tuple-element.13.own_ref) | copy-start | bytes 1228804
  21.4 4.4 %collective-permute-start.2 = (bf16[2,128,256]{2,1,0:T(8,128)(2,1)S(1)}, bf16[2,128,256]{2,1,0:T(8,128)(2,1)S(1)}, u32[]{:S(2)}, u32[]{:S(2)}) collective-permute-start(bf16[2,128,256]{2,1,0:T(8,128)(2,1)S(1)} %get-tuple-element.17), channel_id=1, source_target_pairs={{0,32},{32,0},{64,96},{96,64},{128,160},{160,128},{192,224},{224,1... | collective-permute-start | bytes 393224 | tf_op jit(solution)/shard_map/ppermute | solution.py:271
